TPU v7x, 256 devices: a whole 4x4x8 slice. The times are simulated.
256 devices in a mesh: cp: 64 (over y, z, core), tp: 4 (over x).
Axes of the slice: x: 4, y: 4, z: 8, core: 2. Of those that a mesh axis runs over, the one named last changes fastest.
Arguments:
- queries: bfloat16 [32768, 4096], P('cp', 'tp'), may hold values from -6 to 6
- key_rows: bfloat16 [32768, 512], P('cp', 'tp'), may hold values from -6 to 6
- value_rows: bfloat16 [32768, 512], P('cp', 'tp'), may hold values from -6 to 6
- out_proj: bfloat16 [4096, 4096], P('tp'), may hold values from -0.09375 to 0.09375
- grad_mixed: bfloat16 [32768, 4096], P('cp', 'tp'), may hold values from -6 to 6
- doc_start: int32 [256], replicated, may hold values from 0 to 255, as said below
- balanced_source: int32 [256], replicated, may hold values from 0 to 255, as said below
Outputs:
- mixed: bfloat16 [32768, 4096], P('cp', 'tp')
- query_grad: bfloat16 [32768, 4096], P('cp', 'tp')
- key_grad: bfloat16 [32768, 512], P('cp', 'tp')
- value_grad: bfloat16 [32768, 512], P('cp', 'tp')
Inputs may be any that keep to these rules, and one draw needn't show every extreme that they name: doc_start[b] is the first block of the document that holds block b; documents are runs of 1 to 8 consecutive blocks, one of them has exactly 8, and the last block is a document of one block. `balanced_source`: a permutation of the blocks that maps each aligned run of 16 blocks onto itself.
All inputs are finite; a program needn't handle non-finite values.
Results may differ from a plain program's by a relative error of at most 0.024.
Values may be sent and summed in bfloat16 or wider, within the bound.
No kernel may reach another device: no remote copies, remote signals or barrier semaphores. Data moves between devices by JAX's collectives and lax.ppermute only.
A program may use at most 128 MiB of HBM per device.

v0:
```python
import math

import jax
import jax.numpy as jnp
from jax import lax
from jax.sharding import PartitionSpec as P

QH = 32
KVH = 4
HD = 128
BLOCK = 128
BLK_DEV = 4
MAXB = 8
GROUP = 4


masked_score = -1e30


def swapped(block, axis, apart):
    count = lax.axis_size(axis)
    route = []
    for low in range(count):
        high = low | 1 << apart
        if high != low and high < count:
            route += [(low, high), (high, low)]
    return lax.ppermute(block, axis, route)


def from_behind(block, axis, distance):
    devices = range(lax.axis_size(axis))
    route = [(i - distance, i) for i in devices if i - distance in devices]
    return lax.ppermute(block, axis, route)


def collect_group(blocks_in, device, move_rows):
    held_rows = blocks_in
    for step_bit in range(GROUP.bit_length() - 1):
        partner_rows = move_rows(held_rows, step_bit)
        upper_bit = (device >> step_bit) % 2
        held_rows = jnp.where(
            upper_bit == 1,
            jnp.concatenate([partner_rows, held_rows], 0),
            jnp.concatenate([held_rows, partner_rows], 0),
        )
    return held_rows


def shards(queries, key_rows, value_rows, out_proj, grad_mixed, doc_start, balanced_source):
    device = lax.axis_index("cp")
    member = device % GROUP
    group_blocks = GROUP * BLK_DEV
    group_first = device // GROUP * group_blocks
    head_width = queries.shape[1]
    kv_width = key_rows.shape[1]
    local_kv = kv_width // HD
    head_ratio = QH // KVH
    scale_value = 1.0 / math.sqrt(HD)
    token_rows = queries.shape[0]
    group_sources = (
        lax.dynamic_slice_in_dim(balanced_source, group_first, group_blocks) - group_first
    )
    slot_ids = jnp.arange(group_blocks, dtype=jnp.int32)
    block_slot = jnp.sum(
        jnp.where(group_sources[None, :] == slot_ids[:, None], slot_ids[None, :], 0), axis=1
    )
    own_range = member * BLK_DEV + jnp.arange(BLK_DEV, dtype=jnp.int32)
    wanted_blocks = group_sources[own_range]
    query_blocks = queries.reshape(BLK_DEV, BLOCK, head_width)
    kv_blocks = jnp.concatenate([key_rows, value_rows], 1).reshape(BLK_DEV, BLOCK, 2 * kv_width)
    packed = jnp.concatenate([query_blocks, kv_blocks], 2)
    group_rows = collect_group(
        packed, device, lambda held_rows, step_bit: swapped(held_rows, "cp", step_bit)
    )
    local_queries = group_rows[wanted_blocks][:, :, :head_width]
    group_kv = group_rows[:, :, head_width:]
    prior_blocks = MAXB - 1
    earlier = from_behind(group_kv[group_blocks - prior_blocks :], "cp", GROUP)
    key_pool = jnp.concatenate([earlier, group_kv], 0)
    pool_len = key_pool.shape[0]
    pool_first = group_first - prior_blocks
    pool_keys = key_pool[:, :, :kv_width].reshape(pool_len, BLOCK, local_kv, HD)
    pool_values = key_pool[:, :, kv_width:].reshape(pool_len, BLOCK, local_kv, HD)
    query_global = group_first + wanted_blocks
    query_starts = doc_start[query_global]
    offsets = jnp.arange(MAXB, dtype=jnp.int32)
    key_global = query_starts[:, None] + offsets[None, :]
    live_tiles = (key_global <= query_global[:, None]).reshape(-1)
    tile_order = jnp.argsort(jnp.where(live_tiles, 0, 1), stable=True)
    tile_query = jnp.broadcast_to(
        jnp.arange(BLK_DEV, dtype=jnp.int32)[:, None], (BLK_DEV, MAXB)
    ).reshape(-1)[tile_order]
    tile_key = (key_global - pool_first).reshape(-1)[tile_order]
    tile_diag = (key_global == query_global[:, None]).reshape(-1)[tile_order]
    tile_count = jnp.sum(live_tiles.astype(jnp.int32))
    query_heads = local_queries.reshape(BLK_DEV, BLOCK, local_kv, head_ratio, HD)
    positions = jnp.arange(BLOCK, dtype=jnp.int32)
    lower_half = positions[None, :] <= positions[:, None]

    def tile_scores(tile_id):
        which_query = tile_query[tile_id]
        which_key = jnp.clip(tile_key[tile_id], 0, pool_len - 1)
        allowed = lower_half | jnp.logical_not(tile_diag[tile_id])
        scores = (
            jnp.einsum(
                "ikrd,jkd->krij",
                query_heads[which_query],
                pool_keys[which_key],
                preferred_element_type=jnp.float32,
            )
            * scale_value
        )
        scores = jnp.where(allowed, scores, masked_score)
        return (which_query, which_key, scores, allowed)

    def stats_step(tile_id, running):
        top_all, total_all = running
        which_query, which_key, scores, allowed = tile_scores(tile_id)
        top_old = top_all[which_query]
        total_old = total_all[which_query]
        top_new = jnp.maximum(top_old, jnp.max(scores, axis=-1))
        total_new = total_old * jnp.exp(top_old - top_new) + jnp.sum(
            jnp.exp(scores - top_new[..., None]), axis=-1
        )
        return (top_all.at[which_query].set(top_new), total_all.at[which_query].set(total_new))

    stat_shape = (BLK_DEV, local_kv, head_ratio, BLOCK)
    top_all, total_all = lax.fori_loop(
        0,
        tile_count,
        stats_step,
        (jnp.full(stat_shape, masked_score, jnp.float32), jnp.zeros(stat_shape, jnp.float32)),
    )
    log_total = top_all + jnp.log(total_all)

    def output_step(tile_id, accumulated):
        which_query, which_key, scores, allowed = tile_scores(tile_id)
        weights = jnp.where(
            allowed, jnp.exp(scores - log_total[which_query][..., None]), 0.0
        ).astype(jnp.bfloat16)
        partial_out = jnp.einsum(
            "krij,jkd->ikrd", weights, pool_values[which_key], preferred_element_type=jnp.float32
        )
        return accumulated.at[which_query].add(partial_out)

    head_shape = (BLK_DEV, BLOCK, local_kv, head_ratio, HD)
    attended = lax.fori_loop(0, tile_count, output_step, jnp.zeros(head_shape, jnp.float32)).astype(
        jnp.bfloat16
    )
    attended_rows = attended.reshape(token_rows, head_width)
    head_terms = jnp.dot(attended_rows, out_proj, preferred_element_type=jnp.float32)
    mixed = lax.psum_scatter(head_terms.astype(jnp.bfloat16), "tp", scatter_dimension=1, tiled=True)
    grad_attended = lax.dot_general(
        lax.all_gather(grad_mixed, "tp", axis=1, tiled=True),
        out_proj,
        (((1,), (1,)), ((), ())),
        preferred_element_type=jnp.float32,
    ).astype(jnp.bfloat16)
    grad_heads = grad_attended.reshape(head_shape)
    row_delta = jnp.sum(grad_heads.astype(jnp.float32) * attended.astype(jnp.float32), axis=-1)
    row_delta = jnp.transpose(row_delta, (0, 2, 3, 1))

    def grad_step(tile_id, running):
        query_acc, key_acc, value_acc = running
        which_query, which_key, scores, allowed = tile_scores(tile_id)
        weights = jnp.where(allowed, jnp.exp(scores - log_total[which_query][..., None]), 0.0)
        weights_low = weights.astype(jnp.bfloat16)
        weights_back = lax.optimization_barrier(weights_low).astype(jnp.float32)
        key_tile = pool_keys[which_key]
        value_tile = pool_values[which_key]
        grad_tile = grad_heads[which_query]
        query_tile = query_heads[which_query]
        grad_weights = jnp.einsum(
            "ikrd,jkd->krij", grad_tile, value_tile, preferred_element_type=jnp.float32
        )
        grad_scores = (weights_back * (grad_weights - row_delta[which_query][..., None])).astype(
            jnp.bfloat16
        )
        query_part = jnp.einsum(
            "krij,jkd->ikrd", grad_scores, key_tile, preferred_element_type=jnp.float32
        )
        key_part = (
            jnp.einsum(
                "krij,ikrd->jkd", grad_scores, query_tile, preferred_element_type=jnp.float32
            )
            * scale_value
        )
        value_part = jnp.einsum(
            "krij,ikrd->jkd", weights_low, grad_tile, preferred_element_type=jnp.float32
        )
        return (
            query_acc.at[which_query].add(query_part),
            key_acc.at[which_key].add(key_part),
            value_acc.at[which_key].add(value_part),
        )

    pool_shape = (pool_len, BLOCK, local_kv, HD)
    query_acc, key_acc, value_acc = lax.fori_loop(
        0,
        tile_count,
        grad_step,
        (
            jnp.zeros(head_shape, jnp.float32),
            jnp.zeros(pool_shape, jnp.float32),
            jnp.zeros(pool_shape, jnp.float32),
        ),
    )
    balanced_grad = (
        (query_acc * scale_value).astype(jnp.bfloat16).reshape(BLK_DEV, BLOCK, head_width)
    )
    wanted_slots = block_slot[own_range]
    gathered = collect_group(
        balanced_grad, device, lambda held_rows, step_bit: swapped(held_rows, "cp", step_bit)
    )
    query_grad = gathered[wanted_slots]
    kv_grads = jnp.concatenate(
        [key_acc.reshape(pool_len, BLOCK, kv_width), value_acc.reshape(pool_len, BLOCK, kv_width)],
        2,
    )
    returned = from_behind(kv_grads[:prior_blocks].astype(jnp.bfloat16), "cp", -GROUP).astype(
        jnp.float32
    )
    own_grads = kv_grads[prior_blocks:]
    own_grads = own_grads.at[group_blocks - prior_blocks :].add(returned)
    for step_bit in reversed(range(GROUP.bit_length() - 1)):
        half_rows = own_grads.shape[0] // 2
        upper_bit = (device >> step_bit) % 2
        keep_part = jnp.where(upper_bit == 1, own_grads[half_rows:], own_grads[:half_rows])
        give_part = jnp.where(upper_bit == 1, own_grads[:half_rows], own_grads[half_rows:])
        own_grads = keep_part + swapped(give_part.astype(jnp.bfloat16), "cp", step_bit).astype(
            give_part.dtype
        )
    key_grad = own_grads[:, :, :kv_width].reshape(token_rows, kv_width).astype(jnp.bfloat16)
    value_grad = own_grads[:, :, kv_width:].reshape(token_rows, kv_width).astype(jnp.bfloat16)
    return (mixed, query_grad.reshape(token_rows, head_width), key_grad, value_grad)


def solution(mesh):
    placed = (P("cp", "tp"), P("cp", "tp"), P("cp", "tp"), P("tp", None), P("cp", "tp"), P(), P())
    return jax.shard_map(
        shards,
        mesh=mesh,
        in_specs=placed,
        out_specs=(P("cp", "tp"), P("cp", "tp"), P("cp", "tp"), P("cp", "tp")),
        check_vma=False,
    )
```

profile of v0, /device:TPU:9, one launch (start us, length us, event | category | flops | bytes accessed | tf_op | source)
XLA Modules:
  0.0 987.3 jit_solution(18338826203966219761)
XLA Ops:
  10.3 2.8 collective-permute-done
  13.1 2.7 maximum_select_fusion.3
  21.5 53.0 %collective-permute-done.1 = bf16[8,128,1280]{2,1,0:T(8,128)(2,1)} collective-permute-done((bf16[8,128,1280]{2,1,0:T(8,128)(2,1)S(1)}, bf16[8,128,1280]{2,1,0:T(8,128)(2,1)}, u32[]{:S(2)}, u32[]{:S(2)}) %collective-permute-start.1) | collective-permute-done | bytes 2621472 | tf_op jit(solution)/shard_map/ppermute | solution.py:27
  74.5 3.6 maximum_select_fusion.1
  78.1 2.3 copy-done.5
  81.2 4.9 collective-permute-start.2
  90.1 3.1 gather_fusion.5
  96.4 5.2 collective-permute-done.2
  101.6 2.7 fusion.106
  104.3 166.7 %while.46 = (s32[]{:T(128)}, f32[4,1,8,128]{3,2,1,0:T(8,128)S(1)}, f32[4,1,8,128]{3,2,1,0:T(8,128)S(1)}, s32[]{:T(128)}, s32[32]{0:T(128)}, /*index=5*/pred[32]{...) while((s32[]{:T(128)}, f32[4,1,8,128]{3,2,1,0:T(8,128)S(1)}, ...), condition=%wide.region_6.7_spmd.clone, body=%wide.region_2.6_spmd.clone.sunk | while | flops 34247716 | bytes 1425732 | solution.py:128
  272.1 207.6 %while.47 = (s32[]{:T(128)}, f32[4,128,1,8,128]{1,4,3,2,0:T(8,128)S(1)}, s32[]{:T(128)}, s32[32]{0:T(128)}, s32[32]{0:T(128)}, /*index=5*/bf16[23,128,1,128]{3,1...) while((s32[]{:T(128)}, ...), condition=%wide.region_9.10_spmd.clone, body=%wide.region_7.9_spmd.clone.sunk | while | flops 68059168 | bytes 1424247 | solution.py:147
  339.2 1.9 fusion.144
  350.7 1.9 fusion.144
  362.2 1.9 fusion.144
  408.2 1.9 fusion.144
  419.7 1.9 fusion.144
  481.1 9.2 fusion.89
  491.4 2.6 multiply_reduce_fusion
  494.8 9.4 convolution_convert_fusion
  506.1 369.7 %while.48 = (s32[]{:T(128)}, f32[4,128,1,8,128]{1,4,3,2,0:T(8,128)}, f32[23,128,1,128]{1,3,2,0:T(8,128)S(1)}, f32[23,128,1,128]{1,3,2,0:T(8,128)S(1)}, s32[]{:T(...) while((s32[]{:T(128)}, ...), condition=%wide.region_15.16_spmd.clone, body=%wide.region_12.15_spmd.clone.sunk | while | flops 169328688 | bytes 5665757 | solution.py:198
  519.4 2.8 fusion.156
  522.9 1.9 fusion.157
  539.9 2.7 fusion.156
  543.4 1.9 fusion.157
  560.4 2.7 fusion.156
  563.9 1.9 fusion.157
  580.9 2.7 fusion.156
  584.4 1.9 fusion.157
  601.4 2.7 fusion.156
  604.9 1.9 fusion.157
  621.9 2.7 fusion.156
  625.4 1.9 fusion.157
  642.4 2.7 fusion.156
  645.8 1.9 fusion.157
  662.9 2.7 fusion.156
  666.3 1.9 fusion.157
  683.3 2.8 fusion.156
  686.9 1.9 fusion.157
  703.9 2.8 fusion.156
  707.4 1.9 fusion.157
  724.4 2.8 fusion.156
  727.9 1.9 fusion.157
  744.9 2.8 fusion.156
  748.4 1.9 fusion.157
  765.4 2.8 fusion.156
  768.9 1.9 fusion.157
  785.9 2.8 fusion.156
  789.4 1.9 fusion.157
  806.5 2.8 fusion.156
  810.0 1.9 fusion.157
  827.0 2.8 fusion.156
  830.5 1.9 fusion.157
  847.5 2.8 fusion.156
  851.0 1.9 fusion.157
  868.0 2.8 fusion.156
  871.5 1.9 fusion.157
  875.8 2.9 multiply_convert_fusion
  878.7 2.3 copy.91
  881.0 2.2 collective-permute-start.3
  883.3 1.9 collective-permute-start.5
  885.4 22.7 %collective-permute-done.5 = bf16[7,128,256]{1,2,0:T(8,128)(2,1)S(1)} collective-permute-done((bf16[7,128,256]{1,2,0:T(8,128)(2,1)S(1)}, bf16[7,128,256]{1,2,0:T(8,128)(2,1)S(1)}, u32[]{:S(2)}, u32[]{:S(2)}) %collective-permute-start.5) | collective-permute-done | bytes 458784 | tf_op jit(solution)/shard_map/ppermute | solution.py:33
  911.1 55.2 %collective-permute-done.6 = bf16[8,128,256]{1,2,0:T(8,128)(2,1)S(1)} collective-permute-done((bf16[8,128,256]{1,2,0:T(8,128)(2,1)S(1)}, bf16[8,128,256]{1,2,0:T(8,128)(2,1)S(1)}, u32[]{:S(2)}, u32[]{:S(2)}) %collective-permute-start.6) | collective-permute-done | bytes 524320 | tf_op jit(solution)/shard_map/ppermute | solution.py:27
  972.6 4.1 maximum_select_fusion.2
  976.7 3.8 gather_fusion.7
  (646 shorter events, 472.0 us)
Async XLA Ops:
  7.2 11.3 %copy-start = (s32[256]{0:T(256)S(1)}, s32[256]{0:T(256)}, u32[]{:S(2)}) copy-start(s32[256]{0:T(256)} %param.32) | copy-start | bytes 3076
  7.2 472.7 %all-gather.2.cloned.1.call-start = ((), (), s32[]{:S(2)}) async-start(), calls=%async_computation.2 | async-start | bytes 5242880 | tf_op jit(solution)/shard_map/all_gather | solution.py:154
  9.6 3.6 collective-permute-start
  10.3 7.4 copy-start.12
  15.8 58.6 %collective-permute-start.1 = (bf16[8,128,1280]{2,1,0:T(8,128)(2,1)S(1)}, bf16[8,128,1280]{2,1,0:T(8,128)(2,1)}, u32[]{:S(2)}, u32[]{:S(2)}) collective-permute-start(bf16[8,128,1280]{2,1,0:T(8,128)(2,1)S(1)} %maximum_select_fusion.3), channel_id=1, source_target_pairs={{0,8},{8,0},{4,12},{12,4},{16,24},{24,16},{20,28},{28,20},{32,40},... | collective-permute-start | bytes 7864328 | tf_op jit(solution)/shard_map/ppermute | solution.py:27
  17.6 962.9 %reduce-scatter.2.cloned.1.call-start = ((), (), s32[]{:S(2)}) async-start(), calls=%async_computation.1 | async-start | bytes 5242880 | tf_op jit(solution)/shard_map/reduce_scatter | solution.py:152
  78.1 2.3 copy-start.5
  81.2 20.4 %collective-permute-start.2 = (bf16[7,128,256]{2,1,0:T(8,128)(2,1)}, bf16[7,128,256]{2,1,0:T(8,128)(2,1)}, u32[]{:S(2)}, u32[]{:S(2)}) collective-permute-start(bf16[7,128,256]{2,1,0:T(8,128)(2,1)} %slice.256), channel_id=1, source_target_pairs={{0,16},{4,20},{8,24},{12,28},{16,32},{20,36},{24,40},{28,44},{32,4... | collective-permute-start | bytes 1376264 | tf_op jit(solution)/shard_map/ppermute | solution.py:33
  93.4 8.2 slice-start
  96.4 7.9 copy-start.11
  271.0 0.9 copy-start.9
  479.8 1.3 copy-start.7
  479.8 10.5 %copy-start.4 = (bf16[4,128,1,8,128]{4,1,3,2,0:T(8,128)(2,1)}, bf16[4,128,1,8,128]{4,1,3,2,0:T(8,128)(2,1)S(1)}, u32[]{:S(2)}) copy-start(bf16[4,128,1,8,128]{4,1,3,2,0:T(8,128)(2,1)S(1)} %get-tuple-element.954) | copy-start | bytes 3145732
  490.6 3.5 copy-start.6
  504.2 1.9 copy-start.10
  515.9 1.1 copy-start.2
  536.4 1.1 copy-start.2
  556.9 1.1 copy-start.2
  577.4 1.1 copy-start.2
  597.9 1.1 copy-start.2
  618.4 1.1 copy-start.2
  638.9 1.1 copy-start.2
  659.3 1.1 copy-start.2
  679.8 1.1 copy-start.2
  700.3 1.1 copy-start.2
  720.9 1.1 copy-start.2
  741.4 1.1 copy-start.2
  761.9 1.1 copy-start.2
  782.4 1.1 copy-start.2
  803.0 1.1 copy-start.2
  823.5 1.1 copy-start.2
  844.0 1.1 copy-start.2
  864.5 1.1 copy-start.2
  881.0 27.3 %collective-permute-start.3 = (bf16[4,128,1024]{2,1,0:T(8,128)(2,1)}, bf16[4,128,1024]{2,1,0:T(8,128)(2,1)S(1)}, u32[]{:S(2)}, u32[]{:S(2)}) collective-permute-start(bf16[4,128,1024]{2,1,0:T(8,128)(2,1)} %copy.91), channel_id=1, source_target_pairs={{0,4},{4,0},{8,12},{12,8},{16,20},{20,16},{24,28},{28,24},{32,36},... | collective-permute-start | bytes 3145736 | tf_op jit(solution)/shard_map/ppermute | solution.py:27
  883.3 24.8 %collective-permute-start.5 = (bf16[7,128,256]{1,2,0:T(8,128)(2,1)S(1)}, bf16[7,128,256]{1,2,0:T(8,128)(2,1)S(1)}, u32[]{:S(2)}, u32[]{:S(2)}) collective-permute-start(bf16[7,128,256]{1,2,0:T(8,128)(2,1)S(1)} %fusion.95), channel_id=1, source_target_pairs={{16,0},{20,4},{24,8},{28,12},{32,16},{36,20},{40,24},{44,28},{48,3... | collective-permute-start | bytes 1376264 | tf_op jit(solution)/shard_map/ppermute | solution.py:33
  885.4 22.9 %copy-start.8 = (bf16[4,128,1024]{2,1,0:T(8,128)(2,1)S(1)}, bf16[4,128,1024]{2,1,0:T(8,128)(2,1)}, u32[]{:S(2)}) copy-start(bf16[4,128,1024]{2,1,0:T(8,128)(2,1)} %copy.91) | copy-start | bytes 3145732
  908.2 1.3 copy-start.3
  908.6 64.1 %collective-permute-start.4 = (bf16[8,128,1024]{2,1,0:T(8,128)(2,1)S(1)}, bf16[8,128,1024]{2,1,0:T(8,128)(2,1)}, u32[]{:S(2)}, u32[]{:S(2)}) collective-permute-start(bf16[8,128,1024]{2,1,0:T(8,128)(2,1)S(1)} %maximum_select_fusion.4), channel_id=1, source_target_pairs={{0,8},{8,0},{4,12},{12,4},{16,24},{24,16},{20,28},{28,20},{32,40},... | collective-permute-start | bytes 6291464 | tf_op jit(solution)/shard_map/ppermute | solution.py:27
  909.6 56.6 %collective-permute-start.6 = (bf16[8,128,256]{1,2,0:T(8,128)(2,1)S(1)}, bf16[8,128,256]{1,2,0:T(8,128)(2,1)S(1)}, u32[]{:S(2)}, u32[]{:S(2)}) collective-permute-start(bf16[8,128,256]{1,2,0:T(8,128)(2,1)S(1)} %select_convert_fusion), channel_id=1, source_target_pairs={{0,8},{8,0},{4,12},{12,4},{16,24},{24,16},{20,28},{28,20},{32,40},... | collective-permute-start | bytes 1572872 | tf_op jit(solution)/shard_map/ppermute | solution.py:27
  968.0 2.9 collective-permute-start.7
  972.6 7.9 copy-start.1
Sparse Core Ops, SparseCore 0:
  17.7 52.7 all-gather.1
  504.3 52.4 reduce-scatter.1
where the time goes:
time: 1000 us; the launch traced here: 987 us
  local copies, waits for them, and re-layouts  277 us (28%)
  matrix products  214 us (21%)
  loops' own time  212 us (21%)
  waiting for transfers between devices  140 us (14%)
  other arithmetic  116 us (12%)
  between operations  14.5 us (1%)
  starting transfers between devices  14.2 us (1%)
    ppermute x6, waiting for transfers between devices, swapped(): return lax.ppermute(block, axis, route)  112 us
    another operation x74, other arithmetic  74.8 us
    another operation x1, loops' own time, shards(): lax.fori_loop(0, tile_count, grad_step, (jnp.zeros(head_shape, jnp.float3...  73 us
    dynamic_slice x54, local copies, waits for them, and re-layouts, tile_scores(): allowed = lower_half | jnp.logical_not(tile_diag[tile_id])  69.9 us
    another operation x1, loops' own time, shards(): lax.fori_loop(0, tile_count, stats_step, (jnp.full(stat_shape, masked_sco...  69.7 us
    another operation x1, loops' own time, shards(): lax.fori_loop(0, tile_count, output_step, jnp.zeros(head_shape, jnp.float...  69.1 us
    dynamic_slice x54, local copies, waits for them, and re-layouts, tile_scores(): which_key = jnp.clip(tile_key[tile_id], 0, pool_len - 1)  66.7 us
    dynamic_slice x54, local copies, waits for them, and re-layouts, tile_scores(): which_query = tile_query[tile_id]  63.6 us
  transfers between devices with their start and end apart: 10, of which 6 were waited for; matrix products, arithmetic and copies ran while one was open for 58% of the time, Pallas kernels for 0%

commit v1 on v0

v1 whole, which is shorter than its diff:
```python
import math

import jax
import jax.numpy as jnp
from jax import lax
from jax.experimental import pallas as pl
from jax.experimental.pallas import tpu as pltpu
from jax.sharding import PartitionSpec as P

HD = 128
BLOCK = 128
BLK_DEV = 4
MAXB = 8
GROUP = 4
PRIOR = MAXB - 1
POOL = PRIOR + BLK_DEV
ROWS = BLOCK * BLK_DEV
WIDTH = 1024
CHUNKS = 2
CW = WIDTH // CHUNKS
PAIRS = CW // 256

SCALE = 1.0 / math.sqrt(HD)
SCALE_LOG2 = SCALE * math.log2(math.e)
MASKED = -1e30

START, GRAD_REL, GRAD_IDX, ATT_REL, ATT_IDX, CORE, TP = 0, 4, 8, 12, 16, 20, 21

ANY = pl.BlockSpec(memory_space=pl.ANY)
SMEM = pl.BlockSpec(memory_space=pltpu.SMEM)
VMEM_LIMIT = 48 * 1024 * 1024


def params(dims=1):
    return pltpu.CompilerParams(
        dimension_semantics=("arbitrary",) * dims, vmem_limit_bytes=VMEM_LIMIT
    )


def dot(a, b):
    return jnp.dot(a, b, preferred_element_type=jnp.float32)


def dot_nt(a, b):
    return lax.dot_general(a, b, (((1,), (1,)), ((), ())), preferred_element_type=jnp.float32)


def swap_cp(block, mask):
    count = lax.axis_size("cp")
    return lax.ppermute(block, "cp", [(i, i ^ mask) for i in range(count)])


def shift_cp(block, distance):
    count = lax.axis_size("cp")
    route = [(i, i + distance) for i in range(count) if 0 <= i + distance < count]
    return lax.ppermute(block, "cp", route)


def shift_tp(block, distance):
    count = lax.axis_size("tp")
    return lax.ppermute(block, "tp", [(i, (i + distance) % count) for i in range(count)])


def pool_copies(kv, far, near_own, near_far, keys, values, sems):
    def pair(src, row, rows, place, at):
        return [
            pltpu.make_async_copy(
                src.at[pl.ds(row, rows)], keys.at[pl.ds(place, rows)], sems.at[at]
            ),
            pltpu.make_async_copy(
                src.at[pl.ds(ROWS + row, rows)], values.at[pl.ds(place, rows)], sems.at[at + 1]
            ),
        ]

    own = pair(kv, 0, ROWS, PRIOR * BLOCK, 0)
    far_part = pair(far, BLOCK, ROWS - BLOCK, 0, 2)
    near_a = pair(near_far, 0, ROWS, ROWS - BLOCK, 4)
    near_b = pair(near_own, 0, ROWS, ROWS - BLOCK, 4)
    return own, far_part, near_a, near_b


def fill_pool(table, kv, far, near_own, near_far, keys, values, sems):
    own, far_part, near_a, near_b = pool_copies(
        kv, far, near_own, near_far, keys, values, sems
    )
    for copy in own + far_part:
        copy.start()

    @pl.when(table[CORE] == 0)
    def _():
        for copy in near_a:
            copy.start()

    @pl.when(table[CORE] != 0)
    def _():
        for copy in near_b:
            copy.start()

    for copy in own + far_part + near_a:
        copy.wait()


def transposed_pool(pool, flipped):
    for at in range(POOL):
        flipped[at] = pool[at * BLOCK : (at + 1) * BLOCK, :].T


def pair_of(flipped, block):
    return jnp.concatenate([flipped[block], flipped[block + 1]], axis=1)


def first_mask(start, low_block):
    key_pos = lax.broadcasted_iota(jnp.int32, (256, 256), 0)
    row_pos = lax.broadcasted_iota(jnp.int32, (256, 256), 1) % BLOCK + BLOCK
    return (key_pos <= row_pos) & (key_pos >= (start - low_block) * BLOCK)


def later_mask(start, low_block):
    key_pos = lax.broadcasted_iota(jnp.int32, (256, 256), 0)
    return key_pos >= (start - low_block) * BLOCK


def heads_flipped(block):
    return jnp.concatenate([block[:, :HD].T, block[:, HD:].T], axis=1)


def heads_stacked(block):
    return jnp.concatenate([block[:, :HD], block[:, HD:]], axis=0)


def forward_kernel(
    table, q_ref, kv, far, near_own, near_far, att_ref, att_t_ref, total_ref, keys, values, values_t, sems
):
    b = pl.program_id(0)

    @pl.when(b == 0)
    def _():
        fill_pool(table, kv, far, near_own, near_far, keys, values, sems)
        transposed_pool(values, values_t)

    start = jnp.maximum(table[START + b], 0)
    diag = PRIOR + b
    steps = (diag - start) // 2 + 1

    def scores(step, q_t):
        low_block = diag - 1 - 2 * step
        low = pl.multiple_of(low_block * BLOCK, BLOCK)
        return low_block, dot(keys[pl.ds(low, 256), :], q_t) * SCALE_LOG2

    for pair in range(PAIRS):
        cols = slice(pair * 256, (pair + 1) * 256)
        q_t = heads_flipped(q_ref[:, cols])
        low_block, s = scores(0, q_t)
        s = jnp.where(first_mask(start, low_block), s, MASKED)
        top = jnp.max(s, axis=0, keepdims=True)
        p = jnp.exp2(s - top)
        total = jnp.sum(p, axis=0, keepdims=True)
        acc = dot(pair_of(values_t, low_block), p.astype(jnp.bfloat16))

        def body(step, carry):
            top, total, acc = carry
            low_block, s = scores(step, q_t)
            s = jnp.where(later_mask(start, low_block), s, MASKED)
            top_new = jnp.maximum(top, jnp.max(s, axis=0, keepdims=True))
            fade = jnp.exp2(top - top_new)
            p = jnp.exp2(s - top_new)
            total = total * fade + jnp.sum(p, axis=0, keepdims=True)
            acc = acc * fade + dot(pair_of(values_t, low_block), p.astype(jnp.bfloat16))
            return top_new, total, acc

        top, total, acc = lax.fori_loop(1, steps, body, (top, total, acc))
        out = acc * (1.0 / total)
        att_t_ref[0, :, cols] = out.astype(jnp.bfloat16)
        for head in range(2):
            at = pair * 256 + head * HD
            att_ref[:, at : at + HD] = out[:, head * HD : (head + 1) * HD].T.astype(jnp.bfloat16)
        total_ref[0, :, cols] = top + jnp.log2(total)


def forward(table, queries, kv, far, near_own, near_far, chunk):
    return pl.pallas_call(
        forward_kernel,
        grid=(BLK_DEV,),
        in_specs=[SMEM, pl.BlockSpec((BLOCK, CW), lambda b: (b, chunk)), ANY, ANY, ANY, ANY],
        out_specs=[
            pl.BlockSpec((BLOCK, CW), lambda b: (b, 0)),
            pl.BlockSpec((1, HD, CW), lambda b: (b, 0, 0)),
            pl.BlockSpec((1, 1, CW), lambda b: (b, 0, 0)),
        ],
        out_shape=[
            jax.ShapeDtypeStruct((ROWS, CW), jnp.bfloat16),
            jax.ShapeDtypeStruct((BLK_DEV, HD, CW), jnp.bfloat16),
            jax.ShapeDtypeStruct((BLK_DEV, 1, CW), jnp.float32),
        ],
        scratch_shapes=[
            pltpu.VMEM((POOL * BLOCK, HD), jnp.bfloat16),
            pltpu.VMEM((POOL * BLOCK, HD), jnp.bfloat16),
            pltpu.VMEM((POOL, HD, BLOCK), jnp.bfloat16),
            pltpu.SemaphoreType.DMA((6,)),
        ],
        compiler_params=params(),
        name="attention_forward",
    )(table, queries, kv, far, near_own, near_far)


def start_chosen(rel, index, sources, place, sem, col=0):
    for at, source in enumerate(sources):
        @pl.when(rel == at)
        def _():
            pltpu.make_async_copy(
                source.at[pl.ds(pl.multiple_of(index * BLOCK, BLOCK), BLOCK)], place, sem
            ).start()


def backward_kernel(last, first, *refs):
    refs = list(refs)
    table, q_ref, att_t_ref, total_ref, kv, far, near_own, near_far = refs[:8]
    sources = refs[8:12]
    refs = refs[12:]
    if not first:
        key_in, value_in = refs[:2]
        refs = refs[2:]
    dq_ref = refs[0]
    if last:
        own_ref, near_ref, far_ref = refs[1:4]
        refs = refs[4:]
    else:
        key_out, value_out = refs[1:3]
        refs = refs[3:]
    keys, values, keys_t, grads, key_acc, value_acc, sems, grad_sems = refs
    b = pl.program_id(0)

    def grad_place(at):
        return grads.at[pl.ds(at * BLOCK, BLOCK)]

    @pl.when(b == 0)
    def _():
        for at in range(BLK_DEV):
            start_chosen(
                table[GRAD_REL + at], table[GRAD_IDX + at], sources, grad_place(at), grad_sems.at[at]
            )
        if first:
            key_acc[...] = jnp.zeros_like(key_acc)
            value_acc[...] = jnp.zeros_like(value_acc)
        else:
            key_acc[...] = key_in[...]
            value_acc[...] = value_in[...]
        fill_pool(table, kv, far, near_own, near_far, keys, values, sems)
        transposed_pool(keys, keys_t)
        for at in range(BLK_DEV):
            pltpu.make_async_copy(
                sources[0].at[pl.ds(0, BLOCK)], grad_place(at), grad_sems.at[at]
            ).wait()

    start = jnp.maximum(table[START + b], 0)
    diag = PRIOR + b
    steps = (diag - start) // 2 + 1
    grad_row = pl.multiple_of(b * BLOCK, BLOCK)

    for pair in range(PAIRS):
        cols = slice(pair * 256, (pair + 1) * 256)
        q = q_ref[:, cols]
        q_t = heads_flipped(q)
        q_s = heads_stacked(q)
        g = grads[pl.ds(grad_row, BLOCK), cols]
        g_t = heads_flipped(g)
        g_s = heads_stacked(g)
        delta = jnp.sum(
            g_t.astype(jnp.float32) * att_t_ref[0, :, cols].astype(jnp.float32),
            axis=0,
            keepdims=True,
        )
        log_total = total_ref[0, :, cols]

        def tile(step, mask):
            low_block = diag - 1 - 2 * step
            low = pl.multiple_of(low_block * BLOCK, BLOCK)
            k = keys[pl.ds(low, 256), :]
            v = values[pl.ds(low, 256), :]
            s = dot(k, q_t) * SCALE_LOG2
            s = jnp.where(mask(start, low_block), s, MASKED)
            p = jnp.exp2(s - log_total).astype(jnp.bfloat16)
            dp = dot(v, g_t)
            ds = (p.astype(jnp.float32) * (dp - delta)).astype(jnp.bfloat16)
            value_acc[pl.ds(low, 256), :] += dot(p, g_s)
            key_acc[pl.ds(low, 256), :] += dot(ds, q_s)
            return dot(pair_of(keys_t, low_block), ds)

        dq_t = tile(0, first_mask)
        dq_t = lax.fori_loop(1, steps, lambda step, acc: acc + tile(step, later_mask), dq_t)
        dq_t = dq_t * SCALE
        for head in range(2):
            at = pair * 256 + head * HD
            dq_ref[:, at : at + HD] = dq_t[:, head * HD : (head + 1) * HD].T.astype(jnp.bfloat16)

    @pl.when(b == BLK_DEV - 1)
    def _():
        if last:
            near_at = ROWS - BLOCK
            own_at = PRIOR * BLOCK
            own_ref[:ROWS] = key_acc[own_at:] * SCALE
            own_ref[ROWS:] = value_acc[own_at:]
            near_ref[:ROWS] = (key_acc[near_at:own_at] * SCALE).astype(jnp.bfloat16)
            near_ref[ROWS:] = value_acc[near_at:own_at].astype(jnp.bfloat16)
            empty = jnp.zeros((BLOCK, HD), jnp.bfloat16)
            far_ref[:BLOCK] = empty
            far_ref[BLOCK:ROWS] = (key_acc[:near_at] * SCALE).astype(jnp.bfloat16)
            far_ref[ROWS : ROWS + BLOCK] = empty
            far_ref[ROWS + BLOCK :] = value_acc[:near_at].astype(jnp.bfloat16)
        else:
            key_out[...] = key_acc[...]
            value_out[...] = value_acc[...]


def backward(table, queries, att_t, totals, pool, sources, carried, chunk, last):
    first = carried is None
    whole = lambda shape: pl.BlockSpec(shape, lambda b: (0,) * len(shape))
    pool_shape = (POOL * BLOCK, HD)
    in_specs = [
        SMEM,
        pl.BlockSpec((BLOCK, CW), lambda b: (b, chunk)),
        pl.BlockSpec((1, HD, CW), lambda b: (b, 0, 0)),
        pl.BlockSpec((1, 1, CW), lambda b: (b, 0, 0)),
    ] + [ANY] * 8
    if not first:
        in_specs += [whole(pool_shape)] * 2
    out_specs = [pl.BlockSpec((BLOCK, CW), lambda b: (b, 0))]
    out_shape = [jax.ShapeDtypeStruct((ROWS, CW), jnp.bfloat16)]
    if last:
        out_specs += [whole((2 * ROWS, HD))] * 3
        out_shape += [
            jax.ShapeDtypeStruct((2 * ROWS, HD), jnp.float32),
            jax.ShapeDtypeStruct((2 * ROWS, HD), jnp.bfloat16),
            jax.ShapeDtypeStruct((2 * ROWS, HD), jnp.bfloat16),
        ]
    else:
        out_specs += [whole(pool_shape)] * 2
        out_shape += [jax.ShapeDtypeStruct(pool_shape, jnp.float32)] * 2

    def kernel(*refs):
        backward_kernel(last, first, *refs)

    return pl.pallas_call(
        kernel,
        grid=(BLK_DEV,),
        in_specs=in_specs,
        out_specs=out_specs,
        out_shape=out_shape,
        scratch_shapes=[
            pltpu.VMEM(pool_shape, jnp.bfloat16),
            pltpu.VMEM(pool_shape, jnp.bfloat16),
            pltpu.VMEM((POOL, HD, BLOCK), jnp.bfloat16),
            pltpu.VMEM((ROWS, CW), jnp.bfloat16),
            pltpu.VMEM(pool_shape, jnp.float32),
            pltpu.VMEM(pool_shape, jnp.float32),
            pltpu.SemaphoreType.DMA((6,)),
            pltpu.SemaphoreType.DMA((BLK_DEV,)),
        ],
        compiler_params=params(),
        name="attention_backward",
    )(table, queries, att_t, totals, *pool, *sources, *([] if first else carried))


def grad_matmul_kernel(table, *refs):
    pieces, weight, outs = refs[:8], refs[8], refs[9:]
    j = pl.program_id(0)
    per_out = CW // 256
    for half in range(2):
        total = None
        for ahead in range(4):
            at = pl.multiple_of(((table[TP] + ahead) % 4) * WIDTH, WIDTH)
            term = dot_nt(pieces[2 * ahead + half][...], weight[:, pl.ds(at, WIDTH)])
            total = term if total is None else total + term
        value = total.astype(jnp.bfloat16)
        for c in range(CHUNKS):
            @pl.when(j // per_out == c)
            def _():
                outs[c][half * 256 : (half + 1) * 256, :] = value


def grad_matmul(table, pieces, weight):
    per_out = CW // 256

    def out_spec(c):
        return pl.BlockSpec(
            (ROWS, 256), lambda j, table: (0, jnp.clip(j - c * per_out, 0, per_out - 1))
        )

    return pl.pallas_call(
        grad_matmul_kernel,
        grid_spec=pltpu.PrefetchScalarGridSpec(
            num_scalar_prefetch=1,
            grid=(4,),
            in_specs=[pl.BlockSpec((ROWS // 2, WIDTH), lambda j, table: (0, 0))] * 8
            + [pl.BlockSpec((256, 4 * WIDTH), lambda j, table: (j, 0))],
            out_specs=[out_spec(c) for c in range(CHUNKS)],
        ),
        out_shape=[jax.ShapeDtypeStruct((ROWS, CW), jnp.bfloat16)] * CHUNKS,
        compiler_params=params(),
        name="grad_projection",
    )(table, *pieces, weight)


def far_product_kernel(table, *refs):
    sources = [refs[4 * c : 4 * c + 4] for c in range(CHUNKS)]
    weight, left, right, rows_out, rows, sems = refs[4 * CHUNKS :]
    j = pl.program_id(0)

    @pl.when(j == 0)
    def _():
        def place(c, at):
            return rows.at[pl.ds(at * BLOCK, BLOCK), pl.ds(c * CW, CW)]

        for c in range(CHUNKS):
            for at in range(BLK_DEV):
                start_chosen(
                    table[ATT_REL + at],
                    table[ATT_IDX + at],
                    sources[c],
                    place(c, at),
                    sems.at[c * BLK_DEV + at],
                )
        for c in range(CHUNKS):
            for at in range(BLK_DEV):
                pltpu.make_async_copy(
                    sources[c][0].at[pl.ds(0, BLOCK)], place(c, at), sems.at[c * BLK_DEV + at]
                ).wait()
        rows_out[...] = rows[...]

    value = dot(rows[...], weight[...]).astype(jnp.bfloat16)

    @pl.when(j < 2)
    def _():
        left[...] = value

    @pl.when(j >= 2)
    def _():
        right[...] = value


def far_product(table, sources, weight):
    flat = [source for group in sources for source in group]
    return pl.pallas_call(
        far_product_kernel,
        grid_spec=pltpu.PrefetchScalarGridSpec(
            num_scalar_prefetch=1,
            grid=(4,),
            in_specs=[ANY] * (4 * CHUNKS)
            + [pl.BlockSpec((WIDTH, 256), lambda j, table: (0, ((table[TP] + 2) % 4) * 4 + j))],
            out_specs=[
                pl.BlockSpec((ROWS, 256), lambda j, table: (0, jnp.minimum(j, 1))),
                pl.BlockSpec((ROWS, 256), lambda j, table: (0, jnp.maximum(j - 2, 0))),
                pl.BlockSpec((ROWS, WIDTH), lambda j, table: (0, 0)),
            ],
            scratch_shapes=[
                pltpu.VMEM((ROWS, WIDTH), jnp.bfloat16),
                pltpu.SemaphoreType.DMA((4 * CHUNKS,)),
            ],
        ),
        out_shape=[jax.ShapeDtypeStruct((ROWS, 512), jnp.bfloat16)] * 2
        + [jax.ShapeDtypeStruct((ROWS, WIDTH), jnp.bfloat16)],
        compiler_params=params(),
        name="far_product",
    )(table, *flat, weight)


def side_block(table, j, first_half):
    ahead = jnp.where(j < 2, 1, 3)
    half = jnp.where(j < 2, first_half, 1 - first_half)
    return ((table[TP] + ahead) % 4) * 4 + half * 2 + j % 2


def near_product_kernel(table, rows, weight, onward, back):
    value = dot(rows[...], weight[...]).astype(jnp.bfloat16)
    j = pl.program_id(0)

    @pl.when(j < 2)
    def _():
        onward[...] = value

    @pl.when(j >= 2)
    def _():
        back[...] = value


def sum_product_kernel(table, rows, weight, from_before, from_after, onward, back):
    value = dot(rows[...], weight[...])
    j = pl.program_id(0)

    @pl.when(j < 2)
    def _():
        onward[...] = (value + from_before[...].astype(jnp.float32)).astype(jnp.bfloat16)

    @pl.when(j >= 2)
    def _():
        back[...] = (value + from_after[...].astype(jnp.float32)).astype(jnp.bfloat16)


def side_products(table, rows, weight, received, first_half):
    front = pl.BlockSpec((ROWS, 256), lambda j, table: (0, jnp.minimum(j, 1)))
    rear = pl.BlockSpec((ROWS, 256), lambda j, table: (0, jnp.maximum(j - 2, 0)))
    return pl.pallas_call(
        near_product_kernel if received is None else sum_product_kernel,
        grid_spec=pltpu.PrefetchScalarGridSpec(
            num_scalar_prefetch=1,
            grid=(4,),
            in_specs=[
                pl.BlockSpec((ROWS, WIDTH), lambda j, table: (0, 0)),
                pl.BlockSpec((WIDTH, 256), lambda j, table: (0, side_block(table, j, first_half))),
            ]
            + ([] if received is None else [front, rear]),
            out_specs=[front, rear],
        ),
        out_shape=[jax.ShapeDtypeStruct((ROWS, 512), jnp.bfloat16)] * 2,
        compiler_params=params(),
        name="side_products",
    )(table, rows, weight, *([] if received is None else received))


def own_product_kernel(table, rows, weight, out):
    out[...] = dot(rows[...], weight[...])


def own_product(table, rows, weight):
    return pl.pallas_call(
        own_product_kernel,
        grid_spec=pltpu.PrefetchScalarGridSpec(
            num_scalar_prefetch=1,
            grid=(4,),
            in_specs=[
                pl.BlockSpec((ROWS, WIDTH), lambda j, table: (0, 0)),
                pl.BlockSpec((WIDTH, 256), lambda j, table: (0, table[TP] * 4 + j)),
            ],
            out_specs=pl.BlockSpec((ROWS, 256), lambda j, table: (0, j)),
        ),
        out_shape=jax.ShapeDtypeStruct((ROWS, WIDTH), jnp.float32),
        compiler_params=params(),
        name="own_product",
    )(table, rows, weight)


def last_sum_kernel(own, before_a, before_b, after_a, after_b, out):
    for half, before, after in ((0, before_a, after_a), (1, before_b, after_b)):
        cols = slice(half * 512, (half + 1) * 512)
        out[:, cols] = (
            own[:, cols] + before[...].astype(jnp.float32) + after[...].astype(jnp.float32)
        ).astype(jnp.bfloat16)


def last_sum(own, before_a, before_b, after_a, after_b):
    part = pl.BlockSpec((BLOCK, 512), lambda j: (j, 0))
    full = pl.BlockSpec((BLOCK, WIDTH), lambda j: (j, 0))
    return pl.pallas_call(
        last_sum_kernel,
        grid=(4,),
        in_specs=[full, part, part, part, part],
        out_specs=full,
        out_shape=jax.ShapeDtypeStruct((ROWS, WIDTH), jnp.bfloat16),
        compiler_params=params(),
        name="last_sum",
    )(own, before_a, before_b, after_a, after_b)


def scalar_table(doc_start, balanced_source):
    device = lax.axis_index("cp")
    member = device % GROUP
    group_blocks = GROUP * BLK_DEV
    group_first = device // GROUP * group_blocks
    sources = lax.dynamic_slice_in_dim(balanced_source, group_first, group_blocks) - group_first
    slots = jnp.arange(group_blocks, dtype=jnp.int32)
    slot_of = jnp.sum(
        jnp.where(sources[None, :] == slots[:, None], slots[None, :], 0), axis=1, dtype=jnp.int32
    )
    mine = member * BLK_DEV
    wanted = lax.dynamic_slice_in_dim(sources, mine, BLK_DEV)
    held = lax.dynamic_slice_in_dim(slot_of, mine, BLK_DEV)
    starts = lax.dynamic_slice_in_dim(doc_start, device * BLK_DEV, BLK_DEV)
    starts = starts - (device * BLK_DEV - PRIOR)
    return jnp.concatenate(
        [
            starts,
            (held // BLK_DEV) ^ member,
            held % BLK_DEV,
            (wanted // BLK_DEV) ^ member,
            wanted % BLK_DEV,
            jnp.stack([device % 2, lax.axis_index("tp")]),
        ]
    ).astype(jnp.int32)


def group_exchange(block):
    across = swap_cp(block, 2)
    return [block, swap_cp(block, 1), across, swap_cp(across, 1)]


def shards(queries, key_rows, value_rows, out_proj, grad_mixed, doc_start, balanced_source):
    table = scalar_table(doc_start, balanced_source)

    kv = jnp.concatenate([key_rows, value_rows], axis=0)
    far = shift_cp(kv, 2)
    near_own = swap_cp(kv, 1)
    near_far = swap_cp(far, 1)
    pool = (kv, far, near_own, near_far)

    half = ROWS // 2
    upper, lower = grad_mixed[:half], grad_mixed[half:]
    before_upper = shift_tp(upper, 1)
    after_lower = shift_tp(lower, -1)
    before_lower = shift_tp(lower, 1)
    after_upper = shift_tp(upper, -1)
    opposite_upper = shift_tp(before_upper, 1)
    opposite_lower = shift_tp(after_lower, -1)

    attended, attended_t, totals, exchanged = [], [], [], []
    for chunk in range(CHUNKS):
        att, att_t, total = forward(table, queries, *pool, chunk)
        attended_t.append(att_t)
        totals.append(total)
        exchanged.append(group_exchange(att))

    far_left, far_right, rows = far_product(table, exchanged, out_proj)
    from_before = shift_tp(far_left, 1)
    from_after = shift_tp(far_right, -1)
    onward_b, back_a = side_products(table, rows, out_proj, None, 1)
    before_b = shift_tp(onward_b, 1)
    after_a = shift_tp(back_a, -1)
    onward_a, back_b = side_products(table, rows, out_proj, (from_before, from_after), 0)
    before_a = shift_tp(onward_a, 1)
    after_b = shift_tp(back_b, -1)
    own = own_product(table, rows, out_proj)
    mixed = last_sum(own, before_a, before_b, after_a, after_b)

    pieces = [
        upper,
        lower,
        after_upper,
        after_lower,
        opposite_upper,
        opposite_lower,
        before_upper,
        before_lower,
    ]
    grad_attended = grad_matmul(table, pieces, out_proj)
    carried = None
    query_grads = []
    for chunk in range(CHUNKS):
        sources = group_exchange(grad_attended[chunk])
        outs = backward(
            table, queries, attended_t[chunk], totals[chunk], pool, sources, carried, chunk,
            chunk == CHUNKS - 1,
        )
        query_grads.append(outs[0])
        carried = outs[1:]
    query_grad = jnp.concatenate(query_grads, axis=1)
    own_grads, near_grads, far_grads = carried
    near_back = shift_cp(near_grads, -1)
    far_back = shift_cp(far_grads, -2)
    kv_grads = (
        own_grads + near_back.astype(jnp.float32) + far_back.astype(jnp.float32)
    ).astype(jnp.bfloat16)
    return (mixed, query_grad, kv_grads[:ROWS], kv_grads[ROWS:])


def solution(mesh):
    placed = (P("cp", "tp"), P("cp", "tp"), P("cp", "tp"), P("tp", None), P("cp", "tp"), P(), P())
    return jax.shard_map(
        shards,
        mesh=mesh,
        in_specs=placed,
        out_specs=(P("cp", "tp"),) * 4,
        check_vma=False,
    )
```

time: 1000 us -> 181 us (0.18)
  the two profiles are of different devices: /device:TPU:9 before, /device:TPU:174 now
where the time goes in v1:
time: 181 us
  Pallas kernels  92.8 us (51%)
  waiting for transfers between devices  57.4 us (32%)
  starting transfers between devices  24.7 us (14%)
  local copies, waits for them, and re-layouts  3.09 us (2%)
    pallas_call x2, Pallas kernels, backward(): pl.pallas_call(kernel, grid=(BLK_DEV,), in_specs=in_specs, out_specs=out_...  30.4 us
    ppermute x12, waiting for transfers between devices, shift_tp(): lax.ppermute(block, 'tp', [(i, (i + distance) % count) for i in range(cou...  29.3 us
    pallas_call x2, Pallas kernels, forward(): pl.pallas_call(forward_kernel, grid=(BLK_DEV,), in_specs=[SMEM, pl.BlockS...  28.9 us
    ppermute x14, waiting for transfers between devices, swap_cp(): return lax.ppermute(block, 'cp', [(i, i ^ mask) for i in range(count)])  23 us
    ppermute x12, starting transfers between devices, shift_tp(): lax.ppermute(block, 'tp', [(i, (i + distance) % count) for i in range(cou...  14 us
    pallas_call x1, Pallas kernels, grad_matmul(): pl.pallas_call(grad_matmul_kernel, grid_spec=pltpu.PrefetchScalarGridSpec...  13.3 us
    pallas_call x2, Pallas kernels, side_products(): pl.pallas_call(near_product_kernel if received is None else sum_product_k...  8.71 us
    ppermute x3, starting transfers between devices, shift_cp(): return lax.ppermute(block, 'cp', route)  6.77 us
  transfers between devices with their start and end apart: 29, of which 9 were waited for; matrix products, arithmetic and copies ran while one was open for 1% of the time, Pallas kernels for 50%

profile of v1, /device:TPU:174, one launch (start us, length us, event | category | flops | bytes accessed | tf_op | source)
XLA Modules:
  0.0 180.6 jit_solution(894820918837127233)
XLA Ops:
  0.7 0.0 copy-start
  0.7 1.4 fusion.2
  2.1 0.6 collective-permute-start.17
  2.6 1.5 collective-permute-start.15
  4.2 2.9 %collective-permute-start = (bf16[1024,128]{1,0:T(8,128)(2,1)S(1)}, bf16[1024,128]{1,0:T(8,128)(2,1)S(1)}, u32[]{:S(2)}, u32[]{:S(2)}) collective-permute-start(bf16[1024,128]{1,0:T(8,128)(2,1)S(1)} %constant_dynamic-update-slice_fusion.kv.refs_4_), channel_id=1, source_target_pairs={{0,8},{4,12},{8,16},{12,20},{16,24},{20,28},{24,32},{28,36},{32,40... | collective-permute-start | bytes 786440 | tf_op jit(solution)/shard_map/ppermute | solution.py:56
  7.2 0.1 collective-permute-start.1
  7.3 0.9 collective-permute-start.16
  8.2 0.1 dynamic-slice_subtract_fusion
  8.2 0.1 select_reduce_fusion
  8.4 0.1 and_select_fusion
  8.5 0.1 and_select_fusion.2
  8.5 5.1 %collective-permute-done.far.refs_5_ = bf16[1024,128]{1,0:T(8,128)(2,1)S(1)} collective-permute-done((bf16[1024,128]{1,0:T(8,128)(2,1)S(1)}, bf16[1024,128]{1,0:T(8,128)(2,1)S(1)}, u32[]{:S(2)}, u32[]{:S(2)}) %collective-permute-start) | collective-permute-done | bytes 262176 | tf_op jit(solution)/shard_map/ppermute | solution.py:56
  13.6 1.7 collective-permute-start.20
  15.3 1.8 collective-permute-done.17.refs_6_
  17.1 0.5 collective-permute-start.18
  17.6 0.1 dynamic-slice_subtract_fusion.1
  17.7 0.1 fusion
  17.8 0.1 concatenate.9.table.refs_0_
  17.9 10.7 %collective-permute-done.16.refs_3_ = bf16[256,1024]{1,0:T(8,128)(2,1)} collective-permute-done((bf16[256,1024]{1,0:T(8,128)(2,1)S(1)}, bf16[256,1024]{1,0:T(8,128)(2,1)}, u32[]{:S(2)}, u32[]{:S(2)}) %collective-permute-start.16) | collective-permute-done | bytes 524320 | tf_op jit(solution)/shard_map/ppermute | solution.py:61
  28.6 0.3 collective-permute-start.19
  28.9 0.0 collective-permute-done.2.near_far.refs_7_
  28.9 14.4 %attention_forward.3 = (bf16[512,512]{1,0:T(8,128)(2,1)S(1)}, bf16[4,128,512]{2,1,0:T(8,128)(2,1)S(1)}, f32[4,1,512]{2,1,0:T(1,128)S(1)}) custom-call(s32[22]{0:T(128)S(1)} %concatenate.9.table.refs_0_, bf16[512,1024]{1,0:T(8,128)(2,1)S(1)} %copy-done, bf16[1024,128]{1,0:T(8,128)(2,1)S(1)} %constant_dynamic-update-slice_fusion.kv.refs_4_, ...), custom_call_target="tpu_custom_call" | custom-call | tf_op jit(solution)/shard_map/attention_forward/pallas_call | solution.py:181
  43.3 0.1 collective-permute-start.7
  43.5 0.1 collective-permute-start.6
  43.6 14.5 %attention_forward.2 = (bf16[512,512]{1,0:T(8,128)(2,1)S(1)}, bf16[4,128,512]{2,1,0:T(8,128)(2,1)S(1)}, f32[4,1,512]{2,1,0:T(1,128)S(1)}) custom-call(s32[22]{0:T(128)S(1)} %concatenate.9.table.refs_0_, bf16[512,1024]{1,0:T(8,128)(2,1)S(1)} %copy-done, bf16[1024,128]{1,0:T(8,128)(2,1)S(1)} %constant_dynamic-update-slice_fusion.kv.refs_4_, ...), custom_call_target="tpu_custom_call" | custom-call | tf_op jit(solution)/shard_map/attention_forward/pallas_call | solution.py:181
  58.0 0.0 collective-permute-done.20.refs_7_
  58.0 0.1 collective-permute-start.4
  58.1 0.1 collective-permute-start.3
  58.2 0.0 collective-permute-done.19.refs_5_
  58.3 13.3 %grad_projection.1 = (bf16[512,512]{1,0:T(8,128)(2,1)S(1)}, bf16[512,512]{1,0:T(8,128)(2,1)S(1)}) custom-call(s32[22]{0:T(128)S(1)} %concatenate.9.table.refs_0_, bf16[256,1024]{1,0:T(8,128)(2,1)S(1)} %get-tuple-element.53.refs_0_, bf16[256,1024]{1,0:T(8,128)(2,1)S(1)} %get-tuple-element.52.refs_1_, bf16[256,1024]{1,0:T(8,128)(2,1)} %collective-permute-done.15.refs_2_, ...), custom_call_target="tpu_custom_call" | custom-call | tf_op jit(solution)/shard_map/grad_projection/pallas_call | solution.py:389
  71.6 2.2 %collective-permute-start.22 = (bf16[512,512]{1,0:T(8,128)(2,1)S(1)}, bf16[512,512]{1,0:T(8,128)(2,1)S(1)}, u32[]{:S(2)}, u32[]{:S(2)}) collective-permute-start(bf16[512,512]{1,0:T(8,128)(2,1)S(1)} %get-tuple-element.37.refs_8_), channel_id=1, source_target_pairs={{0,8},{4,12},{8,0},{12,4},{16,24},{20,28},{24,16},{28,20},{32,40},... | collective-permute-start | bytes 1572872 | tf_op jit(solution)/shard_map/ppermute | solution.py:50
  73.8 0.0 collective-permute-done.7.refs_6_
  73.8 0.1 collective-permute-start.25
  73.9 0.0 collective-permute-done.6.refs_5_
  73.9 0.2 collective-permute-start.8
  74.1 0.0 collective-permute-done.4.refs_2_
  74.1 0.3 collective-permute-start.5
  74.4 0.2 collective-permute-start.21
  74.6 12.0 %collective-permute-done.22.refs_10_ = bf16[512,512]{1,0:T(8,128)(2,1)S(1)} collective-permute-done((bf16[512,512]{1,0:T(8,128)(2,1)S(1)}, bf16[512,512]{1,0:T(8,128)(2,1)S(1)}, u32[]{:S(2)}, u32[]{:S(2)}) %collective-permute-start.22) | collective-permute-done | bytes 524320 | tf_op jit(solution)/shard_map/ppermute | solution.py:50
  86.7 10.9 %collective-permute-done.25.refs_10_ = bf16[512,512]{1,0:T(8,128)(2,1)S(1)} collective-permute-done((bf16[512,512]{1,0:T(8,128)(2,1)S(1)}, bf16[512,512]{1,0:T(8,128)(2,1)S(1)}, u32[]{:S(2)}, u32[]{:S(2)}) %collective-permute-start.25) | collective-permute-done | bytes 524320 | tf_op jit(solution)/shard_map/ppermute | solution.py:50
  97.6 0.5 collective-permute-start.26
  98.1 5.6 %far_product.1 = (bf16[512,512]{1,0:T(8,128)(2,1)S(1)}, bf16[512,512]{1,0:T(8,128)(2,1)S(1)}, bf16[512,1024]{1,0:T(8,128)(2,1)}) custom-call(s32[22]{0:T(128)S(1)} %concatenate.9.table.refs_0_, bf16[512,512]{1,0:T(8,128)(2,1)S(1)} %get-tuple-element.26.refs_0_, bf16[512,512]{1,0:T(8,128)(2,1)S(1)} %collective-permute-done.3.refs_1_, ...), custom_call_target="tpu_custom_call" | custom-call | tf_op jit(solution)/shard_map/far_product/pallas_call | solution.py:443
  103.7 0.9 collective-permute-start.10
  104.6 2.4 %collective-permute-start.9 = (bf16[512,512]{1,0:T(8,128)(2,1)S(1)}, bf16[512,512]{1,0:T(8,128)(2,1)S(1)}, u32[]{:S(2)}, u32[]{:S(2)}) collective-permute-start(bf16[512,512]{1,0:T(8,128)(2,1)S(1)} %get-tuple-element.29), channel_id=1, source_target_pairs={{0,1},{1,2},{2,3},{3,0},{4,5},{5,6},{6,7},{7,4},{8,9},{9,10},{10,1... | collective-permute-start | bytes 1572872 | tf_op jit(solution)/shard_map/ppermute | solution.py:61
  107.0 15.0 %attention_backward.2 = (bf16[512,512]{1,0:T(8,128)(2,1)S(1)}, f32[1408,128]{1,0:T(8,128)S(1)}, f32[1408,128]{1,0:T(8,128)S(1)}) custom-call(s32[22]{0:T(128)S(1)} %concatenate.9.table.refs_0_, bf16[512,1024]{1,0:T(8,128)(2,1)} %refs_1_.3, bf16[4,128,512]{2,1,0:T(8,128)(2,1)S(1)} %get-tuple-element.35.refs_2_, f32[4,1,512]{2,1,0:T(1,128)S(1)} %get-tuple-element.36.refs_3_, ...), custom_call_target="tpu_custom_call" | custom-call | tf_op jit(solution)/shard_map/attention_backward/pallas_call | solution.py:343
  122.0 0.0 copy-start.2
  122.0 0.8 copy-done.2
  122.8 15.5 %attention_backward.3 = (bf16[512,512]{1,0:T(8,128)(2,1)S(1)}, f32[1024,128]{1,0:T(8,128)S(1)}, bf16[1024,128]{1,0:T(8,128)(2,1)S(1)}, bf16[1024,128]{1,0:T(8,128)(2,1)S(1)}) custom-call(s32[22]{0:T(128)S(1)} %concatenate.9.table.refs_0_, bf16[512,1024]{1,0:T(8,128)(2,1)} %refs_1_.3, bf16[4,128,512]{2,1,0:T(8,128)(2,1)S(1)} %get-tuple-element.39.refs_2_, ...), custom_call_target="tpu_custom_call" | custom-call | tf_op jit(solution)/shard_map/attention_backward/pallas_call | solution.py:343
  138.3 1.9 %collective-permute-start.27 = (bf16[1024,128]{1,0:T(8,128)(2,1)S(1)}, bf16[1024,128]{1,0:T(8,128)(2,1)S(1)}, u32[]{:S(2)}, u32[]{:S(2)}) collective-permute-start(bf16[1024,128]{1,0:T(8,128)(2,1)S(1)} %get-tuple-element.46), channel_id=1, source_target_pairs={{4,0},{8,4},{12,8},{16,12},{20,16},{24,20},{28,24},{32,28},{36,32}... | collective-permute-start | bytes 786440 | tf_op jit(solution)/shard_map/ppermute | solution.py:56
  140.3 1.9 %collective-permute-start.28 = (bf16[1024,128]{1,0:T(8,128)(2,1)S(1)}, bf16[1024,128]{1,0:T(8,128)(2,1)S(1)}, u32[]{:S(2)}, u32[]{:S(2)}) collective-permute-start(bf16[1024,128]{1,0:T(8,128)(2,1)S(1)} %get-tuple-element.47), channel_id=1, source_target_pairs={{8,0},{12,4},{16,8},{20,12},{24,16},{28,20},{32,24},{36,28},{40,32... | collective-permute-start | bytes 786440 | tf_op jit(solution)/shard_map/ppermute | solution.py:56
  142.2 4.1 %own_product.1.own = f32[512,1024]{1,0:T(8,128)S(1)} custom-call(s32[22]{0:T(128)S(1)} %concatenate.9.table.refs_0_, bf16[512,1024]{1,0:T(8,128)(2,1)S(1)} %copy-done.1, bf16[1024,4096]{1,0:T(8,128)(2,1)} %refs_8_.3), custom_call_target="tpu_custom_call" | custom-call | tf_op jit(solution)/shard_map/own_product/pallas_call | solution.py:525
  146.3 4.3 %side_products.3 = (bf16[512,512]{1,0:T(8,128)(2,1)S(1)}, bf16[512,512]{1,0:T(8,128)(2,1)S(1)}) custom-call(s32[22]{0:T(128)S(1)} %concatenate.9.table.refs_0_, bf16[512,1024]{1,0:T(8,128)(2,1)S(1)} %copy-done.1, bf16[1024,4096]{1,0:T(8,128)(2,1)} %refs_8_.3), custom_call_target="tpu_custom_call" | custom-call | tf_op jit(solution)/shard_map/side_products/pallas_call | solution.py:502
  150.6 1.8 collective-permute-start.12
  152.4 0.3 collective-permute-start.13
  152.7 4.4 %side_products.2 = (bf16[512,512]{1,0:T(8,128)(2,1)S(1)}, bf16[512,512]{1,0:T(8,128)(2,1)S(1)}) custom-call(s32[22]{0:T(128)S(1)} %concatenate.9.table.refs_0_, bf16[512,1024]{1,0:T(8,128)(2,1)S(1)} %copy-done.1, bf16[1024,4096]{1,0:T(8,128)(2,1)} %refs_8_.3, bf16[512,512]{1,0:T(8,128)(2,1)S(1)} %collective-permute-done.9.from_before, ...), custom_call_target="tpu_custom_call" | custom-call | tf_op jit(solution)/shard_map/side_products/pallas_call | solution.py:502
  157.2 3.0 %collective-permute-start.11 = (bf16[512,512]{1,0:T(8,128)(2,1)S(1)}, bf16[512,512]{1,0:T(8,128)(2,1)S(1)}, u32[]{:S(2)}, u32[]{:S(2)}) collective-permute-start(bf16[512,512]{1,0:T(8,128)(2,1)S(1)} %get-tuple-element.31), channel_id=1, source_target_pairs={{0,1},{1,2},{2,3},{3,0},{4,5},{5,6},{6,7},{7,4},{8,9},{9,10},{10,1... | collective-permute-start | bytes 1572872 | tf_op jit(solution)/shard_map/ppermute | solution.py:61
  160.2 1.1 pad_maximum_fusion
  161.3 0.1 add_convert_fusion
  161.3 0.7 fusion.3
  162.1 3.4 %collective-permute-done.12.before_b = bf16[512,512]{1,0:T(8,128)(2,1)S(1)} collective-permute-done((bf16[512,512]{1,0:T(8,128)(2,1)S(1)}, bf16[512,512]{1,0:T(8,128)(2,1)S(1)}, u32[]{:S(2)}, u32[]{:S(2)}) %collective-permute-start.12) | collective-permute-done | bytes 524320 | tf_op jit(solution)/shard_map/ppermute | solution.py:61
  165.4 2.9 %collective-permute-done.13.after_a = bf16[512,512]{1,0:T(8,128)(2,1)S(1)} collective-permute-done((bf16[512,512]{1,0:T(8,128)(2,1)S(1)}, bf16[512,512]{1,0:T(8,128)(2,1)S(1)}, u32[]{:S(2)}, u32[]{:S(2)}) %collective-permute-start.13) | collective-permute-done | bytes 524320 | tf_op jit(solution)/shard_map/ppermute | solution.py:61
  168.4 7.9 %collective-permute-done.11.before_a = bf16[512,512]{1,0:T(8,128)(2,1)S(1)} collective-permute-done((bf16[512,512]{1,0:T(8,128)(2,1)S(1)}, bf16[512,512]{1,0:T(8,128)(2,1)S(1)}, u32[]{:S(2)}, u32[]{:S(2)}) %collective-permute-start.11) | collective-permute-done | bytes 524320 | tf_op jit(solution)/shard_map/ppermute | solution.py:61
  176.3 2.6 %collective-permute-done.14.after_b = bf16[512,512]{1,0:T(8,128)(2,1)S(1)} collective-permute-done((bf16[512,512]{1,0:T(8,128)(2,1)S(1)}, bf16[512,512]{1,0:T(8,128)(2,1)S(1)}, u32[]{:S(2)}, u32[]{:S(2)}) %collective-permute-start.14) | collective-permute-done | bytes 524320 | tf_op jit(solution)/shard_map/ppermute | solution.py:61
  178.9 1.7 last_sum.1
  (31 shorter events, 0.1 us)
Async XLA Ops:
  0.6 3.5 %copy-start.3 = (bf16[512,128]{1,0:T(8,128)(2,1)S(1)}, bf16[512,128]{1,0:T(8,128)(2,1)}, u32[]{:S(2)}) copy-start(bf16[512,128]{1,0:T(8,128)(2,1)} %param.8) | copy-start | bytes 393220
  0.6 3.5 %copy-start.4 = (bf16[512,128]{1,0:T(8,128)(2,1)S(1)}, bf16[512,128]{1,0:T(8,128)(2,1)}, u32[]{:S(2)}) copy-start(bf16[512,128]{1,0:T(8,128)(2,1)} %param.9) | copy-start | bytes 393220
  0.7 7.5 %copy-start.5 = (s32[256]{0:T(256)S(1)}, s32[256]{0:T(256)}, u32[]{:S(2)}) copy-start(s32[256]{0:T(256)} %param.13) | copy-start | bytes 3076
  0.7 16.9 %copy-start.6 = (s32[256]{0:T(256)S(1)}, s32[256]{0:T(256)}, u32[]{:S(2)}) copy-start(s32[256]{0:T(256)} %param.12) | copy-start | bytes 3076
  0.7 28.2 %copy-start = (bf16[512,1024]{1,0:T(8,128)(2,1)S(1)}, bf16[512,1024]{1,0:T(8,128)(2,1)}, u32[]{:S(2)}) copy-start(bf16[512,1024]{1,0:T(8,128)(2,1)} %refs_1_.3) | copy-start | bytes 3145732
  2.1 15.0 %collective-permute-start.17 = (bf16[256,1024]{1,0:T(8,128)(2,1)S(1)}, bf16[256,1024]{1,0:T(8,128)(2,1)}, u32[]{:S(2)}, u32[]{:S(2)}) collective-permute-start(bf16[256,1024]{1,0:T(8,128)(2,1)S(1)} %get-tuple-element.53.refs_0_), channel_id=1, source_target_pairs={{0,1},{1,2},{2,3},{3,0},{4,5},{5,6},{6,7},{7,4},{8,9},{9,10},{10,1... | collective-permute-start | bytes 1572872 | tf_op jit(solution)/shard_map/ppermute | solution.py:61
  2.6 40.8 %collective-permute-start.15 = (bf16[256,1024]{1,0:T(8,128)(2,1)S(1)}, bf16[256,1024]{1,0:T(8,128)(2,1)}, u32[]{:S(2)}, u32[]{:S(2)}) collective-permute-start(bf16[256,1024]{1,0:T(8,128)(2,1)S(1)} %get-tuple-element.53.refs_0_), channel_id=1, source_target_pairs={{0,3},{1,0},{2,1},{3,2},{4,7},{5,4},{6,5},{7,6},{8,11},{9,8},{10,9... | collective-permute-start | bytes 1572872 | tf_op jit(solution)/shard_map/ppermute | solution.py:61
  4.2 9.4 %collective-permute-start = (bf16[1024,128]{1,0:T(8,128)(2,1)S(1)}, bf16[1024,128]{1,0:T(8,128)(2,1)S(1)}, u32[]{:S(2)}, u32[]{:S(2)}) collective-permute-start(bf16[1024,128]{1,0:T(8,128)(2,1)S(1)} %constant_dynamic-update-slice_fusion.kv.refs_4_), channel_id=1, source_target_pairs={{0,8},{4,12},{8,16},{12,20},{16,24},{20,28},{24,32},{28,36},{32,40... | collective-permute-start | bytes 786440 | tf_op jit(solution)/shard_map/ppermute | solution.py:56
  7.2 8.1 %collective-permute-start.1 = (bf16[1024,128]{1,0:T(8,128)(2,1)S(1)}, bf16[1024,128]{1,0:T(8,128)(2,1)S(1)}, u32[]{:S(2)}, u32[]{:S(2)}) collective-permute-start(bf16[1024,128]{1,0:T(8,128)(2,1)S(1)} %constant_dynamic-update-slice_fusion.kv.refs_4_), channel_id=1, source_target_pairs={{0,4},{4,0},{8,12},{12,8},{16,20},{20,16},{24,28},{28,24},{32,36},... | collective-permute-start | bytes 786440 | tf_op jit(solution)/shard_map/ppermute | solution.py:50
  7.3 21.3 %collective-permute-start.16 = (bf16[256,1024]{1,0:T(8,128)(2,1)S(1)}, bf16[256,1024]{1,0:T(8,128)(2,1)}, u32[]{:S(2)}, u32[]{:S(2)}) collective-permute-start(bf16[256,1024]{1,0:T(8,128)(2,1)S(1)} %get-tuple-element.52.refs_1_), channel_id=1, source_target_pairs={{0,3},{1,0},{2,1},{3,2},{4,7},{5,4},{6,5},{7,6},{8,11},{9,8},{10,9... | collective-permute-start | bytes 1572872 | tf_op jit(solution)/shard_map/ppermute | solution.py:61
  13.6 44.4 %collective-permute-start.20 = (bf16[256,1024]{1,0:T(8,128)(2,1)S(1)}, bf16[256,1024]{1,0:T(8,128)(2,1)}, u32[]{:S(2)}, u32[]{:S(2)}) collective-permute-start(bf16[256,1024]{1,0:T(8,128)(2,1)S(1)} %get-tuple-element.52.refs_1_), channel_id=1, source_target_pairs={{0,1},{1,2},{2,3},{3,0},{4,5},{5,6},{6,7},{7,4},{8,9},{9,10},{10,1... | collective-permute-start | bytes 1572872 | tf_op jit(solution)/shard_map/ppermute | solution.py:61
  15.3 13.6 %collective-permute-start.2 = (bf16[1024,128]{1,0:T(8,128)(2,1)S(1)}, bf16[1024,128]{1,0:T(8,128)(2,1)S(1)}, u32[]{:S(2)}, u32[]{:S(2)}) collective-permute-start(bf16[1024,128]{1,0:T(8,128)(2,1)S(1)} %collective-permute-done.far.refs_5_), channel_id=1, source_target_pairs={{0,4},{4,0},{8,12},{12,8},{16,20},{20,16},{24,28},{28,24},{32,36},... | collective-permute-start | bytes 786440 | tf_op jit(solution)/shard_map/ppermute | solution.py:50
  17.1 41.1 %collective-permute-start.18 = (bf16[256,1024]{1,0:T(8,128)(2,1)}, bf16[256,1024]{1,0:T(8,128)(2,1)}, u32[]{:S(2)}, u32[]{:S(2)}) collective-permute-start(bf16[256,1024]{1,0:T(8,128)(2,1)} %collective-permute-done.17.refs_6_), channel_id=1, source_target_pairs={{0,1},{1,2},{2,3},{3,0},{4,5},{5,6},{6,7},{7,4},{8,9},{9,10},{10,1... | collective-permute-start | bytes 1572872 | tf_op jit(solution)/shard_map/ppermute | solution.py:61
  28.6 29.7 %collective-permute-start.19 = (bf16[256,1024]{1,0:T(8,128)(2,1)}, bf16[256,1024]{1,0:T(8,128)(2,1)S(1)}, u32[]{:S(2)}, u32[]{:S(2)}) collective-permute-start(bf16[256,1024]{1,0:T(8,128)(2,1)} %collective-permute-done.16.refs_3_), channel_id=1, source_target_pairs={{0,3},{1,0},{2,1},{3,2},{4,7},{5,4},{6,5},{7,6},{8,11},{9,8},{10,9... | collective-permute-start | bytes 1572872 | tf_op jit(solution)/shard_map/ppermute | solution.py:61
  43.3 30.4 %collective-permute-start.7 = (bf16[512,512]{1,0:T(8,128)(2,1)S(1)}, bf16[512,512]{1,0:T(8,128)(2,1)S(1)}, u32[]{:S(2)}, u32[]{:S(2)}) collective-permute-start(bf16[512,512]{1,0:T(8,128)(2,1)S(1)} %get-tuple-element.27.refs_4_), channel_id=1, source_target_pairs={{0,8},{4,12},{8,0},{12,4},{16,24},{20,28},{24,16},{28,20},{32,40},... | collective-permute-start | bytes 1572872 | tf_op jit(solution)/shard_map/ppermute | solution.py:50
  43.5 30.5 %collective-permute-start.6 = (bf16[512,512]{1,0:T(8,128)(2,1)S(1)}, bf16[512,512]{1,0:T(8,128)(2,1)S(1)}, u32[]{:S(2)}, u32[]{:S(2)}) collective-permute-start(bf16[512,512]{1,0:T(8,128)(2,1)S(1)} %get-tuple-element.27.refs_4_), channel_id=1, source_target_pairs={{0,4},{4,0},{8,12},{12,8},{16,20},{20,16},{24,28},{28,24},{32,36},... | collective-permute-start | bytes 1572872 | tf_op jit(solution)/shard_map/ppermute | solution.py:50
  58.0 16.1 %collective-permute-start.4 = (bf16[512,512]{1,0:T(8,128)(2,1)S(1)}, bf16[512,512]{1,0:T(8,128)(2,1)S(1)}, u32[]{:S(2)}, u32[]{:S(2)}) collective-permute-start(bf16[512,512]{1,0:T(8,128)(2,1)S(1)} %get-tuple-element.26.refs_0_), channel_id=1, source_target_pairs={{0,8},{4,12},{8,0},{12,4},{16,24},{20,28},{24,16},{28,20},{32,40},... | collective-permute-start | bytes 1572872 | tf_op jit(solution)/shard_map/ppermute | solution.py:50
  58.1 16.3 %collective-permute-start.3 = (bf16[512,512]{1,0:T(8,128)(2,1)S(1)}, bf16[512,512]{1,0:T(8,128)(2,1)S(1)}, u32[]{:S(2)}, u32[]{:S(2)}) collective-permute-start(bf16[512,512]{1,0:T(8,128)(2,1)S(1)} %get-tuple-element.26.refs_0_), channel_id=1, source_target_pairs={{0,4},{4,0},{8,12},{12,8},{16,20},{20,16},{24,28},{28,24},{32,36},... | collective-permute-start | bytes 1572872 | tf_op jit(solution)/shard_map/ppermute | solution.py:50
  71.6 15.1 %collective-permute-start.22 = (bf16[512,512]{1,0:T(8,128)(2,1)S(1)}, bf16[512,512]{1,0:T(8,128)(2,1)S(1)}, u32[]{:S(2)}, u32[]{:S(2)}) collective-permute-start(bf16[512,512]{1,0:T(8,128)(2,1)S(1)} %get-tuple-element.37.refs_8_), channel_id=1, source_target_pairs={{0,8},{4,12},{8,0},{12,4},{16,24},{20,28},{24,16},{28,20},{32,40},... | collective-permute-start | bytes 1572872 | tf_op jit(solution)/shard_map/ppermute | solution.py:50
  73.8 23.8 %collective-permute-start.25 = (bf16[512,512]{1,0:T(8,128)(2,1)S(1)}, bf16[512,512]{1,0:T(8,128)(2,1)S(1)}, u32[]{:S(2)}, u32[]{:S(2)}) collective-permute-start(bf16[512,512]{1,0:T(8,128)(2,1)S(1)} %get-tuple-element.41.refs_8_), channel_id=1, source_target_pairs={{0,8},{4,12},{8,0},{12,4},{16,24},{20,28},{24,16},{28,20},{32,40},... | collective-permute-start | bytes 1572872 | tf_op jit(solution)/shard_map/ppermute | solution.py:50
  73.9 23.7 %collective-permute-start.8 = (bf16[512,512]{1,0:T(8,128)(2,1)S(1)}, bf16[512,512]{1,0:T(8,128)(2,1)S(1)}, u32[]{:S(2)}, u32[]{:S(2)}) collective-permute-start(bf16[512,512]{1,0:T(8,128)(2,1)S(1)} %collective-permute-done.7.refs_6_), channel_id=1, source_target_pairs={{0,4},{4,0},{8,12},{12,8},{16,20},{20,16},{24,28},{28,24},{32,36},... | collective-permute-start | bytes 1572872 | tf_op jit(solution)/shard_map/ppermute | solution.py:50
  74.1 24.0 %collective-permute-start.5 = (bf16[512,512]{1,0:T(8,128)(2,1)S(1)}, bf16[512,512]{1,0:T(8,128)(2,1)S(1)}, u32[]{:S(2)}, u32[]{:S(2)}) collective-permute-start(bf16[512,512]{1,0:T(8,128)(2,1)S(1)} %collective-permute-done.4.refs_2_), channel_id=1, source_target_pairs={{0,4},{4,0},{8,12},{12,8},{16,20},{20,16},{24,28},{28,24},{32,36},... | collective-permute-start | bytes 1572872 | tf_op jit(solution)/shard_map/ppermute | solution.py:50
  74.4 30.2 %collective-permute-start.21 = (bf16[512,512]{1,0:T(8,128)(2,1)S(1)}, bf16[512,512]{1,0:T(8,128)(2,1)S(1)}, u32[]{:S(2)}, u32[]{:S(2)}) collective-permute-start(bf16[512,512]{1,0:T(8,128)(2,1)S(1)} %get-tuple-element.37.refs_8_), channel_id=1, source_target_pairs={{0,4},{4,0},{8,12},{12,8},{16,20},{20,16},{24,28},{28,24},{32,36},... | collective-permute-start | bytes 1572872 | tf_op jit(solution)/shard_map/ppermute | solution.py:50
  86.7 20.3 %collective-permute-start.23 = (bf16[512,512]{1,0:T(8,128)(2,1)S(1)}, bf16[512,512]{1,0:T(8,128)(2,1)S(1)}, u32[]{:S(2)}, u32[]{:S(2)}) collective-permute-start(bf16[512,512]{1,0:T(8,128)(2,1)S(1)} %collective-permute-done.22.refs_10_), channel_id=1, source_target_pairs={{0,4},{4,0},{8,12},{12,8},{16,20},{20,16},{24,28},{28,24},{32,36},... | collective-permute-start | bytes 1572872 | tf_op jit(solution)/shard_map/ppermute | solution.py:50
  97.6 25.2 %collective-permute-start.24 = (bf16[512,512]{1,0:T(8,128)(2,1)S(1)}, bf16[512,512]{1,0:T(8,128)(2,1)S(1)}, u32[]{:S(2)}, u32[]{:S(2)}) collective-permute-start(bf16[512,512]{1,0:T(8,128)(2,1)S(1)} %get-tuple-element.41.refs_8_), channel_id=1, source_target_pairs={{0,4},{4,0},{8,12},{12,8},{16,20},{20,16},{24,28},{28,24},{32,36},... | collective-permute-start | bytes 1572872 | tf_op jit(solution)/shard_map/ppermute | solution.py:50
  97.6 25.2 %collective-permute-start.26 = (bf16[512,512]{1,0:T(8,128)(2,1)S(1)}, bf16[512,512]{1,0:T(8,128)(2,1)S(1)}, u32[]{:S(2)}, u32[]{:S(2)}) collective-permute-start(bf16[512,512]{1,0:T(8,128)(2,1)S(1)} %collective-permute-done.25.refs_10_), channel_id=1, source_target_pairs={{0,4},{4,0},{8,12},{12,8},{16,20},{20,16},{24,28},{28,24},{32,36},... | collective-permute-start | bytes 1572872 | tf_op jit(solution)/shard_map/ppermute | solution.py:50
  103.7 48.7 %collective-permute-start.10 = (bf16[512,512]{1,0:T(8,128)(2,1)S(1)}, bf16[512,512]{1,0:T(8,128)(2,1)S(1)}, u32[]{:S(2)}, u32[]{:S(2)}) collective-permute-start(bf16[512,512]{1,0:T(8,128)(2,1)S(1)} %get-tuple-element.30), channel_id=1, source_target_pairs={{0,3},{1,0},{2,1},{3,2},{4,7},{5,4},{6,5},{7,6},{8,11},{9,8},{10,9... | collective-permute-start | bytes 1572872 | tf_op jit(solution)/shard_map/ppermute | solution.py:61
  104.6 48.1 %collective-permute-start.9 = (bf16[512,512]{1,0:T(8,128)(2,1)S(1)}, bf16[512,512]{1,0:T(8,128)(2,1)S(1)}, u32[]{:S(2)}, u32[]{:S(2)}) collective-permute-start(bf16[512,512]{1,0:T(8,128)(2,1)S(1)} %get-tuple-element.29), channel_id=1, source_target_pairs={{0,1},{1,2},{2,3},{3,0},{4,5},{5,6},{6,7},{7,4},{8,9},{9,10},{10,1... | collective-permute-start | bytes 1572872 | tf_op jit(solution)/shard_map/ppermute | solution.py:61
  122.0 0.9 copy-start.2
  122.8 19.4 %copy-start.1 = (bf16[512,1024]{1,0:T(8,128)(2,1)S(1)}, bf16[512,1024]{1,0:T(8,128)(2,1)}, u32[]{:S(2)}) copy-start(bf16[512,1024]{1,0:T(8,128)(2,1)} %get-tuple-element.28.rows) | copy-start | bytes 3145732
  138.3 21.8 %collective-permute-start.27 = (bf16[1024,128]{1,0:T(8,128)(2,1)S(1)}, bf16[1024,128]{1,0:T(8,128)(2,1)S(1)}, u32[]{:S(2)}, u32[]{:S(2)}) collective-permute-start(bf16[1024,128]{1,0:T(8,128)(2,1)S(1)} %get-tuple-element.46), channel_id=1, source_target_pairs={{4,0},{8,4},{12,8},{16,12},{20,16},{24,20},{28,24},{32,28},{36,32}... | collective-permute-start | bytes 786440 | tf_op jit(solution)/shard_map/ppermute | solution.py:56
  140.3 21.0 %collective-permute-start.28 = (bf16[1024,128]{1,0:T(8,128)(2,1)S(1)}, bf16[1024,128]{1,0:T(8,128)(2,1)S(1)}, u32[]{:S(2)}, u32[]{:S(2)}) collective-permute-start(bf16[1024,128]{1,0:T(8,128)(2,1)S(1)} %get-tuple-element.47), channel_id=1, source_target_pairs={{8,0},{12,4},{16,8},{20,12},{24,16},{28,20},{32,24},{36,28},{40,32... | collective-permute-start | bytes 786440 | tf_op jit(solution)/shard_map/ppermute | solution.py:56
  150.6 14.8 %collective-permute-start.12 = (bf16[512,512]{1,0:T(8,128)(2,1)S(1)}, bf16[512,512]{1,0:T(8,128)(2,1)S(1)}, u32[]{:S(2)}, u32[]{:S(2)}) collective-permute-start(bf16[512,512]{1,0:T(8,128)(2,1)S(1)} %get-tuple-element.32), channel_id=1, source_target_pairs={{0,1},{1,2},{2,3},{3,0},{4,5},{5,6},{6,7},{7,4},{8,9},{9,10},{10,1... | collective-permute-start | bytes 1572872 | tf_op jit(solution)/shard_map/ppermute | solution.py:61
  152.4 16.0 %collective-permute-start.13 = (bf16[512,512]{1,0:T(8,128)(2,1)S(1)}, bf16[512,512]{1,0:T(8,128)(2,1)S(1)}, u32[]{:S(2)}, u32[]{:S(2)}) collective-permute-start(bf16[512,512]{1,0:T(8,128)(2,1)S(1)} %get-tuple-element.33), channel_id=1, source_target_pairs={{0,3},{1,0},{2,1},{3,2},{4,7},{5,4},{6,5},{7,6},{8,11},{9,8},{10,9... | collective-permute-start | bytes 1572872 | tf_op jit(solution)/shard_map/ppermute | solution.py:61
  157.2 19.1 %collective-permute-start.11 = (bf16[512,512]{1,0:T(8,128)(2,1)S(1)}, bf16[512,512]{1,0:T(8,128)(2,1)S(1)}, u32[]{:S(2)}, u32[]{:S(2)}) collective-permute-start(bf16[512,512]{1,0:T(8,128)(2,1)S(1)} %get-tuple-element.31), channel_id=1, source_target_pairs={{0,1},{1,2},{2,3},{3,0},{4,5},{5,6},{6,7},{7,4},{8,9},{9,10},{10,1... | collective-permute-start | bytes 1572872 | tf_op jit(solution)/shard_map/ppermute | solution.py:61
  160.1 18.8 %collective-permute-start.14 = (bf16[512,512]{1,0:T(8,128)(2,1)S(1)}, bf16[512,512]{1,0:T(8,128)(2,1)S(1)}, u32[]{:S(2)}, u32[]{:S(2)}) collective-permute-start(bf16[512,512]{1,0:T(8,128)(2,1)S(1)} %get-tuple-element.34), channel_id=1, source_target_pairs={{0,3},{1,0},{2,1},{3,2},{4,7},{5,4},{6,5},{7,6},{8,11},{9,8},{10,9... | collective-permute-start | bytes 1572872 | tf_op jit(solution)/shard_map/ppermute | solution.py:61

commit v2 on v0

v2 whole, which is shorter than its diff:
```python
import math

import jax
import jax.numpy as jnp
from jax import lax
from jax.experimental import pallas as pl
from jax.experimental.pallas import tpu as pltpu
from jax.sharding import PartitionSpec as P

HD = 128
BLOCK = 128
BLK_DEV = 4
MAXB = 8
GROUP = 4
PRIOR = MAXB - 1
POOL = PRIOR + BLK_DEV
ROWS = BLOCK * BLK_DEV
WIDTH = 1024
FAR_ROWS = (PRIOR - BLK_DEV) * BLOCK
CHUNKS = 2
CW = WIDTH // CHUNKS
FW = 512
BW = 512

SCALE = 1.0 / math.sqrt(HD)
SCALE_LOG2 = SCALE * math.log2(math.e)
MASKED = -1e30

START, GRAD_REL, GRAD_IDX, ATT_REL, ATT_IDX, CORE, TP = 0, 4, 8, 12, 16, 20, 21

ANY = pl.BlockSpec(memory_space=pl.ANY)
WHOLE = pl.BlockSpec(memory_space=pltpu.VMEM)
HBM = pl.BlockSpec(memory_space=pltpu.HBM)
SMEM = pl.BlockSpec(memory_space=pltpu.SMEM)
VMEM_LIMIT = 48 * 1024 * 1024


PARAMS = pltpu.CompilerParams(vmem_limit_bytes=VMEM_LIMIT)


def lasting(us):
    return pl.CostEstimate(
        flops=int(us * 1.15e9), bytes_accessed=int(us * 3.6e6), transcendentals=0
    )


def dot(a, b):
    return jnp.dot(a, b, preferred_element_type=jnp.float32)


def dot_nt(a, b):
    return lax.dot_general(a, b, (((1,), (1,)), ((), ())), preferred_element_type=jnp.float32)


def swap_cp(block, mask):
    count = lax.axis_size("cp")
    return lax.ppermute(block, "cp", [(i, i ^ mask) for i in range(count)])


def shift_cp(block, distance):
    count = lax.axis_size("cp")
    route = [(i, i + distance) for i in range(count) if 0 <= i + distance < count]
    return lax.ppermute(block, "cp", route)


def shift_tp(block, distance):
    count = lax.axis_size("tp")
    return lax.ppermute(block, "tp", [(i, (i + distance) % count) for i in range(count)])


def pool_copies(kv, far, near, keys, values, sems):
    copies = []
    for src, row, rows, place in (
        (kv, 0, ROWS, PRIOR * BLOCK),
        (far, 0, FAR_ROWS, 0),
        (near, 0, ROWS, ROWS - BLOCK),
    ):
        for col, pool in ((0, keys), (HD, values)):
            copies.append(
                pltpu.make_async_copy(
                    src.at[pl.ds(row, rows), pl.ds(col, HD)],
                    pool.at[pl.ds(place, rows)],
                    sems.at[len(copies)],
                )
            )
    return copies


def block_rows(b):
    return pl.ds(pl.multiple_of(b * BLOCK, BLOCK), BLOCK)


def first_mask(odd, width):
    key_pos = lax.broadcasted_iota(jnp.int32, (256, width), 0)
    row_pos = lax.broadcasted_iota(jnp.int32, (256, width), 1) % BLOCK + BLOCK
    return (key_pos <= row_pos) & (key_pos >= odd * BLOCK)


def flipped_heads(block):
    heads = block.shape[1] // HD
    return jnp.concatenate([block[:, h * HD : (h + 1) * HD].T for h in range(heads)], axis=1)


def stacked_heads(block):
    heads = block.shape[1] // HD
    return jnp.concatenate([block[:, h * HD : (h + 1) * HD] for h in range(heads)], axis=0)


def tiles_of(table, b):
    diag = PRIOR + b
    count = diag - jnp.maximum(table[START + b], 0) + 1
    return (count + 1) // 2, count % 2, diag


def low_of(step, odd, diag):
    block = diag - 1 - 2 * step + jnp.where(step > 0, odd, 0)
    return pl.multiple_of(block * BLOCK, BLOCK)


def forward_kernel(
    chunk, table, q_hbm, kv, far, near, att_hbm, att_t_hbm, total_ref,
    keys, values, q_ref, att, att_t, sems, out_sems,
):
    copies = [pltpu.make_async_copy(q_hbm.at[:, pl.ds(chunk * CW, CW)], q_ref, sems.at[6])]
    copies += pool_copies(kv, far, near, keys, values, sems)
    for copy in copies:
        copy.start()
    for copy in copies:
        copy.wait()

    def outward(b):
        return [
            pltpu.make_async_copy(att.at[block_rows(b)], att_hbm.at[block_rows(b)], out_sems.at[b]),
            pltpu.make_async_copy(att_t.at[b], att_t_hbm.at[b], out_sems.at[BLK_DEV + b]),
        ]

    groups = [slice(at, at + FW) for at in range(0, CW, FW)]

    def block(b, _):
        steps, odd, diag = tiles_of(table, b)
        q_t = [flipped_heads(q_ref[block_rows(b), cols]) for cols in groups]

        def tile(step, mask, carry):
            low = low_of(step, odd, diag)
            k = keys[pl.ds(low, 256), :]
            v_t = values[pl.ds(low, 256), :].T
            result = []
            for at in range(len(groups)):
                s = dot(k, q_t[at]) * SCALE_LOG2
                if carry is None:
                    s = jnp.where(mask, s, MASKED)
                    top = jnp.max(s, axis=0, keepdims=True)
                    p = jnp.exp2(s - top)
                    total = jnp.sum(p, axis=0, keepdims=True)
                    acc = dot(v_t, p.astype(jnp.bfloat16))
                else:
                    top_old, total, acc = carry[at]
                    top = jnp.maximum(top_old, jnp.max(s, axis=0, keepdims=True))
                    fade = jnp.exp2(top_old - top)
                    p = jnp.exp2(s - top)
                    total = total * fade + jnp.sum(p, axis=0, keepdims=True)
                    acc = acc * fade + dot(v_t, p.astype(jnp.bfloat16))
                result.append((top, total, acc))
            return result

        carry = tile(0, first_mask(odd, FW), None)
        carry = lax.fori_loop(1, steps, lambda step, carry: tile(step, None, carry), carry)
        for cols, (top, total, acc) in zip(groups, carry):
            out = (acc * (1.0 / total)).astype(jnp.bfloat16)
            att_t[b, :, cols] = out
            for head in range(FW // HD):
                at = cols.start + head * HD
                att[block_rows(b), at : at + HD] = out[:, head * HD : (head + 1) * HD].T
            total_ref[b, :, cols] = top + jnp.log2(total)
        for copy in outward(b):
            copy.start()
        return _

    lax.fori_loop(0, BLK_DEV, block, 0)
    for b in range(BLK_DEV):
        for copy in outward(b):
            copy.wait()


def forward(table, queries, kv, far, near, chunk):
    def kernel(*refs):
        forward_kernel(chunk, *refs)

    return pl.pallas_call(
        kernel,
        in_specs=[SMEM] + [ANY] * 4,
        out_specs=[ANY, ANY, WHOLE],
        out_shape=[
            jax.ShapeDtypeStruct((ROWS, CW), jnp.bfloat16),
            jax.ShapeDtypeStruct((BLK_DEV, HD, CW), jnp.bfloat16),
            jax.ShapeDtypeStruct((BLK_DEV, 1, CW), jnp.float32),
        ],
        scratch_shapes=[
            pltpu.VMEM((POOL * BLOCK, HD), jnp.bfloat16),
            pltpu.VMEM((POOL * BLOCK, HD), jnp.bfloat16),
            pltpu.VMEM((ROWS, CW), jnp.bfloat16),
            pltpu.VMEM((ROWS, CW), jnp.bfloat16),
            pltpu.VMEM((BLK_DEV, HD, CW), jnp.bfloat16),
            pltpu.SemaphoreType.DMA((7,)),
            pltpu.SemaphoreType.DMA((2 * BLK_DEV,)),
        ],
        compiler_params=PARAMS,
        cost_estimate=lasting(8),
        name="attention_forward",
    )(table, queries, kv, far, near)


def start_chosen(rel, index, sources, place, sem, col=0):
    for at, source in enumerate(sources):
        @pl.when(rel == at)
        def _():
            pltpu.make_async_copy(
                source.at[pl.ds(pl.multiple_of(index * BLOCK, BLOCK), BLOCK)], place, sem
            ).start()


def backward_kernel(chunk, last, first, *refs):
    refs = list(refs)
    table, q_hbm, att_t_hbm, total_ref, kv, far, near = refs[:7]
    sources = refs[7:11]
    refs = refs[11:]
    if not first:
        key_in, value_in = refs[1:3]
        refs = refs[3:]
    dq_hbm = refs[0]
    if last:
        own_ref, near_ref, far_ref = refs[1:4]
        refs = refs[4:]
        key_acc, value_acc = refs[:2]
    else:
        key_acc, value_acc = refs[1:3]
        refs = refs[3:]
    keys, values, q_ref, att_t, grads, dq, sems, grad_sems, out_sems = refs[-9:]

    incoming = [
        pltpu.make_async_copy(q_hbm.at[:, pl.ds(chunk * CW, CW)], q_ref, sems.at[6]),
        pltpu.make_async_copy(att_t_hbm, att_t, sems.at[7]),
    ]
    if not first:
        incoming += [
            pltpu.make_async_copy(key_in, key_acc, sems.at[8]),
            pltpu.make_async_copy(value_in, value_acc, sems.at[9]),
        ]
    incoming += pool_copies(kv, far, near, keys, values, sems)
    for at in range(BLK_DEV):
        start_chosen(
            table[GRAD_REL + at], table[GRAD_IDX + at], sources, grads.at[block_rows(at)], grad_sems.at[at]
        )
    for copy in incoming:
        copy.start()
    if first:
        key_acc[...] = jnp.zeros_like(key_acc)
        value_acc[...] = jnp.zeros_like(value_acc)
    for copy in incoming:
        copy.wait()
    for at in range(BLK_DEV):
        pltpu.make_async_copy(
            sources[0].at[pl.ds(0, BLOCK)], grads.at[block_rows(at)], grad_sems.at[at]
        ).wait()

    def outward(b):
        return pltpu.make_async_copy(
            dq.at[block_rows(b)], dq_hbm.at[block_rows(b), pl.ds(chunk * CW, CW)], out_sems.at[b]
        )

    groups = [slice(at, at + BW) for at in range(0, CW, BW)]

    def block(b, _):
        steps, odd, diag = tiles_of(table, b)
        held = []
        for cols in groups:
            q = q_ref[block_rows(b), cols]
            g = grads[block_rows(b), cols]
            g_t = flipped_heads(g)
            delta = jnp.sum(
                g_t.astype(jnp.float32) * att_t[b, :, cols].astype(jnp.float32),
                axis=0,
                keepdims=True,
            )
            held.append(
                (flipped_heads(q), stacked_heads(q), g_t, stacked_heads(g), delta, total_ref[b, :, cols])
            )

        def tile(step, mask, carry):
            low = low_of(step, odd, diag)
            k = keys[pl.ds(low, 256), :]
            k_t = k.T
            v = values[pl.ds(low, 256), :]
            result = []
            key_part = value_part = None
            for at, (q_t, q_s, g_t, g_s, delta, log_total) in enumerate(held):
                s = dot(k, q_t) * SCALE_LOG2
                if mask is not None:
                    s = jnp.where(mask, s, MASKED)
                p = jnp.exp2(s - log_total).astype(jnp.bfloat16)
                dp = dot(v, g_t)
                ds = (p.astype(jnp.float32) * (dp - delta)).astype(jnp.bfloat16)
                value_term, key_term, query_term = dot(p, g_s), dot(ds, q_s), dot(k_t, ds)
                value_part = value_term if value_part is None else value_part + value_term
                key_part = key_term if key_part is None else key_part + key_term
                result.append(query_term if carry is None else carry[at] + query_term)
            value_acc[pl.ds(low, 256), :] += value_part
            key_acc[pl.ds(low, 256), :] += key_part
            return result

        carry = tile(0, first_mask(odd, BW), None)
        carry = lax.fori_loop(1, steps, lambda step, carry: tile(step, None, carry), carry)
        for cols, dq_t in zip(groups, carry):
            dq_t = (dq_t * SCALE).astype(jnp.bfloat16)
            for head in range(BW // HD):
                at = cols.start + head * HD
                dq[block_rows(b), at : at + HD] = dq_t[:, head * HD : (head + 1) * HD].T
        outward(b).start()
        return _

    lax.fori_loop(0, BLK_DEV, block, 0)

    if last:
        near_at = ROWS - BLOCK
        own_at = PRIOR * BLOCK
        for acc, cols, factor in ((key_acc, slice(0, HD), SCALE), (value_acc, slice(HD, 2 * HD), 1.0)):
            own_ref[:, cols] = acc[own_at:] * factor
            near_ref[:, cols] = (acc[near_at:own_at] * factor).astype(jnp.bfloat16)
            far_ref[:, cols] = (acc[:near_at] * factor).astype(jnp.bfloat16)
    for b in range(BLK_DEV):
        outward(b).wait()


def backward(table, queries, att_t, totals, pool, sources, carried, chunk, last):
    first = carried is None
    pool_shape = (POOL * BLOCK, HD)
    sums = [jax.ShapeDtypeStruct(pool_shape, jnp.float32)] * 2
    if last:
        out_shape = [
            jax.ShapeDtypeStruct((ROWS, 2 * HD), jnp.float32),
            jax.ShapeDtypeStruct((ROWS, 2 * HD), jnp.bfloat16),
            jax.ShapeDtypeStruct((FAR_ROWS, 2 * HD), jnp.bfloat16),
        ]
        scratch = [pltpu.VMEM(pool_shape, jnp.float32)] * 2
    else:
        out_shape, scratch = sums, []

    def kernel(*refs):
        backward_kernel(chunk, last, first, *refs)

    return pl.pallas_call(
        kernel,
        in_specs=[SMEM, ANY, ANY, WHOLE] + [ANY] * (7 if first else 10),
        out_specs=[ANY] + [WHOLE] * len(out_shape),
        out_shape=[jax.ShapeDtypeStruct((ROWS, WIDTH), jnp.bfloat16)] + out_shape,
        input_output_aliases={} if first else {11: 0},
        scratch_shapes=scratch
        + [
            pltpu.VMEM(pool_shape, jnp.bfloat16),
            pltpu.VMEM(pool_shape, jnp.bfloat16),
            pltpu.VMEM((ROWS, CW), jnp.bfloat16),
            pltpu.VMEM((BLK_DEV, HD, CW), jnp.bfloat16),
            pltpu.VMEM((ROWS, CW), jnp.bfloat16),
            pltpu.VMEM((ROWS, CW), jnp.bfloat16),
            pltpu.SemaphoreType.DMA((10,)),
            pltpu.SemaphoreType.DMA((BLK_DEV,)),
            pltpu.SemaphoreType.DMA((BLK_DEV,)),
        ],
        compiler_params=PARAMS,
        cost_estimate=lasting(9),
        name="attention_backward",
    )(table, queries, att_t, totals, *pool, *sources, *([] if first else carried))


def grad_matmul_kernel(chunk, table, *refs):
    pieces, weight_hbm, out, weight, sems = refs[:8], *refs[8:]
    half = ROWS // 2
    copies = []
    for ahead in range(4):
        at = pl.multiple_of(((table[TP] + ahead) % 4) * WIDTH, WIDTH)
        copies.append(
            pltpu.make_async_copy(
                weight_hbm.at[pl.ds(chunk * CW, CW), pl.ds(at, WIDTH)],
                weight.at[ahead],
                sems.at[ahead],
            )
        )
        copies[-1].start()
    totals = [None, None]
    for ahead in range(4):
        copies[ahead].wait()
        for part in range(2):
            term = dot_nt(pieces[2 * ahead + part][...], weight[ahead])
            totals[part] = term if totals[part] is None else totals[part] + term
    for part in range(2):
        out[part * half : (part + 1) * half] = totals[part].astype(jnp.bfloat16)


def grad_matmul(table, pieces, weight, chunk):
    def kernel(*refs):
        grad_matmul_kernel(chunk, *refs)

    return pl.pallas_call(
        kernel,
        in_specs=[SMEM] + [WHOLE] * 8 + [ANY],
        out_specs=WHOLE,
        out_shape=jax.ShapeDtypeStruct((ROWS, CW), jnp.bfloat16),
        scratch_shapes=[
            pltpu.VMEM((4, CW, WIDTH), jnp.bfloat16),
            pltpu.SemaphoreType.DMA((4,)),
        ],
        compiler_params=PARAMS,
        cost_estimate=lasting(4),
        name="grad_projection",
    )(table, *pieces, weight)


HALF = WIDTH // 2


def weight_copy(table, weight_hbm, weight, slot, ahead, half, sem):
    at = pl.multiple_of(((table[TP] + ahead) % 4) * WIDTH + half * HALF, HALF)
    return pltpu.make_async_copy(weight_hbm.at[:, pl.ds(at, HALF)], weight.at[slot], sem)


def product_kernel(table, *refs):
    sources = [refs[4 * c : 4 * c + 4] for c in range(CHUNKS)]
    weight_hbm, left, right, onward, back, own, rows, weight, sems, weight_sems = refs[4 * CHUNKS :]

    def place(c, at):
        return rows.at[block_rows(at), pl.ds(c * CW, CW)]

    places = [(c, at, c * BLK_DEV + at) for c in range(CHUNKS) for at in range(BLK_DEV)]
    for c, at, sem in places:
        start_chosen(
            table[ATT_REL + at], table[ATT_IDX + at], sources[c], place(c, at), sems.at[sem]
        )
    parts = ((2, 0), (2, 1), (1, 1), (3, 0), (0, 0), (0, 1))
    weights = [
        weight_copy(table, weight_hbm, weight, slot, ahead, half, weight_sems.at[slot])
        for slot, (ahead, half) in enumerate(parts)
    ]
    for copy in weights:
        copy.start()
    for c, at, sem in places:
        pltpu.make_async_copy(sources[c][0].at[pl.ds(0, BLOCK)], place(c, at), sems.at[sem]).wait()
    for slot, out in enumerate((left, right, onward, back)):
        weights[slot].wait()
        out[...] = dot(rows[...], weight[slot]).astype(jnp.bfloat16)
    for slot in (4, 5):
        weights[slot].wait()
        own[:, (slot - 4) * HALF : (slot - 3) * HALF] = dot(rows[...], weight[slot]).astype(
            jnp.bfloat16
        )


def products(table, sources, weight):
    flat = [source for group in sources for source in group]
    return pl.pallas_call(
        product_kernel,
        in_specs=[SMEM] + [ANY] * (4 * CHUNKS + 1),
        out_specs=[WHOLE] * 6,
        out_shape=[jax.ShapeDtypeStruct((ROWS, HALF), jnp.bfloat16)] * 4
        + [jax.ShapeDtypeStruct((ROWS, WIDTH), jnp.bfloat16)] * 2,
        scratch_shapes=[
            pltpu.VMEM((6, WIDTH, HALF), jnp.bfloat16),
            pltpu.SemaphoreType.DMA((4 * CHUNKS,)),
            pltpu.SemaphoreType.DMA((6,)),
        ],
        compiler_params=PARAMS,
        cost_estimate=lasting(7),
        name="products",
    )(table, *flat, weight)


def sum_product_kernel(table, rows, weight_hbm, before, after_, onward, back, weight, sems):
    weights = [
        weight_copy(table, weight_hbm, weight, 0, 1, 0, sems.at[0]),
        weight_copy(table, weight_hbm, weight, 1, 3, 1, sems.at[1]),
    ]
    for copy in weights:
        copy.start()
    for slot, (extra, out) in enumerate(((before, onward), (after_, back))):
        weights[slot].wait()
        value = dot(rows[...], weight[slot])
        out[...] = (value + extra[...].astype(jnp.float32)).astype(jnp.bfloat16)


def sum_products(table, rows, weight, before, after):
    half = jax.ShapeDtypeStruct((ROWS, HALF), jnp.bfloat16)
    return pl.pallas_call(
        sum_product_kernel,
        in_specs=[SMEM, WHOLE, ANY, WHOLE, WHOLE],
        out_specs=[WHOLE] * 2,
        out_shape=[half] * 2,
        scratch_shapes=[
            pltpu.VMEM((2, WIDTH, HALF), jnp.bfloat16),
            pltpu.SemaphoreType.DMA((2,)),
        ],
        compiler_params=PARAMS,
        cost_estimate=lasting(4),
        name="sum_products",
    )(table, rows, weight, before, after)


def last_sum_kernel(own, before_a, before_b, after_a, after_b, out):
    for half, before, after in ((0, before_a, after_a), (1, before_b, after_b)):
        cols = slice(half * 512, (half + 1) * 512)
        out[:, cols] = (
            own[:, cols].astype(jnp.float32) + before[...].astype(jnp.float32) + after[...].astype(jnp.float32)
        ).astype(jnp.bfloat16)


def last_sum(own, before_a, before_b, after_a, after_b):
    part = pl.BlockSpec((BLOCK, 512), lambda j: (j, 0))
    full = pl.BlockSpec((BLOCK, WIDTH), lambda j: (j, 0))
    return pl.pallas_call(
        last_sum_kernel,
        grid=(4,),
        in_specs=[full, part, part, part, part],
        out_specs=full,
        out_shape=jax.ShapeDtypeStruct((ROWS, WIDTH), jnp.bfloat16),
        compiler_params=PARAMS,
        cost_estimate=lasting(2),
        name="last_sum",
    )(own, before_a, before_b, after_a, after_b)


def scalar_table(doc_start, balanced_source):
    device = lax.axis_index("cp")
    member = device % GROUP
    group_blocks = GROUP * BLK_DEV
    group_first = device // GROUP * group_blocks
    sources = lax.dynamic_slice_in_dim(balanced_source, group_first, group_blocks) - group_first
    slots = jnp.arange(group_blocks, dtype=jnp.int32)
    slot_of = jnp.sum(
        jnp.where(sources[None, :] == slots[:, None], slots[None, :], 0), axis=1, dtype=jnp.int32
    )
    mine = member * BLK_DEV
    wanted = lax.dynamic_slice_in_dim(sources, mine, BLK_DEV)
    held = lax.dynamic_slice_in_dim(slot_of, mine, BLK_DEV)
    starts = lax.dynamic_slice_in_dim(doc_start, device * BLK_DEV, BLK_DEV)
    starts = starts - (device * BLK_DEV - PRIOR)
    return jnp.concatenate(
        [
            starts,
            (held // BLK_DEV) ^ member,
            held % BLK_DEV,
            (wanted // BLK_DEV) ^ member,
            wanted % BLK_DEV,
            jnp.stack([device % 2, lax.axis_index("tp")]),
        ]
    ).astype(jnp.int32)


def group_exchange(block, earlier):
    across = swap_cp(block, 2)
    return [block, swap_cp(after(block, earlier), 1), across, swap_cp(after(across, earlier), 1)]


def copy_all(*pairs, sems):
    copies = [pltpu.make_async_copy(src, dst, sems.at[at]) for at, (src, dst) in enumerate(pairs)]
    for copy in copies:
        copy.start()
    for copy in copies:
        copy.wait()


def join_kernel(keys, values, kv, last, sems):
    tail = pl.ds(ROWS - FAR_ROWS, FAR_ROWS)
    left, right = pl.ds(0, HD), pl.ds(HD, HD)
    copy_all(
        (keys, kv.at[:, left]),
        (values, kv.at[:, right]),
        (keys.at[tail], last.at[:, left]),
        (values.at[tail], last.at[:, right]),
        sems=sems,
    )


def join(keys, values):
    return pl.pallas_call(
        join_kernel,
        in_specs=[HBM] * 2,
        out_specs=[WHOLE] * 2,
        out_shape=[
            jax.ShapeDtypeStruct((ROWS, 2 * HD), jnp.bfloat16),
            jax.ShapeDtypeStruct((FAR_ROWS, 2 * HD), jnp.bfloat16),
        ],
        scratch_shapes=[pltpu.SemaphoreType.DMA((4,))],
        compiler_params=PARAMS,
        cost_estimate=lasting(2),
        name="join",
    )(keys, values)


def halve_kernel(grads, upper, lower, sems):
    half = ROWS // 2
    copy_all(
        (grads.at[pl.ds(0, half)], upper), (grads.at[pl.ds(half, half)], lower), sems=sems
    )


def halve(grads):
    return pl.pallas_call(
        halve_kernel,
        in_specs=[HBM],
        out_specs=[WHOLE] * 2,
        out_shape=[jax.ShapeDtypeStruct((ROWS // 2, WIDTH), jnp.bfloat16)] * 2,
        scratch_shapes=[pltpu.SemaphoreType.DMA((2,))],
        compiler_params=PARAMS,
        cost_estimate=lasting(2),
        name="halve",
    )(grads)


def add_kernel(own, near, far, keys, values):
    total = own[...] + near[...].astype(jnp.float32)
    front = total[: ROWS - FAR_ROWS].astype(jnp.bfloat16)
    rear = (total[ROWS - FAR_ROWS :] + far[...].astype(jnp.float32)).astype(jnp.bfloat16)
    for col, out in ((0, keys), (HD, values)):
        out[: ROWS - FAR_ROWS] = front[:, col : col + HD]
        out[ROWS - FAR_ROWS :] = rear[:, col : col + HD]


def add_terms(own, near, far):
    return pl.pallas_call(
        add_kernel,
        in_specs=[WHOLE] * 3,
        out_specs=[WHOLE] * 2,
        out_shape=[jax.ShapeDtypeStruct((ROWS, HD), jnp.bfloat16)] * 2,
        compiler_params=PARAMS,
        cost_estimate=lasting(1),
        name="add_terms",
    )(own, near, far)


def after(value, earlier):
    return lax.optimization_barrier((value, earlier))[0]


def shards(queries, key_rows, value_rows, out_proj, grad_mixed, doc_start, balanced_source):
    table = scalar_table(doc_start, balanced_source)

    kv, last = join(key_rows, value_rows)
    far = shift_cp(last, 2)
    near = shift_cp(kv, 1)
    pool = (kv, far, near)

    upper, lower = halve(after(grad_mixed, kv))
    before_upper = shift_tp(upper, 1)
    after_lower = shift_tp(lower, -1)
    before_lower = shift_tp(lower, 1)
    after_upper = shift_tp(upper, -1)

    attended, attended_t, totals = [], [], []
    for chunk in range(CHUNKS):
        att, att_t, total = forward(
            after(table, (attended[0], before_upper, after_lower, before_lower, after_upper))
            if chunk
            else table,
            queries,
            *pool,
            chunk,
        )
        attended.append(att)
        attended_t.append(att_t)
        totals.append(total)

    arrived = (attended[0], before_lower, after_upper)
    opposite_upper = shift_tp(after(before_upper, arrived), 1)
    opposite_lower = shift_tp(after(after_lower, arrived), -1)
    pieces = [
        upper,
        lower,
        after_upper,
        after_lower,
        opposite_upper,
        opposite_lower,
        before_upper,
        before_lower,
    ]
    exchanged = [group_exchange(attended[0], attended[1]), None]
    grad_attended = [grad_matmul(table, pieces, out_proj, 0), None]
    exchanged[1] = group_exchange(attended[1], grad_attended[0])
    grad_across = swap_cp(grad_attended[0], 2)
    grad_attended[1] = grad_matmul(after(table, grad_attended[0]), pieces, out_proj, 1)

    far_left, far_right, onward_b, back_a, own, rows = products(
        after(table, grad_attended[1]), exchanged, out_proj
    )
    from_before = shift_tp(far_left, 1)
    from_after = shift_tp(far_right, -1)

    grad_sources = [
        [
            grad_attended[0],
            swap_cp(after(grad_attended[0], own), 1),
            grad_across,
            swap_cp(after(grad_across, own), 1),
        ]
    ]
    carried = backward(
        after(table, own),
        queries, attended_t[0], totals[0], pool, grad_sources[0], None, 0, False,
    )
    query_a = carried[1]
    across = swap_cp(after(grad_attended[1], tuple(grad_sources[0])), 2)
    grad_sources.append(
        [
            grad_attended[1],
            swap_cp(after(grad_attended[1], query_a), 1),
            across,
            swap_cp(after(across, query_a), 1),
        ]
    )
    before_b = shift_tp(onward_b, 1)
    after_a = shift_tp(back_a, -1)
    onward_a, back_b = sum_products(after(table, query_a), rows, out_proj, from_before, from_after)
    before_a = shift_tp(onward_a, 1)
    after_b = shift_tp(back_b, -1)
    query_grad, own_grads, near_grads, far_grads = backward(
        after(table, onward_a),
        queries, attended_t[1], totals[1], pool, grad_sources[1], carried, 1, True,
    )
    far_back = shift_cp(after(far_grads, (before_b, after_a)), -2)
    near_back = shift_cp(after(near_grads, (before_b, after_a)), -1)
    mixed = last_sum(own, before_a, before_b, after_a, after_b)
    key_grad, value_grad = add_terms(after(own_grads, mixed), near_back, far_back)
    return (mixed, query_grad, key_grad, value_grad)


def solution(mesh):
    placed = (P("cp", "tp"), P("cp", "tp"), P("cp", "tp"), P("tp", None), P("cp", "tp"), P(), P())
    return jax.shard_map(
        shards,
        mesh=mesh,
        in_specs=placed,
        out_specs=(P("cp", "tp"),) * 4,
        check_vma=False,
    )
```

time: 1000 us -> 128 us (0.13)
  the two profiles are of different devices: /device:TPU:9 before, /device:TPU:24 now
where the time goes in v2:
time: 128 us; the launch traced here: 127 us
  Pallas kernels  64.8 us (51%)
  starting transfers between devices  35.3 us (28%)
  waiting for transfers between devices  23 us (18%)
  local copies, waits for them, and re-layouts  2.85 us (2%)
    pallas_call x2, Pallas kernels, backward(): pl.pallas_call(kernel, in_specs=[SMEM, ANY, ANY, WHOLE] + [ANY] * (7 if f...  20.4 us
    pallas_call x2, Pallas kernels, forward(): pl.pallas_call(kernel, in_specs=[SMEM] + [ANY] * 4, out_specs=[ANY, ANY,...  20 us
    ppermute x12, starting transfers between devices, shift_tp(): lax.ppermute(block, 'tp', [(i, (i + distance) % count) for i in range(cou...  19.2 us
    ppermute x4, starting transfers between devices, shift_cp(): return lax.ppermute(block, 'cp', route)  11.6 us
    ppermute x4, waiting for transfers between devices, shift_cp(): return lax.ppermute(block, 'cp', route)  11.2 us
    pallas_call x2, Pallas kernels, grad_matmul(): pl.pallas_call(kernel, in_specs=[SMEM] + [WHOLE] * 8 + [ANY], out_specs=W...  10.4 us
    pallas_call x1, Pallas kernels, products(): pl.pallas_call(product_kernel, in_specs=[SMEM] + [ANY] * (4 * CHUNKS + 1)...  7.38 us
    ppermute x12, waiting for transfers between devices, swap_cp(): return lax.ppermute(block, 'cp', [(i, i ^ mask) for i in range(count)])  7.22 us
  transfers between devices with their start and end apart: 28, of which 6 were waited for; matrix products, arithmetic and copies ran while one was open for 0% of the time, Pallas kernels for 50%

profile of v2, /device:TPU:24, one launch (start us, length us, event | category | flops | bytes accessed | tf_op | source)
XLA Modules:
  0.0 127.4 jit_solution(16592628888085677156)
XLA Ops:
  0.6 0.0 copy-start.1
  0.7 1.0 copy-done.2
  1.7 0.9 copy-done.3
  2.6 0.8 join.1
  3.4 0.1 halve.1
  3.5 2.8 %collective-permute-start = (bf16[256,1024]{1,0:T(8,128)(2,1)S(1)}, bf16[256,1024]{1,0:T(8,128)(2,1)S(1)}, u32[]{:S(2)}, u32[]{:S(2)}) collective-permute-start(bf16[256,1024]{1,0:T(8,128)(2,1)S(1)} %get-tuple-element.54.refs_1_), channel_id=1, source_target_pairs={{0,3},{1,0},{2,1},{3,2},{4,7},{5,4},{6,5},{7,6},{8,11},{9,8},{10,9... | collective-permute-start | bytes 1572872 | tf_op jit(solution)/shard_map/ppermute | solution.py:68
  6.4 1.9 %collective-permute-start.4 = (bf16[512,256]{1,0:T(8,128)(2,1)S(1)}, bf16[512,256]{1,0:T(8,128)(2,1)}, u32[]{:S(2)}, u32[]{:S(2)}) collective-permute-start(bf16[512,256]{1,0:T(8,128)(2,1)S(1)} %get-tuple-element.52.refs_2_.refs_4_), channel_id=1, source_target_pairs={{0,4},{4,8},{8,12},{12,16},{16,20},{20,24},{24,28},{28,32},{32,36}... | collective-permute-start | bytes 786440 | tf_op jit(solution)/shard_map/ppermute | solution.py:63
  8.3 3.3 %collective-permute-start.1 = (bf16[256,1024]{1,0:T(8,128)(2,1)S(1)}, bf16[256,1024]{1,0:T(8,128)(2,1)}, u32[]{:S(2)}, u32[]{:S(2)}) collective-permute-start(bf16[256,1024]{1,0:T(8,128)(2,1)S(1)} %get-tuple-element.55.refs_2_), channel_id=1, source_target_pairs={{0,3},{1,0},{2,1},{3,2},{4,7},{5,4},{6,5},{7,6},{8,11},{9,8},{10,9... | collective-permute-start | bytes 1572872 | tf_op jit(solution)/shard_map/ppermute | solution.py:68
  11.6 3.8 %collective-permute-start.3 = (bf16[384,256]{1,0:T(8,128)(2,1)}, bf16[384,256]{1,0:T(8,128)(2,1)}, u32[]{:S(2)}, u32[]{:S(2)}) collective-permute-start(bf16[384,256]{1,0:T(8,128)(2,1)} %get-tuple-element.56), channel_id=1, source_target_pairs={{0,8},{4,12},{8,16},{12,20},{16,24},{20,28},{24,32},{28,36},{32,40... | collective-permute-start | bytes 589832 | tf_op jit(solution)/shard_map/ppermute | solution.py:63
  15.5 0.1 dynamic-slice_subtract_fusion
  15.5 0.1 select_reduce_fusion
  15.7 0.1 and_select_fusion
  15.8 0.1 and_select_fusion.2
  15.8 0.1 dynamic-slice_subtract_fusion.1
  15.9 0.1 fusion
  16.0 0.1 concatenate.3.refs_0_.table
  16.1 8.4 %collective-permute-done.3.refs_3_.refs_5_ = bf16[384,256]{1,0:T(8,128)(2,1)} collective-permute-done((bf16[384,256]{1,0:T(8,128)(2,1)}, bf16[384,256]{1,0:T(8,128)(2,1)}, u32[]{:S(2)}, u32[]{:S(2)}) %collective-permute-start.3) | collective-permute-done | bytes 196640 | tf_op jit(solution)/shard_map/ppermute | solution.py:63
  24.5 0.0 collective-permute-done.4.refs_4_.refs_6_
  24.5 10.0 %attention_forward.2 = (bf16[512,512]{1,0:T(8,128)(2,1)S(1)}, bf16[4,128,512]{2,1,0:T(8,128)(2,1)S(1)}, f32[4,1,512]{2,1,0:T(1,128)S(1)}) custom-call(s32[22]{0:T(128)S(1)} %concatenate.3.refs_0_.table, bf16[512,1024]{1,0:T(8,128)(2,1)S(1)} %copy-done.1, bf16[512,256]{1,0:T(8,128)(2,1)S(1)} %get-tuple-element.52.refs_2_.refs_4_, ...), custom_call_target="tpu_custom_call" | custom-call | flops 9200000000 | bytes 28800000 | tf_op jit(solution)/shard_map/attention_forward/pallas_call | solution.py:189
  34.5 0.1 collective-permute-start.9
  34.6 0.0 collective-permute-done.2.refs_7_
  34.6 3.9 %collective-permute-done.5.refs_8_ = bf16[256,1024]{1,0:T(8,128)(2,1)S(1)} collective-permute-done((bf16[256,1024]{1,0:T(8,128)(2,1)S(1)}, bf16[256,1024]{1,0:T(8,128)(2,1)S(1)}, u32[]{:S(2)}, u32[]{:S(2)}) %collective-permute-start.5) | collective-permute-done | bytes 524320 | tf_op jit(solution)/shard_map/ppermute | solution.py:68
  38.5 0.0 collective-permute-start.6
  38.5 3.2 %collective-permute-start.7 = (bf16[256,1024]{1,0:T(8,128)(2,1)}, bf16[256,1024]{1,0:T(8,128)(2,1)S(1)}, u32[]{:S(2)}, u32[]{:S(2)}) collective-permute-start(bf16[256,1024]{1,0:T(8,128)(2,1)} %collective-permute-done.1.refs_4_), channel_id=1, source_target_pairs={{0,3},{1,0},{2,1},{3,2},{4,7},{5,4},{6,5},{7,6},{8,11},{9,8},{10,9... | collective-permute-start | bytes 1572872 | tf_op jit(solution)/shard_map/ppermute | solution.py:68
  41.7 10.0 %attention_forward.3 = (bf16[512,512]{1,0:T(8,128)(2,1)S(1)}, bf16[4,128,512]{2,1,0:T(8,128)(2,1)S(1)}, f32[4,1,512]{2,1,0:T(1,128)S(1)}) custom-call(s32[22]{0:T(128)S(1)} %concatenate.3.refs_0_.table, bf16[512,1024]{1,0:T(8,128)(2,1)S(1)} %copy-done.1, bf16[512,256]{1,0:T(8,128)(2,1)S(1)} %get-tuple-element.52.refs_2_.refs_4_, ...), custom_call_target="tpu_custom_call" | custom-call | flops 9200000000 | bytes 28800000 | tf_op jit(solution)/shard_map/attention_forward/pallas_call | solution.py:189
  51.7 0.1 collective-permute-start.12
  51.8 0.1 collective-permute-start.8
  51.9 0.5 collective-permute-start.10
  52.4 0.0 collective-permute-done.6.refs_5_
  52.4 0.0 collective-permute-done.7.refs_6_
  52.4 5.2 %grad_projection.2.refs_7_ = bf16[512,512]{1,0:T(8,128)(2,1)S(1)} custom-call(s32[22]{0:T(128)S(1)} %concatenate.3.refs_0_.table, bf16[256,1024]{1,0:T(8,128)(2,1)S(1)} %get-tuple-element.54.refs_1_, bf16[256,1024]{1,0:T(8,128)(2,1)S(1)} %get-tuple-element.55.refs_2_, bf16[256,1024]{1,0:T(8,128)(2,1)S(1)} %collective-permute-done.refs_3_, ...), custom_call_target="tpu_custom_call" | custom-call | flops 4600000000 | bytes 14400000 | tf_op jit(solution)/shard_map/grad_projection/pallas_call | solution.py:403
  57.6 0.2 collective-permute-start.11
  57.8 3.6 %collective-permute-done.12.refs_6_ = bf16[512,512]{1,0:T(8,128)(2,1)S(1)} collective-permute-done((bf16[512,512]{1,0:T(8,128)(2,1)S(1)}, bf16[512,512]{1,0:T(8,128)(2,1)S(1)}, u32[]{:S(2)}, u32[]{:S(2)}) %collective-permute-start.12) | collective-permute-done | bytes 524320 | tf_op jit(solution)/shard_map/ppermute | solution.py:57
  61.4 0.0 collective-permute-start.13
  61.4 1.7 %collective-permute-start.15 = (bf16[512,512]{1,0:T(8,128)(2,1)S(1)}, bf16[512,512]{1,0:T(8,128)(2,1)S(1)}, u32[]{:S(2)}, u32[]{:S(2)}) collective-permute-start(bf16[512,512]{1,0:T(8,128)(2,1)S(1)} %grad_projection.2.refs_7_), channel_id=1, source_target_pairs={{0,8},{4,12},{8,0},{12,4},{16,24},{20,28},{24,16},{28,20},{32,40},... | collective-permute-start | bytes 1572872 | tf_op jit(solution)/shard_map/ppermute | solution.py:57
  63.2 5.2 %grad_projection.3.refs_7_ = bf16[512,512]{1,0:T(8,128)(2,1)S(1)} custom-call(s32[22]{0:T(128)S(1)} %concatenate.3.refs_0_.table, bf16[256,1024]{1,0:T(8,128)(2,1)S(1)} %get-tuple-element.54.refs_1_, bf16[256,1024]{1,0:T(8,128)(2,1)S(1)} %get-tuple-element.55.refs_2_, bf16[256,1024]{1,0:T(8,128)(2,1)S(1)} %collective-permute-done.refs_3_, ...), custom_call_target="tpu_custom_call" | custom-call | flops 4600000000 | bytes 14400000 | tf_op jit(solution)/shard_map/grad_projection/pallas_call | solution.py:403
  68.4 0.0 collective-permute-done.10.refs_3_
  68.4 0.0 collective-permute-done.11.refs_5_
  68.4 0.0 copy-start.8
  68.4 0.8 copy-done.8
  69.2 7.4 %products.1 = (bf16[512,512]{1,0:T(8,128)(2,1)S(1)}, bf16[512,512]{1,0:T(8,128)(2,1)S(1)}, bf16[512,512]{1,0:T(8,128)(2,1)S(1)}, bf16[512,512]{1,0:T(8,128)(2,1)...) custom-call(s32[22]{0:T(128)S(1)} %concatenate.3.refs_0_.table, ...), custom_call_target="tpu_custom_call" | custom-call | flops 8049999872 | bytes 25200000 | tf_op jit(solution)/shard_map/products/pallas_call | solution.py:459
  76.6 1.6 %collective-permute-start.14 = (bf16[512,512]{1,0:T(8,128)(2,1)S(1)}, bf16[512,512]{1,0:T(8,128)(2,1)S(1)}, u32[]{:S(2)}, u32[]{:S(2)}) collective-permute-start(bf16[512,512]{1,0:T(8,128)(2,1)S(1)} %grad_projection.2.refs_7_), channel_id=1, source_target_pairs={{0,4},{4,0},{8,12},{12,8},{16,20},{20,16},{24,28},{28,24},{32,36},... | collective-permute-start | bytes 1572872 | tf_op jit(solution)/shard_map/ppermute | solution.py:57
  78.2 0.1 collective-permute-start.16
  78.3 0.0 collective-permute-start.17
  78.3 3.2 %collective-permute-start.18 = (bf16[512,512]{1,0:T(8,128)(2,1)S(1)}, bf16[512,512]{1,0:T(8,128)(2,1)S(1)}, u32[]{:S(2)}, u32[]{:S(2)}) collective-permute-start(bf16[512,512]{1,0:T(8,128)(2,1)S(1)} %get-tuple-element.78), channel_id=1, source_target_pairs={{0,3},{1,0},{2,1},{3,2},{4,7},{5,4},{6,5},{7,6},{8,11},{9,8},{10,9... | collective-permute-start | bytes 1572872 | tf_op jit(solution)/shard_map/ppermute | solution.py:68
  81.6 0.0 collective-permute-start.24
  81.6 10.0 %attention_backward.2 = (bf16[512,1024]{1,0:T(8,128)(2,1)}, f32[1408,128]{1,0:T(8,128)S(1)}, f32[1408,128]{1,0:T(8,128)S(1)}) custom-call(s32[22]{0:T(128)S(1)} %concatenate.3.refs_0_.table, bf16[512,1024]{1,0:T(8,128)(2,1)S(1)} %copy-done.1, bf16[4,128,512]{2,1,0:T(8,128)(2,1)S(1)} %get-tuple-element.70.refs_2_, ...), custom_call_target="tpu_custom_call" | custom-call | flops 10350000128 | bytes 32400000 | tf_op jit(solution)/shard_map/attention_backward/pallas_call | solution.py:351
  91.6 0.1 collective-permute-start.23
  91.7 3.6 %collective-permute-done.24.refs_9_ = bf16[512,512]{1,0:T(8,128)(2,1)S(1)} collective-permute-done((bf16[512,512]{1,0:T(8,128)(2,1)S(1)}, bf16[512,512]{1,0:T(8,128)(2,1)S(1)}, u32[]{:S(2)}, u32[]{:S(2)}) %collective-permute-start.24) | collective-permute-done | bytes 524320 | tf_op jit(solution)/shard_map/ppermute | solution.py:57
  95.3 0.0 collective-permute-start.25
  95.3 0.0 collective-permute-start.20
  95.3 0.0 collective-permute-done.17.before
  95.3 3.2 %collective-permute-start.21 = (bf16[512,512]{1,0:T(8,128)(2,1)S(1)}, bf16[512,512]{1,0:T(8,128)(2,1)S(1)}, u32[]{:S(2)}, u32[]{:S(2)}) collective-permute-start(bf16[512,512]{1,0:T(8,128)(2,1)S(1)} %get-tuple-element.81), channel_id=1, source_target_pairs={{0,3},{1,0},{2,1},{3,2},{4,7},{5,4},{6,5},{7,6},{8,11},{9,8},{10,9... | collective-permute-start | bytes 1572872 | tf_op jit(solution)/shard_map/ppermute | solution.py:68
  98.5 3.2 %sum_products.1 = (bf16[512,512]{1,0:T(8,128)(2,1)S(1)}, bf16[512,512]{1,0:T(8,128)(2,1)S(1)}) custom-call(s32[22]{0:T(128)S(1)} %concatenate.3.refs_0_.table, bf16[512,1024]{1,0:T(8,128)(2,1)S(1)} %copy-done.5, bf16[1024,4096]{1,0:T(8,128)(2,1)} %weight_hbm.1, bf16[512,512]{1,0:T(8,128)(2,1)S(1)} %collective-permute-done.17.before, ...), custom_call_target="tpu_custom_call" | custom-call | flops 4600000000 | bytes 14400000 | tf_op jit(solution)/shard_map/sum_products/pallas_call | solution.py:491
  101.8 0.1 collective-permute-start.19
  101.9 0.0 collective-permute-done.23.refs_8_
  101.9 3.2 %collective-permute-start.22 = (bf16[512,512]{1,0:T(8,128)(2,1)S(1)}, bf16[512,512]{1,0:T(8,128)(2,1)S(1)}, u32[]{:S(2)}, u32[]{:S(2)}) collective-permute-start(bf16[512,512]{1,0:T(8,128)(2,1)S(1)} %get-tuple-element.82), channel_id=1, source_target_pairs={{0,3},{1,0},{2,1},{3,2},{4,7},{5,4},{6,5},{7,6},{8,11},{9,8},{10,9... | collective-permute-start | bytes 1572872 | tf_op jit(solution)/shard_map/ppermute | solution.py:68
  105.1 10.4 %attention_backward.3 = (bf16[512,1024]{1,0:T(8,128)(2,1)}, f32[512,256]{1,0:T(8,128)S(1)}, bf16[512,256]{1,0:T(8,128)(2,1)S(1)}, bf16[384,256]{1,0:T(8,128)(2,1)S(1)}) custom-call(s32[22]{0:T(128)S(1)} %concatenate.3.refs_0_.table, bf16[512,1024]{1,0:T(8,128)(2,1)} %refs_1_.7, ...), custom_call_target="tpu_custom_call", output_to_operand_aliasing={{0}: (11, {})} | custom-call | flops 10350000128 | bytes 32400000 | tf_op jit(solution)/shard_map/attention_backward/pallas_call | solution.py:351
  115.5 1.9 %collective-permute-start.26 = (bf16[512,256]{1,0:T(8,128)(2,1)S(1)}, bf16[512,256]{1,0:T(8,128)(2,1)S(1)}, u32[]{:S(2)}, u32[]{:S(2)}) collective-permute-start(bf16[512,256]{1,0:T(8,128)(2,1)S(1)} %get-tuple-element.95), channel_id=1, source_target_pairs={{4,0},{8,4},{12,8},{16,12},{20,16},{24,20},{28,24},{32,28},{36,32}... | collective-permute-start | bytes 786440 | tf_op jit(solution)/shard_map/ppermute | solution.py:63
  117.4 4.0 %collective-permute-start.27 = (bf16[384,256]{1,0:T(8,128)(2,1)S(1)}, bf16[384,256]{1,0:T(8,128)(2,1)S(1)}, u32[]{:S(2)}, u32[]{:S(2)}) collective-permute-start(bf16[384,256]{1,0:T(8,128)(2,1)S(1)} %get-tuple-element.97), channel_id=1, source_target_pairs={{8,0},{12,4},{16,8},{20,12},{24,16},{28,20},{32,24},{36,28},{40,32... | collective-permute-start | bytes 589832 | tf_op jit(solution)/shard_map/ppermute | solution.py:63
  121.4 0.6 collective-permute-done.19.before_a
  122.1 1.7 %last_sum.1 = bf16[512,1024]{1,0:T(8,128)(2,1)} custom-call(bf16[512,1024]{1,0:T(8,128)(2,1)S(1)} %copy-done.4, bf16[512,512]{1,0:T(8,128)(2,1)S(1)} %collective-permute-done.19.before_a, bf16[512,512]{1,0:T(8,128)(2,1)S(1)} %collective-permute-done.20.before_b, bf16[512,512]{1,0:T(8,128)(2,1)S(1)} %collective-permute-done.21.after_a, ...), custom_call_target="tpu_custom_call" | custom-call | flops 2300000000 | bytes 7200000 | tf_op jit(solution)/shard_map/last_sum/pallas_call | solution.py:517
  123.8 2.9 %collective-permute-done.27.far = bf16[384,256]{1,0:T(8,128)(2,1)S(1)} collective-permute-done((bf16[384,256]{1,0:T(8,128)(2,1)S(1)}, bf16[384,256]{1,0:T(8,128)(2,1)S(1)}, u32[]{:S(2)}, u32[]{:S(2)}) %collective-permute-start.27) | collective-permute-done | bytes 196640 | tf_op jit(solution)/shard_map/ppermute | solution.py:63
  126.7 0.8 add_terms.1
  (29 shorter events, 0.1 us)
Async XLA Ops:
  0.6 2.8 %copy-start = (bf16[512,1024]{1,0:T(8,128)(2,1)S(1)}, bf16[512,1024]{1,0:T(8,128)(2,1)}, u32[]{:S(2)}) copy-start(bf16[512,1024]{1,0:T(8,128)(2,1)} %grads) | copy-start | bytes 3145732
  0.6 23.8 %copy-start.1 = (bf16[512,1024]{1,0:T(8,128)(2,1)S(1)}, bf16[512,1024]{1,0:T(8,128)(2,1)}, u32[]{:S(2)}) copy-start(bf16[512,1024]{1,0:T(8,128)(2,1)} %refs_1_.7) | copy-start | bytes 3145732
  0.7 1.1 copy-start.2
  1.7 0.9 copy-start.3
  2.6 12.9 %copy-start.6 = (s32[256]{0:T(256)S(1)}, s32[256]{0:T(256)}, u32[]{:S(2)}) copy-start(s32[256]{0:T(256)} %param.13) | copy-start | bytes 3076
  2.6 13.2 %copy-start.7 = (s32[256]{0:T(256)S(1)}, s32[256]{0:T(256)}, u32[]{:S(2)}) copy-start(s32[256]{0:T(256)} %param.12) | copy-start | bytes 3076
  3.5 31.0 %collective-permute-start = (bf16[256,1024]{1,0:T(8,128)(2,1)S(1)}, bf16[256,1024]{1,0:T(8,128)(2,1)S(1)}, u32[]{:S(2)}, u32[]{:S(2)}) collective-permute-start(bf16[256,1024]{1,0:T(8,128)(2,1)S(1)} %get-tuple-element.54.refs_1_), channel_id=1, source_target_pairs={{0,3},{1,0},{2,1},{3,2},{4,7},{5,4},{6,5},{7,6},{8,11},{9,8},{10,9... | collective-permute-start | bytes 1572872 | tf_op jit(solution)/shard_map/ppermute | solution.py:68
  6.4 28.2 %collective-permute-start.2 = (bf16[256,1024]{1,0:T(8,128)(2,1)S(1)}, bf16[256,1024]{1,0:T(8,128)(2,1)S(1)}, u32[]{:S(2)}, u32[]{:S(2)}) collective-permute-start(bf16[256,1024]{1,0:T(8,128)(2,1)S(1)} %get-tuple-element.54.refs_1_), channel_id=1, source_target_pairs={{0,1},{1,2},{2,3},{3,0},{4,5},{5,6},{6,7},{7,4},{8,9},{9,10},{10,1... | collective-permute-start | bytes 1572872 | tf_op jit(solution)/shard_map/ppermute | solution.py:68
  6.4 18.1 %collective-permute-start.4 = (bf16[512,256]{1,0:T(8,128)(2,1)S(1)}, bf16[512,256]{1,0:T(8,128)(2,1)}, u32[]{:S(2)}, u32[]{:S(2)}) collective-permute-start(bf16[512,256]{1,0:T(8,128)(2,1)S(1)} %get-tuple-element.52.refs_2_.refs_4_), channel_id=1, source_target_pairs={{0,4},{4,8},{8,12},{12,16},{16,20},{20,24},{24,28},{28,32},{32,36}... | collective-permute-start | bytes 786440 | tf_op jit(solution)/shard_map/ppermute | solution.py:63
  8.3 30.2 %collective-permute-start.1 = (bf16[256,1024]{1,0:T(8,128)(2,1)S(1)}, bf16[256,1024]{1,0:T(8,128)(2,1)}, u32[]{:S(2)}, u32[]{:S(2)}) collective-permute-start(bf16[256,1024]{1,0:T(8,128)(2,1)S(1)} %get-tuple-element.55.refs_2_), channel_id=1, source_target_pairs={{0,3},{1,0},{2,1},{3,2},{4,7},{5,4},{6,5},{7,6},{8,11},{9,8},{10,9... | collective-permute-start | bytes 1572872 | tf_op jit(solution)/shard_map/ppermute | solution.py:68
  11.6 12.9 %collective-permute-start.3 = (bf16[384,256]{1,0:T(8,128)(2,1)}, bf16[384,256]{1,0:T(8,128)(2,1)}, u32[]{:S(2)}, u32[]{:S(2)}) collective-permute-start(bf16[384,256]{1,0:T(8,128)(2,1)} %get-tuple-element.56), channel_id=1, source_target_pairs={{0,8},{4,12},{8,16},{12,20},{16,24},{20,28},{24,32},{28,36},{32,40... | collective-permute-start | bytes 589832 | tf_op jit(solution)/shard_map/ppermute | solution.py:63
  24.5 14.0 %collective-permute-start.5 = (bf16[256,1024]{1,0:T(8,128)(2,1)S(1)}, bf16[256,1024]{1,0:T(8,128)(2,1)S(1)}, u32[]{:S(2)}, u32[]{:S(2)}) collective-permute-start(bf16[256,1024]{1,0:T(8,128)(2,1)S(1)} %get-tuple-element.55.refs_2_), channel_id=1, source_target_pairs={{0,1},{1,2},{2,3},{3,0},{4,5},{5,6},{6,7},{7,4},{8,9},{9,10},{10,1... | collective-permute-start | bytes 1572872 | tf_op jit(solution)/shard_map/ppermute | solution.py:68
  34.5 17.4 %collective-permute-start.9 = (bf16[512,512]{1,0:T(8,128)(2,1)S(1)}, bf16[512,512]{1,0:T(8,128)(2,1)S(1)}, u32[]{:S(2)}, u32[]{:S(2)}) collective-permute-start(bf16[512,512]{1,0:T(8,128)(2,1)S(1)} %get-tuple-element.64.refs_0_), channel_id=1, source_target_pairs={{0,8},{4,12},{8,0},{12,4},{16,24},{20,28},{24,16},{28,20},{32,40},... | collective-permute-start | bytes 1572872 | tf_op jit(solution)/shard_map/ppermute | solution.py:57
  38.5 13.9 %collective-permute-start.6 = (bf16[256,1024]{1,0:T(8,128)(2,1)S(1)}, bf16[256,1024]{1,0:T(8,128)(2,1)S(1)}, u32[]{:S(2)}, u32[]{:S(2)}) collective-permute-start(bf16[256,1024]{1,0:T(8,128)(2,1)S(1)} %collective-permute-done.2.refs_7_), channel_id=1, source_target_pairs={{0,1},{1,2},{2,3},{3,0},{4,5},{5,6},{6,7},{7,4},{8,9},{9,10},{10,1... | collective-permute-start | bytes 1572872 | tf_op jit(solution)/shard_map/ppermute | solution.py:68
  38.5 13.9 %collective-permute-start.7 = (bf16[256,1024]{1,0:T(8,128)(2,1)}, bf16[256,1024]{1,0:T(8,128)(2,1)S(1)}, u32[]{:S(2)}, u32[]{:S(2)}) collective-permute-start(bf16[256,1024]{1,0:T(8,128)(2,1)} %collective-permute-done.1.refs_4_), channel_id=1, source_target_pairs={{0,3},{1,0},{2,1},{3,2},{4,7},{5,4},{6,5},{7,6},{8,11},{9,8},{10,9... | collective-permute-start | bytes 1572872 | tf_op jit(solution)/shard_map/ppermute | solution.py:68
  51.7 9.7 %collective-permute-start.12 = (bf16[512,512]{1,0:T(8,128)(2,1)S(1)}, bf16[512,512]{1,0:T(8,128)(2,1)S(1)}, u32[]{:S(2)}, u32[]{:S(2)}) collective-permute-start(bf16[512,512]{1,0:T(8,128)(2,1)S(1)} %get-tuple-element.66.refs_4_), channel_id=1, source_target_pairs={{0,8},{4,12},{8,0},{12,4},{16,24},{20,28},{24,16},{28,20},{32,40},... | collective-permute-start | bytes 1572872 | tf_op jit(solution)/shard_map/ppermute | solution.py:57
  51.8 16.6 %collective-permute-start.8 = (bf16[512,512]{1,0:T(8,128)(2,1)S(1)}, bf16[512,512]{1,0:T(8,128)(2,1)S(1)}, u32[]{:S(2)}, u32[]{:S(2)}) collective-permute-start(bf16[512,512]{1,0:T(8,128)(2,1)S(1)} %get-tuple-element.64.refs_0_), channel_id=1, source_target_pairs={{0,4},{4,0},{8,12},{12,8},{16,20},{20,16},{24,28},{28,24},{32,36},... | collective-permute-start | bytes 1572872 | tf_op jit(solution)/shard_map/ppermute | solution.py:57
  51.9 16.5 %collective-permute-start.10 = (bf16[512,512]{1,0:T(8,128)(2,1)S(1)}, bf16[512,512]{1,0:T(8,128)(2,1)S(1)}, u32[]{:S(2)}, u32[]{:S(2)}) collective-permute-start(bf16[512,512]{1,0:T(8,128)(2,1)S(1)} %collective-permute-done.9.refs_2_), channel_id=1, source_target_pairs={{0,4},{4,0},{8,12},{12,8},{16,20},{20,16},{24,28},{28,24},{32,36},... | collective-permute-start | bytes 1572872 | tf_op jit(solution)/shard_map/ppermute | solution.py:57
  57.6 10.8 %collective-permute-start.11 = (bf16[512,512]{1,0:T(8,128)(2,1)S(1)}, bf16[512,512]{1,0:T(8,128)(2,1)S(1)}, u32[]{:S(2)}, u32[]{:S(2)}) collective-permute-start(bf16[512,512]{1,0:T(8,128)(2,1)S(1)} %get-tuple-element.66.refs_4_), channel_id=1, source_target_pairs={{0,4},{4,0},{8,12},{12,8},{16,20},{20,16},{24,28},{28,24},{32,36},... | collective-permute-start | bytes 1572872 | tf_op jit(solution)/shard_map/ppermute | solution.py:57
  61.4 7.0 %collective-permute-start.13 = (bf16[512,512]{1,0:T(8,128)(2,1)S(1)}, bf16[512,512]{1,0:T(8,128)(2,1)S(1)}, u32[]{:S(2)}, u32[]{:S(2)}) collective-permute-start(bf16[512,512]{1,0:T(8,128)(2,1)S(1)} %collective-permute-done.12.refs_6_), channel_id=1, source_target_pairs={{0,4},{4,0},{8,12},{12,8},{16,20},{20,16},{24,28},{28,24},{32,36},... | collective-permute-start | bytes 1572872 | tf_op jit(solution)/shard_map/ppermute | solution.py:57
  61.4 16.8 %collective-permute-start.15 = (bf16[512,512]{1,0:T(8,128)(2,1)S(1)}, bf16[512,512]{1,0:T(8,128)(2,1)S(1)}, u32[]{:S(2)}, u32[]{:S(2)}) collective-permute-start(bf16[512,512]{1,0:T(8,128)(2,1)S(1)} %grad_projection.2.refs_7_), channel_id=1, source_target_pairs={{0,8},{4,12},{8,0},{12,4},{16,24},{20,28},{24,16},{28,20},{32,40},... | collective-permute-start | bytes 1572872 | tf_op jit(solution)/shard_map/ppermute | solution.py:57
  68.4 0.8 copy-start.8
  76.6 5.0 %collective-permute-start.14 = (bf16[512,512]{1,0:T(8,128)(2,1)S(1)}, bf16[512,512]{1,0:T(8,128)(2,1)S(1)}, u32[]{:S(2)}, u32[]{:S(2)}) collective-permute-start(bf16[512,512]{1,0:T(8,128)(2,1)S(1)} %grad_projection.2.refs_7_), channel_id=1, source_target_pairs={{0,4},{4,0},{8,12},{12,8},{16,20},{20,16},{24,28},{28,24},{32,36},... | collective-permute-start | bytes 1572872 | tf_op jit(solution)/shard_map/ppermute | solution.py:57
  78.2 3.4 %collective-permute-start.16 = (bf16[512,512]{1,0:T(8,128)(2,1)S(1)}, bf16[512,512]{1,0:T(8,128)(2,1)S(1)}, u32[]{:S(2)}, u32[]{:S(2)}) collective-permute-start(bf16[512,512]{1,0:T(8,128)(2,1)S(1)} %collective-permute-done.15.refs_9_), channel_id=1, source_target_pairs={{0,4},{4,0},{8,12},{12,8},{16,20},{20,16},{24,28},{28,24},{32,36},... | collective-permute-start | bytes 1572872 | tf_op jit(solution)/shard_map/ppermute | solution.py:57
  78.3 17.0 %collective-permute-start.17 = (bf16[512,512]{1,0:T(8,128)(2,1)S(1)}, bf16[512,512]{1,0:T(8,128)(2,1)S(1)}, u32[]{:S(2)}, u32[]{:S(2)}) collective-permute-start(bf16[512,512]{1,0:T(8,128)(2,1)S(1)} %get-tuple-element.77), channel_id=1, source_target_pairs={{0,1},{1,2},{2,3},{3,0},{4,5},{5,6},{6,7},{7,4},{8,9},{9,10},{10,1... | collective-permute-start | bytes 1572872 | tf_op jit(solution)/shard_map/ppermute | solution.py:68
  78.3 20.2 %collective-permute-start.18 = (bf16[512,512]{1,0:T(8,128)(2,1)S(1)}, bf16[512,512]{1,0:T(8,128)(2,1)S(1)}, u32[]{:S(2)}, u32[]{:S(2)}) collective-permute-start(bf16[512,512]{1,0:T(8,128)(2,1)S(1)} %get-tuple-element.78), channel_id=1, source_target_pairs={{0,3},{1,0},{2,1},{3,2},{4,7},{5,4},{6,5},{7,6},{8,11},{9,8},{10,9... | collective-permute-start | bytes 1572872 | tf_op jit(solution)/shard_map/ppermute | solution.py:68
  81.6 13.7 %collective-permute-start.24 = (bf16[512,512]{1,0:T(8,128)(2,1)S(1)}, bf16[512,512]{1,0:T(8,128)(2,1)S(1)}, u32[]{:S(2)}, u32[]{:S(2)}) collective-permute-start(bf16[512,512]{1,0:T(8,128)(2,1)S(1)} %grad_projection.3.refs_7_), channel_id=1, source_target_pairs={{0,8},{4,12},{8,0},{12,4},{16,24},{20,28},{24,16},{28,20},{32,40},... | collective-permute-start | bytes 1572872 | tf_op jit(solution)/shard_map/ppermute | solution.py:57
  81.6 16.9 %copy-start.5 = (bf16[512,1024]{1,0:T(8,128)(2,1)S(1)}, bf16[512,1024]{1,0:T(8,128)(2,1)}, u32[]{:S(2)}) copy-start(bf16[512,1024]{1,0:T(8,128)(2,1)} %get-tuple-element.76.rows) | copy-start | bytes 3145732
  91.6 10.2 %collective-permute-start.23 = (bf16[512,512]{1,0:T(8,128)(2,1)S(1)}, bf16[512,512]{1,0:T(8,128)(2,1)S(1)}, u32[]{:S(2)}, u32[]{:S(2)}) collective-permute-start(bf16[512,512]{1,0:T(8,128)(2,1)S(1)} %grad_projection.3.refs_7_), channel_id=1, source_target_pairs={{0,4},{4,0},{8,12},{12,8},{16,20},{20,16},{24,28},{28,24},{32,36},... | collective-permute-start | bytes 1572872 | tf_op jit(solution)/shard_map/ppermute | solution.py:57
  95.3 9.8 %collective-permute-start.25 = (bf16[512,512]{1,0:T(8,128)(2,1)S(1)}, bf16[512,512]{1,0:T(8,128)(2,1)S(1)}, u32[]{:S(2)}, u32[]{:S(2)}) collective-permute-start(bf16[512,512]{1,0:T(8,128)(2,1)S(1)} %collective-permute-done.24.refs_9_), channel_id=1, source_target_pairs={{0,4},{4,0},{8,12},{12,8},{16,20},{20,16},{24,28},{28,24},{32,36},... | collective-permute-start | bytes 1572872 | tf_op jit(solution)/shard_map/ppermute | solution.py:57
  95.3 20.2 %collective-permute-start.20 = (bf16[512,512]{1,0:T(8,128)(2,1)S(1)}, bf16[512,512]{1,0:T(8,128)(2,1)S(1)}, u32[]{:S(2)}, u32[]{:S(2)}) collective-permute-start(bf16[512,512]{1,0:T(8,128)(2,1)S(1)} %get-tuple-element.80), channel_id=1, source_target_pairs={{0,1},{1,2},{2,3},{3,0},{4,5},{5,6},{6,7},{7,4},{8,9},{9,10},{10,1... | collective-permute-start | bytes 1572872 | tf_op jit(solution)/shard_map/ppermute | solution.py:68
  95.3 20.2 %collective-permute-start.21 = (bf16[512,512]{1,0:T(8,128)(2,1)S(1)}, bf16[512,512]{1,0:T(8,128)(2,1)S(1)}, u32[]{:S(2)}, u32[]{:S(2)}) collective-permute-start(bf16[512,512]{1,0:T(8,128)(2,1)S(1)} %get-tuple-element.81), channel_id=1, source_target_pairs={{0,3},{1,0},{2,1},{3,2},{4,7},{5,4},{6,5},{7,6},{8,11},{9,8},{10,9... | collective-permute-start | bytes 1572872 | tf_op jit(solution)/shard_map/ppermute | solution.py:68
  101.8 20.3 %collective-permute-start.19 = (bf16[512,512]{1,0:T(8,128)(2,1)S(1)}, bf16[512,512]{1,0:T(8,128)(2,1)S(1)}, u32[]{:S(2)}, u32[]{:S(2)}) collective-permute-start(bf16[512,512]{1,0:T(8,128)(2,1)S(1)} %get-tuple-element.79), channel_id=1, source_target_pairs={{0,1},{1,2},{2,3},{3,0},{4,5},{5,6},{6,7},{7,4},{8,9},{9,10},{10,1... | collective-permute-start | bytes 1572872 | tf_op jit(solution)/shard_map/ppermute | solution.py:68
  101.9 20.2 %collective-permute-start.22 = (bf16[512,512]{1,0:T(8,128)(2,1)S(1)}, bf16[512,512]{1,0:T(8,128)(2,1)S(1)}, u32[]{:S(2)}, u32[]{:S(2)}) collective-permute-start(bf16[512,512]{1,0:T(8,128)(2,1)S(1)} %get-tuple-element.82), channel_id=1, source_target_pairs={{0,3},{1,0},{2,1},{3,2},{4,7},{5,4},{6,5},{7,6},{8,11},{9,8},{10,9... | collective-permute-start | bytes 1572872 | tf_op jit(solution)/shard_map/ppermute | solution.py:68
  105.1 17.0 %copy-start.4 = (bf16[512,1024]{1,0:T(8,128)(2,1)S(1)}, bf16[512,1024]{1,0:T(8,128)(2,1)}, u32[]{:S(2)}) copy-start(bf16[512,1024]{1,0:T(8,128)(2,1)} %get-tuple-element.68.own) | copy-start | bytes 3145732
  115.5 11.1 %collective-permute-start.26 = (bf16[512,256]{1,0:T(8,128)(2,1)S(1)}, bf16[512,256]{1,0:T(8,128)(2,1)S(1)}, u32[]{:S(2)}, u32[]{:S(2)}) collective-permute-start(bf16[512,256]{1,0:T(8,128)(2,1)S(1)} %get-tuple-element.95), channel_id=1, source_target_pairs={{4,0},{8,4},{12,8},{16,12},{20,16},{24,20},{28,24},{32,28},{36,32}... | collective-permute-start | bytes 786440 | tf_op jit(solution)/shard_map/ppermute | solution.py:63
  117.4 9.2 %collective-permute-start.27 = (bf16[384,256]{1,0:T(8,128)(2,1)S(1)}, bf16[384,256]{1,0:T(8,128)(2,1)S(1)}, u32[]{:S(2)}, u32[]{:S(2)}) collective-permute-start(bf16[384,256]{1,0:T(8,128)(2,1)S(1)} %get-tuple-element.97), channel_id=1, source_target_pairs={{8,0},{12,4},{16,8},{20,12},{24,16},{28,20},{32,24},{36,28},{40,32... | collective-permute-start | bytes 589832 | tf_op jit(solution)/shard_map/ppermute | solution.py:63

commit v3 on v2

--- a/solution.py
+++ b/solution.py
@@ -118,27 +118,22 @@
 
 
 def forward_kernel(
-    chunk, table, q_hbm, kv, far, near, att_hbm, att_t_hbm, total_ref,
-    keys, values, q_ref, att, att_t, sems, out_sems,
+    chunk, table, q_ref, kv, far, near, att, att_t, total_ref, keys, values, sems
 ):
-    copies = [pltpu.make_async_copy(q_hbm.at[:, pl.ds(chunk * CW, CW)], q_ref, sems.at[6])]
-    copies += pool_copies(kv, far, near, keys, values, sems)
+    copies = pool_copies(kv, far, near, keys, values, sems)
     for copy in copies:
         copy.start()
     for copy in copies:
         copy.wait()
 
-    def outward(b):
-        return [
-            pltpu.make_async_copy(att.at[block_rows(b)], att_hbm.at[block_rows(b)], out_sems.at[b]),
-            pltpu.make_async_copy(att_t.at[b], att_t_hbm.at[b], out_sems.at[BLK_DEV + b]),
-        ]
-
     groups = [slice(at, at + FW) for at in range(0, CW, FW)]
 
     def block(b, _):
         steps, odd, diag = tiles_of(table, b)
-        q_t = [flipped_heads(q_ref[block_rows(b), cols]) for cols in groups]
+        q_t = [
+            flipped_heads(q_ref[block_rows(b), chunk * CW + cols.start : chunk * CW + cols.stop])
+            for cols in groups
+        ]
 
         def tile(step, mask, carry):
             low = low_of(step, odd, diag)
@@ -172,14 +167,9 @@
                 at = cols.start + head * HD
                 att[block_rows(b), at : at + HD] = out[:, head * HD : (head + 1) * HD].T
             total_ref[b, :, cols] = top + jnp.log2(total)
-        for copy in outward(b):
-            copy.start()
         return _
 
     lax.fori_loop(0, BLK_DEV, block, 0)
-    for b in range(BLK_DEV):
-        for copy in outward(b):
-            copy.wait()
 
 
 def forward(table, queries, kv, far, near, chunk):
@@ -188,8 +178,8 @@
 
     return pl.pallas_call(
         kernel,
-        in_specs=[SMEM] + [ANY] * 4,
-        out_specs=[ANY, ANY, WHOLE],
+        in_specs=[SMEM, WHOLE] + [ANY] * 3,
+        out_specs=[WHOLE] * 3,
         out_shape=[
             jax.ShapeDtypeStruct((ROWS, CW), jnp.bfloat16),
             jax.ShapeDtypeStruct((BLK_DEV, HD, CW), jnp.bfloat16),
@@ -198,11 +188,7 @@
         scratch_shapes=[
             pltpu.VMEM((POOL * BLOCK, HD), jnp.bfloat16),
             pltpu.VMEM((POOL * BLOCK, HD), jnp.bfloat16),
-            pltpu.VMEM((ROWS, CW), jnp.bfloat16),
-            pltpu.VMEM((ROWS, CW), jnp.bfloat16),
-            pltpu.VMEM((BLK_DEV, HD, CW), jnp.bfloat16),
-            pltpu.SemaphoreType.DMA((7,)),
-            pltpu.SemaphoreType.DMA((2 * BLK_DEV,)),
+            pltpu.SemaphoreType.DMA((6,)),
         ],
         compiler_params=PARAMS,
         cost_estimate=lasting(8),
@@ -221,7 +207,7 @@
 
 def backward_kernel(chunk, last, first, *refs):
     refs = list(refs)
-    table, q_hbm, att_t_hbm, total_ref, kv, far, near = refs[:7]
+    table, q_ref, att_t, total_ref, kv, far, near = refs[:7]
     sources = refs[7:11]
     refs = refs[11:]
     if not first:
@@ -235,16 +221,13 @@
     else:
         key_acc, value_acc = refs[1:3]
         refs = refs[3:]
-    keys, values, q_ref, att_t, grads, dq, sems, grad_sems, out_sems = refs[-9:]
-
-    incoming = [
-        pltpu.make_async_copy(q_hbm.at[:, pl.ds(chunk * CW, CW)], q_ref, sems.at[6]),
-        pltpu.make_async_copy(att_t_hbm, att_t, sems.at[7]),
-    ]
+    keys, values, grads, dq, sems, grad_sems, out_sems = refs[-7:]
+
+    incoming = []
     if not first:
         incoming += [
-            pltpu.make_async_copy(key_in, key_acc, sems.at[8]),
-            pltpu.make_async_copy(value_in, value_acc, sems.at[9]),
+            pltpu.make_async_copy(key_in, key_acc, sems.at[6]),
+            pltpu.make_async_copy(value_in, value_acc, sems.at[7]),
         ]
     incoming += pool_copies(kv, far, near, keys, values, sems)
     for at in range(BLK_DEV):
@@ -274,7 +257,7 @@
         steps, odd, diag = tiles_of(table, b)
         held = []
         for cols in groups:
-            q = q_ref[block_rows(b), cols]
+            q = q_ref[block_rows(b), chunk * CW + cols.start : chunk * CW + cols.stop]
             g = grads[block_rows(b), cols]
             g_t = flipped_heads(g)
             delta = jnp.sum(
@@ -350,7 +333,7 @@
 
     return pl.pallas_call(
         kernel,
-        in_specs=[SMEM, ANY, ANY, WHOLE] + [ANY] * (7 if first else 10),
+        in_specs=[SMEM] + [WHOLE] * 3 + [ANY] * (7 if first else 10),
         out_specs=[ANY] + [WHOLE] * len(out_shape),
         out_shape=[jax.ShapeDtypeStruct((ROWS, WIDTH), jnp.bfloat16)] + out_shape,
         input_output_aliases={} if first else {11: 0},
@@ -359,10 +342,8 @@
             pltpu.VMEM(pool_shape, jnp.bfloat16),
             pltpu.VMEM(pool_shape, jnp.bfloat16),
             pltpu.VMEM((ROWS, CW), jnp.bfloat16),
-            pltpu.VMEM((BLK_DEV, HD, CW), jnp.bfloat16),
             pltpu.VMEM((ROWS, CW), jnp.bfloat16),
-            pltpu.VMEM((ROWS, CW), jnp.bfloat16),
-            pltpu.SemaphoreType.DMA((10,)),
+            pltpu.SemaphoreType.DMA((8,)),
             pltpu.SemaphoreType.DMA((BLK_DEV,)),
             pltpu.SemaphoreType.DMA((BLK_DEV,)),
         ],
@@ -372,45 +353,53 @@
     )(table, queries, att_t, totals, *pool, *sources, *([] if first else carried))
 
 
-def grad_matmul_kernel(chunk, table, *refs):
-    pieces, weight_hbm, out, weight, sems = refs[:8], *refs[8:]
+def grad_matmul_kernel(
+    table, own, ahead_rows, opposite_upper, opposite_lower, before_rows, weight_hbm, *refs
+):
+    outs, weight, sems = refs[:CHUNKS], *refs[CHUNKS:]
     half = ROWS // 2
     copies = []
-    for ahead in range(4):
-        at = pl.multiple_of(((table[TP] + ahead) % 4) * WIDTH, WIDTH)
-        copies.append(
-            pltpu.make_async_copy(
-                weight_hbm.at[pl.ds(chunk * CW, CW), pl.ds(at, WIDTH)],
-                weight.at[ahead],
-                sems.at[ahead],
+    for chunk in range(CHUNKS):
+        for ahead in range(4):
+            at = pl.multiple_of(((table[TP] + ahead) % 4) * WIDTH, WIDTH)
+            copies.append(
+                pltpu.make_async_copy(
+                    weight_hbm.at[pl.ds(chunk * CW, CW), pl.ds(at, WIDTH)],
+                    weight.at[4 * chunk + ahead],
+                    sems.at[4 * chunk + ahead],
+                )
             )
-        )
-        copies[-1].start()
-    totals = [None, None]
-    for ahead in range(4):
-        copies[ahead].wait()
-        for part in range(2):
-            term = dot_nt(pieces[2 * ahead + part][...], weight[ahead])
-            totals[part] = term if totals[part] is None else totals[part] + term
-    for part in range(2):
-        out[part * half : (part + 1) * half] = totals[part].astype(jnp.bfloat16)
-
-
-def grad_matmul(table, pieces, weight, chunk):
-    def kernel(*refs):
-        grad_matmul_kernel(chunk, *refs)
-
-    return pl.pallas_call(
-        kernel,
-        in_specs=[SMEM] + [WHOLE] * 8 + [ANY],
-        out_specs=WHOLE,
-        out_shape=jax.ShapeDtypeStruct((ROWS, CW), jnp.bfloat16),
+            copies[-1].start()
+    for chunk in range(CHUNKS):
+        total = None
+        for ahead, rows in enumerate((own, ahead_rows, None, before_rows)):
+            slot = 4 * chunk + ahead
+            copies[slot].wait()
+            if rows is None:
+                term = jnp.concatenate(
+                    [
+                        dot_nt(part[...], weight[slot]) for part in (opposite_upper, opposite_lower)
+                    ],
+                    axis=0,
+                )
+            else:
+                term = dot_nt(rows[...], weight[slot])
+            total = term if total is None else total + term
+        outs[chunk][...] = total.astype(jnp.bfloat16)
+
+
+def grad_matmul(table, pieces, weight):
+    return pl.pallas_call(
+        grad_matmul_kernel,
+        in_specs=[SMEM] + [WHOLE] * 5 + [ANY],
+        out_specs=[WHOLE] * CHUNKS,
+        out_shape=[jax.ShapeDtypeStruct((ROWS, CW), jnp.bfloat16)] * CHUNKS,
         scratch_shapes=[
-            pltpu.VMEM((4, CW, WIDTH), jnp.bfloat16),
-            pltpu.SemaphoreType.DMA((4,)),
+            pltpu.VMEM((4 * CHUNKS, CW, WIDTH), jnp.bfloat16),
+            pltpu.SemaphoreType.DMA((4 * CHUNKS,)),
         ],
         compiler_params=PARAMS,
-        cost_estimate=lasting(4),
+        cost_estimate=lasting(7),
         name="grad_projection",
     )(table, *pieces, weight)
 
@@ -594,24 +583,22 @@
     )(keys, values)
 
 
-def halve_kernel(grads, upper, lower, sems):
+def halve_kernel(before, ahead, upper, lower, sems):
     half = ROWS // 2
-    copy_all(
-        (grads.at[pl.ds(0, half)], upper), (grads.at[pl.ds(half, half)], lower), sems=sems
-    )
-
-
-def halve(grads):
+    copy_all((before.at[pl.ds(0, half)], upper), (ahead.at[pl.ds(half, half)], lower), sems=sems)
+
+
+def halve(before, ahead):
     return pl.pallas_call(
         halve_kernel,
-        in_specs=[HBM],
+        in_specs=[ANY] * 2,
         out_specs=[WHOLE] * 2,
         out_shape=[jax.ShapeDtypeStruct((ROWS // 2, WIDTH), jnp.bfloat16)] * 2,
         scratch_shapes=[pltpu.SemaphoreType.DMA((2,))],
         compiler_params=PARAMS,
-        cost_estimate=lasting(2),
+        cost_estimate=lasting(1),
         name="halve",
-    )(grads)
+    )(before, ahead)
 
 
 def add_kernel(own, near, far, keys, values):
@@ -647,44 +634,31 @@
     near = shift_cp(kv, 1)
     pool = (kv, far, near)
 
-    upper, lower = halve(after(grad_mixed, kv))
-    before_upper = shift_tp(upper, 1)
-    after_lower = shift_tp(lower, -1)
-    before_lower = shift_tp(lower, 1)
-    after_upper = shift_tp(upper, -1)
+    grads_in = after(grad_mixed, kv)
+    grads_before = shift_tp(grads_in, 1)
+    grads_ahead = shift_tp(grads_in, -1)
 
     attended, attended_t, totals = [], [], []
     for chunk in range(CHUNKS):
         att, att_t, total = forward(
-            after(table, (attended[0], before_upper, after_lower, before_lower, after_upper))
+            after(table, (attended[0], upper, lower))
             if chunk
             else table,
             queries,
             *pool,
             chunk,
         )
+        if chunk == 0:
+            upper, lower = halve(after(grads_before, att), grads_ahead)
         attended.append(att)
         attended_t.append(att_t)
         totals.append(total)
 
-    arrived = (attended[0], before_lower, after_upper)
-    opposite_upper = shift_tp(after(before_upper, arrived), 1)
-    opposite_lower = shift_tp(after(after_lower, arrived), -1)
-    pieces = [
-        upper,
-        lower,
-        after_upper,
-        after_lower,
-        opposite_upper,
-        opposite_lower,
-        before_upper,
-        before_lower,
-    ]
+    pieces = (grad_mixed, grads_ahead, shift_tp(upper, 1), shift_tp(lower, -1), grads_before)
     exchanged = [group_exchange(attended[0], attended[1]), None]
-    grad_attended = [grad_matmul(table, pieces, out_proj, 0), None]
-    exchanged[1] = group_exchange(attended[1], grad_attended[0])
+    grad_attended = grad_matmul(table, pieces, out_proj)
+    exchanged[1] = group_exchange(attended[1], grad_attended[1])
     grad_across = swap_cp(grad_attended[0], 2)
-    grad_attended[1] = grad_matmul(after(table, grad_attended[0]), pieces, out_proj, 1)
 
     far_left, far_right, onward_b, back_a, own, rows = products(
         after(table, grad_attended[1]), exchanged, out_proj
@@ -720,7 +694,7 @@
     before_a = shift_tp(onward_a, 1)
     after_b = shift_tp(back_b, -1)
     query_grad, own_grads, near_grads, far_grads = backward(
-        after(table, onward_a),
+        after(table, (onward_a, before_b, after_a)),
         queries, attended_t[1], totals[1], pool, grad_sources[1], carried, 1, True,
     )
     far_back = shift_cp(after(far_grads, (before_b, after_a)), -2)

time: 128 us -> 127 us (level)
  Pallas kernels: 64.8 us -> 51.3 us
  waiting for transfers between devices: 23 us -> 30.7 us
  starting transfers between devices: 35.3 us -> 40.1 us
    pallas_call x7 -> x6, Pallas kernels: 50.9 us -> 37.4 us  [the longest x2 16.4 us: backward(): pl.pallas_call(kernel, in_specs=[SMEM] + [WHOLE] * 3 + [ANY] * (7 if firs...]
    ppermute x4, starting transfers between devices: 11.6 us -> 18.7 us  [shift_cp(): return lax.ppermute(block, 'cp', route)]
    ppermute x12 -> x10, waiting for transfers between devices: 4.51 us -> 10.7 us  [shift_tp(): lax.ppermute(block, 'tp', [(i, (i + distance) % count) for i in range(cou...]
    ppermute x12 -> x10, starting transfers between devices: 19.2 us -> 14.8 us  [shift_tp(): lax.ppermute(block, 'tp', [(i, (i + distance) % count) for i in range(cou...]
    ppermute x12, starting transfers between devices: 4.51 us -> 6.56 us  [swap_cp(): return lax.ppermute(block, 'cp', [(i, i ^ mask) for i in range(count)])]
  transfers between devices with their start and end apart: 28 -> 26, of which waited for: 6 -> 8; matrix products, arithmetic and copies ran while one was open for 0% -> 0% of each run, Pallas kernels for 50% -> 39%
where the time goes in v3:
time: 127 us; the launch traced here: 126 us
  Pallas kernels  51.3 us (40%)
  starting transfers between devices  40.1 us (32%)
  waiting for transfers between devices  30.7 us (24%)
  local copies, waits for them, and re-layouts  2.85 us (2%)
    ppermute x4, starting transfers between devices, shift_cp(): return lax.ppermute(block, 'cp', route)  18.7 us
    pallas_call x2, Pallas kernels, backward(): pl.pallas_call(kernel, in_specs=[SMEM] + [WHOLE] * 3 + [ANY] * (7 if firs...  16.4 us
    ppermute x10, starting transfers between devices, shift_tp(): lax.ppermute(block, 'tp', [(i, (i + distance) % count) for i in range(cou...  14.8 us
    ppermute x4, waiting for transfers between devices, shift_cp(): return lax.ppermute(block, 'cp', route)  12.1 us
    pallas_call x2, Pallas kernels, forward(): pl.pallas_call(kernel, in_specs=[SMEM, WHOLE] + [ANY] * 3, out_specs=[WHO...  11.8 us
    ppermute x10, waiting for transfers between devices, shift_tp(): lax.ppermute(block, 'tp', [(i, (i + distance) % count) for i in range(cou...  10.7 us
    pallas_call x1, Pallas kernels, grad_matmul(): pl.pallas_call(grad_matmul_kernel, in_specs=[SMEM] + [WHOLE] * 5 + [ANY],...  8.16 us
    ppermute x12, waiting for transfers between devices, swap_cp(): return lax.ppermute(block, 'cp', [(i, i ^ mask) for i in range(count)])  7.87 us
  transfers between devices with their start and end apart: 26, of which 8 were waited for; matrix products, arithmetic and copies ran while one was open for 0% of the time, Pallas kernels for 39%

profile of v3, /device:TPU:24, one launch (start us, length us, event | category | flops | bytes accessed | tf_op | source)
XLA Modules:
  0.0 126.4 jit_solution(14749477067934837770)
XLA Ops:
  0.6 0.0 copy-start.1
  0.7 1.0 copy-done.2
  1.7 0.9 copy-done.3
  2.6 0.8 join.1
  3.4 2.8 %collective-permute-start = (bf16[512,1024]{1,0:T(8,128)(2,1)S(1)}, bf16[512,1024]{1,0:T(8,128)(2,1)S(1)}, u32[]{:S(2)}, u32[]{:S(2)}) collective-permute-start(bf16[512,1024]{1,0:T(8,128)(2,1)S(1)} %copy-done), channel_id=1, source_target_pairs={{0,3},{1,0},{2,1},{3,2},{4,7},{5,4},{6,5},{7,6},{8,11},{9,8},{10,9... | collective-permute-start | bytes 3145736 | tf_op jit(solution)/shard_map/ppermute | solution.py:68
  6.3 0.0 collective-permute-start.1
  6.3 1.9 %collective-permute-start.3 = (bf16[512,256]{1,0:T(8,128)(2,1)S(1)}, bf16[512,256]{1,0:T(8,128)(2,1)}, u32[]{:S(2)}, u32[]{:S(2)}) collective-permute-start(bf16[512,256]{1,0:T(8,128)(2,1)S(1)} %get-tuple-element.52.refs_2_.refs_4_), channel_id=1, source_target_pairs={{0,4},{4,8},{8,12},{12,16},{16,20},{20,24},{24,28},{28,32},{32,36}... | collective-permute-start | bytes 786440 | tf_op jit(solution)/shard_map/ppermute | solution.py:63
  8.2 3.8 %collective-permute-start.2 = (bf16[384,256]{1,0:T(8,128)(2,1)}, bf16[384,256]{1,0:T(8,128)(2,1)}, u32[]{:S(2)}, u32[]{:S(2)}) collective-permute-start(bf16[384,256]{1,0:T(8,128)(2,1)} %get-tuple-element.54), channel_id=1, source_target_pairs={{0,8},{4,12},{8,16},{12,20},{16,24},{20,28},{24,32},{28,36},{32,40... | collective-permute-start | bytes 589832 | tf_op jit(solution)/shard_map/ppermute | solution.py:63
  12.1 0.1 dynamic-slice_subtract_fusion
  12.1 0.1 select_reduce_fusion
  12.3 0.1 and_select_fusion
  12.3 0.1 and_select_fusion.2
  12.4 0.1 dynamic-slice_subtract_fusion.1
  12.5 0.1 fusion
  12.6 0.1 concatenate.3.refs_0_.table
  12.7 9.0 %collective-permute-done.2.refs_3_.refs_5_ = bf16[384,256]{1,0:T(8,128)(2,1)} collective-permute-done((bf16[384,256]{1,0:T(8,128)(2,1)}, bf16[384,256]{1,0:T(8,128)(2,1)}, u32[]{:S(2)}, u32[]{:S(2)}) %collective-permute-start.2) | collective-permute-done | bytes 196640 | tf_op jit(solution)/shard_map/ppermute | solution.py:63
  21.7 0.0 collective-permute-done.3.refs_4_.refs_6_
  21.7 5.9 %attention_forward.2 = (bf16[512,512]{1,0:T(8,128)(2,1)S(1)}, bf16[4,128,512]{2,1,0:T(8,128)(2,1)S(1)}, f32[4,1,512]{2,1,0:T(1,128)S(1)}) custom-call(s32[22]{0:T(128)S(1)} %concatenate.3.refs_0_.table, bf16[512,1024]{1,0:T(8,128)(2,1)S(1)} %copy-done.1, bf16[512,256]{1,0:T(8,128)(2,1)S(1)} %get-tuple-element.52.refs_2_.refs_4_, ...), custom_call_target="tpu_custom_call" | custom-call | flops 9200000000 | bytes 28800000 | tf_op jit(solution)/shard_map/attention_forward/pallas_call | solution.py:179
  27.6 0.1 collective-permute-start.7
  27.7 4.5 %collective-permute-done.1.before.before_rows = bf16[512,1024]{1,0:T(8,128)(2,1)} collective-permute-done((bf16[512,1024]{1,0:T(8,128)(2,1)S(1)}, bf16[512,1024]{1,0:T(8,128)(2,1)}, u32[]{:S(2)}, u32[]{:S(2)}) %collective-permute-start.1) | collective-permute-done | bytes 1048608 | tf_op jit(solution)/shard_map/ppermute | solution.py:68
  32.2 0.0 collective-permute-done.ahead.ahead_rows
  32.2 1.1 halve.1
  33.3 0.1 collective-permute-start.4
  33.4 3.2 %collective-permute-start.5 = (bf16[256,1024]{1,0:T(8,128)(2,1)S(1)}, bf16[256,1024]{1,0:T(8,128)(2,1)S(1)}, u32[]{:S(2)}, u32[]{:S(2)}) collective-permute-start(bf16[256,1024]{1,0:T(8,128)(2,1)S(1)} %get-tuple-element.58), channel_id=1, source_target_pairs={{0,3},{1,0},{2,1},{3,2},{4,7},{5,4},{6,5},{7,6},{8,11},{9,8},{10,9... | collective-permute-start | bytes 1572872 | tf_op jit(solution)/shard_map/ppermute | solution.py:68
  36.6 5.9 %attention_forward.3 = (bf16[512,512]{1,0:T(8,128)(2,1)S(1)}, bf16[4,128,512]{2,1,0:T(8,128)(2,1)S(1)}, f32[4,1,512]{2,1,0:T(1,128)S(1)}) custom-call(s32[22]{0:T(128)S(1)} %concatenate.3.refs_0_.table, bf16[512,1024]{1,0:T(8,128)(2,1)S(1)} %copy-done.1, bf16[512,256]{1,0:T(8,128)(2,1)S(1)} %get-tuple-element.52.refs_2_.refs_4_, ...), custom_call_target="tpu_custom_call" | custom-call | flops 9200000000 | bytes 28800000 | tf_op jit(solution)/shard_map/attention_forward/pallas_call | solution.py:179
  42.5 1.0 collective-permute-start.10
  43.5 0.0 collective-permute-start.6
  43.5 0.0 collective-permute-done.7.refs_2_
  43.5 0.5 collective-permute-start.8
  44.0 3.0 %collective-permute-done.4.opposite_upper = bf16[256,1024]{1,0:T(8,128)(2,1)S(1)} collective-permute-done((bf16[256,1024]{1,0:T(8,128)(2,1)S(1)}, bf16[256,1024]{1,0:T(8,128)(2,1)S(1)}, u32[]{:S(2)}, u32[]{:S(2)}) %collective-permute-start.4) | collective-permute-done | bytes 524320 | tf_op jit(solution)/shard_map/ppermute | solution.py:68
  47.0 0.0 collective-permute-done.5.opposite_lower
  47.0 8.2 %grad_projection.1 = (bf16[512,512]{1,0:T(8,128)(2,1)S(1)}, bf16[512,512]{1,0:T(8,128)(2,1)S(1)}) custom-call(s32[22]{0:T(128)S(1)} %concatenate.3.refs_0_.table, bf16[512,1024]{1,0:T(8,128)(2,1)S(1)} %copy-done, bf16[512,1024]{1,0:T(8,128)(2,1)S(1)} %collective-permute-done.ahead.ahead_rows, bf16[256,1024]{1,0:T(8,128)(2,1)S(1)} %collective-permute-done.4.opposite_upper, ...), custom_call_target="tpu_custom_call" | custom-call | flops 8049999872 | bytes 25200000 | tf_op jit(solution)/shard_map/grad_projection/pallas_call | solution.py:392
  55.2 0.1 collective-permute-start.9
  55.3 0.0 collective-permute-done.10.refs_6_
  55.3 0.5 collective-permute-start.11
  55.8 1.9 %collective-permute-start.13 = (bf16[512,512]{1,0:T(8,128)(2,1)S(1)}, bf16[512,512]{1,0:T(8,128)(2,1)S(1)}, u32[]{:S(2)}, u32[]{:S(2)}) collective-permute-start(bf16[512,512]{1,0:T(8,128)(2,1)S(1)} %get-tuple-element.72.refs_7_), channel_id=1, source_target_pairs={{0,8},{4,12},{8,0},{12,4},{16,24},{20,28},{24,16},{28,20},{32,40},... | collective-permute-start | bytes 1572872 | tf_op jit(solution)/shard_map/ppermute | solution.py:57
  57.7 0.0 collective-permute-done.6.refs_1_
  57.7 0.0 collective-permute-done.8.refs_3_
  57.7 0.0 collective-permute-done.9.refs_5_
  57.7 0.2 collective-permute-done.11.refs_7_
  58.0 0.8 copy-done.8
  58.7 7.4 %products.1 = (bf16[512,512]{1,0:T(8,128)(2,1)S(1)}, bf16[512,512]{1,0:T(8,128)(2,1)S(1)}, bf16[512,512]{1,0:T(8,128)(2,1)S(1)}, bf16[512,512]{1,0:T(8,128)(2,1)...) custom-call(s32[22]{0:T(128)S(1)} %concatenate.3.refs_0_.table, ...), custom_call_target="tpu_custom_call" | custom-call | flops 8049999872 | bytes 25200000 | tf_op jit(solution)/shard_map/products/pallas_call | solution.py:448
  66.1 0.2 collective-permute-start.12
  66.4 3.7 %collective-permute-done.13.refs_9_ = bf16[512,512]{1,0:T(8,128)(2,1)S(1)} collective-permute-done((bf16[512,512]{1,0:T(8,128)(2,1)S(1)}, bf16[512,512]{1,0:T(8,128)(2,1)S(1)}, u32[]{:S(2)}, u32[]{:S(2)}) %collective-permute-start.13) | collective-permute-done | bytes 524320 | tf_op jit(solution)/shard_map/ppermute | solution.py:57
  70.1 0.0 collective-permute-start.14
  70.1 0.0 collective-permute-start.15
  70.1 3.2 %collective-permute-start.16 = (bf16[512,512]{1,0:T(8,128)(2,1)S(1)}, bf16[512,512]{1,0:T(8,128)(2,1)S(1)}, u32[]{:S(2)}, u32[]{:S(2)}) collective-permute-start(bf16[512,512]{1,0:T(8,128)(2,1)S(1)} %get-tuple-element.78), channel_id=1, source_target_pairs={{0,3},{1,0},{2,1},{3,2},{4,7},{5,4},{6,5},{7,6},{8,11},{9,8},{10,9... | collective-permute-start | bytes 1572872 | tf_op jit(solution)/shard_map/ppermute | solution.py:68
  73.4 3.2 %collective-permute-start.19 = (bf16[512,512]{1,0:T(8,128)(2,1)S(1)}, bf16[512,512]{1,0:T(8,128)(2,1)S(1)}, u32[]{:S(2)}, u32[]{:S(2)}) collective-permute-start(bf16[512,512]{1,0:T(8,128)(2,1)S(1)} %get-tuple-element.81), channel_id=1, source_target_pairs={{0,3},{1,0},{2,1},{3,2},{4,7},{5,4},{6,5},{7,6},{8,11},{9,8},{10,9... | collective-permute-start | bytes 1572872 | tf_op jit(solution)/shard_map/ppermute | solution.py:68
  76.6 1.7 %collective-permute-start.22 = (bf16[512,512]{1,0:T(8,128)(2,1)S(1)}, bf16[512,512]{1,0:T(8,128)(2,1)S(1)}, u32[]{:S(2)}, u32[]{:S(2)}) collective-permute-start(bf16[512,512]{1,0:T(8,128)(2,1)S(1)} %get-tuple-element.87.refs_7_), channel_id=1, source_target_pairs={{0,8},{4,12},{8,0},{12,4},{16,24},{20,28},{24,16},{28,20},{32,40},... | collective-permute-start | bytes 1572872 | tf_op jit(solution)/shard_map/ppermute | solution.py:57
  78.3 7.6 %attention_backward.2 = (bf16[512,1024]{1,0:T(8,128)(2,1)}, f32[1408,128]{1,0:T(8,128)S(1)}, f32[1408,128]{1,0:T(8,128)S(1)}) custom-call(s32[22]{0:T(128)S(1)} %concatenate.3.refs_0_.table, bf16[512,1024]{1,0:T(8,128)(2,1)S(1)} %copy-done.1, bf16[4,128,512]{2,1,0:T(8,128)(2,1)S(1)} %get-tuple-element.69.refs_2_, ...), custom_call_target="tpu_custom_call" | custom-call | flops 10350000128 | bytes 32400000 | tf_op jit(solution)/shard_map/attention_backward/pallas_call | solution.py:334
  85.9 3.9 %collective-permute-done.22.refs_9_ = bf16[512,512]{1,0:T(8,128)(2,1)S(1)} collective-permute-done((bf16[512,512]{1,0:T(8,128)(2,1)S(1)}, bf16[512,512]{1,0:T(8,128)(2,1)S(1)}, u32[]{:S(2)}, u32[]{:S(2)}) %collective-permute-start.22) | collective-permute-done | bytes 524320 | tf_op jit(solution)/shard_map/ppermute | solution.py:57
  89.8 0.5 collective-permute-start.23
  90.3 3.2 %sum_products.1 = (bf16[512,512]{1,0:T(8,128)(2,1)S(1)}, bf16[512,512]{1,0:T(8,128)(2,1)S(1)}) custom-call(s32[22]{0:T(128)S(1)} %concatenate.3.refs_0_.table, bf16[512,1024]{1,0:T(8,128)(2,1)S(1)} %copy-done.5, bf16[1024,4096]{1,0:T(8,128)(2,1)} %weight_hbm.3, bf16[512,512]{1,0:T(8,128)(2,1)S(1)} %collective-permute-done.15.before, ...), custom_call_target="tpu_custom_call" | custom-call | flops 4600000000 | bytes 14400000 | tf_op jit(solution)/shard_map/sum_products/pallas_call | solution.py:480
  93.6 0.1 collective-permute-start.17
  93.7 3.2 %collective-permute-done.18.before_b = bf16[512,512]{1,0:T(8,128)(2,1)S(1)} collective-permute-done((bf16[512,512]{1,0:T(8,128)(2,1)S(1)}, bf16[512,512]{1,0:T(8,128)(2,1)S(1)}, u32[]{:S(2)}, u32[]{:S(2)}) %collective-permute-start.18) | collective-permute-done | bytes 524320 | tf_op jit(solution)/shard_map/ppermute | solution.py:68
  96.9 2.1 %collective-permute-start.20 = (bf16[512,512]{1,0:T(8,128)(2,1)S(1)}, bf16[512,512]{1,0:T(8,128)(2,1)S(1)}, u32[]{:S(2)}, u32[]{:S(2)}) collective-permute-start(bf16[512,512]{1,0:T(8,128)(2,1)S(1)} %get-tuple-element.82), channel_id=1, source_target_pairs={{0,3},{1,0},{2,1},{3,2},{4,7},{5,4},{6,5},{7,6},{8,11},{9,8},{10,9... | collective-permute-start | bytes 1572872 | tf_op jit(solution)/shard_map/ppermute | solution.py:68
  99.0 0.0 copy-start.4
  99.0 8.8 %attention_backward.3 = (bf16[512,1024]{1,0:T(8,128)(2,1)}, f32[512,256]{1,0:T(8,128)S(1)}, bf16[512,256]{1,0:T(8,128)(2,1)S(1)}, bf16[384,256]{1,0:T(8,128)(2,1)S(1)}) custom-call(s32[22]{0:T(128)S(1)} %concatenate.3.refs_0_.table, bf16[512,1024]{1,0:T(8,128)(2,1)} %refs_1_.7, ...), custom_call_target="tpu_custom_call", output_to_operand_aliasing={{0}: (11, {})} | custom-call | flops 10350000128 | bytes 32400000 | tf_op jit(solution)/shard_map/attention_backward/pallas_call | solution.py:334
  107.9 6.0 %collective-permute-start.24 = (bf16[512,256]{1,0:T(8,128)(2,1)S(1)}, bf16[512,256]{1,0:T(8,128)(2,1)S(1)}, u32[]{:S(2)}, u32[]{:S(2)}) collective-permute-start(bf16[512,256]{1,0:T(8,128)(2,1)S(1)} %get-tuple-element.95), channel_id=1, source_target_pairs={{4,0},{8,4},{12,8},{16,12},{20,16},{24,20},{28,24},{32,28},{36,32}... | collective-permute-start | bytes 786440 | tf_op jit(solution)/shard_map/ppermute | solution.py:63
  113.8 7.0 %collective-permute-start.25 = (bf16[384,256]{1,0:T(8,128)(2,1)S(1)}, bf16[384,256]{1,0:T(8,128)(2,1)S(1)}, u32[]{:S(2)}, u32[]{:S(2)}) collective-permute-start(bf16[384,256]{1,0:T(8,128)(2,1)S(1)} %get-tuple-element.97), channel_id=1, source_target_pairs={{8,0},{12,4},{16,8},{20,12},{24,16},{28,20},{32,24},{36,28},{40,32... | collective-permute-start | bytes 589832 | tf_op jit(solution)/shard_map/ppermute | solution.py:63
  120.9 0.0 collective-permute-done.20.after_b
  120.9 1.7 %last_sum.1 = bf16[512,1024]{1,0:T(8,128)(2,1)} custom-call(bf16[512,1024]{1,0:T(8,128)(2,1)S(1)} %copy-done.4, bf16[512,512]{1,0:T(8,128)(2,1)S(1)} %collective-permute-done.17.before_a, bf16[512,512]{1,0:T(8,128)(2,1)S(1)} %collective-permute-done.18.before_b, bf16[512,512]{1,0:T(8,128)(2,1)S(1)} %collective-permute-done.19.after_a, ...), custom_call_target="tpu_custom_call" | custom-call | flops 2300000000 | bytes 7200000 | tf_op jit(solution)/shard_map/last_sum/pallas_call | solution.py:506
  122.7 3.0 %collective-permute-done.25.far = bf16[384,256]{1,0:T(8,128)(2,1)S(1)} collective-permute-done((bf16[384,256]{1,0:T(8,128)(2,1)S(1)}, bf16[384,256]{1,0:T(8,128)(2,1)S(1)}, u32[]{:S(2)}, u32[]{:S(2)}) %collective-permute-start.25) | collective-permute-done | bytes 196640 | tf_op jit(solution)/shard_map/ppermute | solution.py:63
  125.7 0.7 add_terms.1
  (24 shorter events, 0.1 us)
Async XLA Ops:
  0.6 2.8 %copy-start = (bf16[512,1024]{1,0:T(8,128)(2,1)S(1)}, bf16[512,1024]{1,0:T(8,128)(2,1)}, u32[]{:S(2)}) copy-start(bf16[512,1024]{1,0:T(8,128)(2,1)} %own.1) | copy-start | bytes 3145732
  0.6 21.1 %copy-start.1 = (bf16[512,1024]{1,0:T(8,128)(2,1)S(1)}, bf16[512,1024]{1,0:T(8,128)(2,1)}, u32[]{:S(2)}) copy-start(bf16[512,1024]{1,0:T(8,128)(2,1)} %refs_1_.7) | copy-start | bytes 3145732
  0.7 1.1 copy-start.2
  1.7 0.9 copy-start.3
  2.6 9.5 %copy-start.6 = (s32[256]{0:T(256)S(1)}, s32[256]{0:T(256)}, u32[]{:S(2)}) copy-start(s32[256]{0:T(256)} %param.13) | copy-start | bytes 3076
  2.6 9.8 %copy-start.7 = (s32[256]{0:T(256)S(1)}, s32[256]{0:T(256)}, u32[]{:S(2)}) copy-start(s32[256]{0:T(256)} %param.12) | copy-start | bytes 3076
  3.4 28.8 %collective-permute-start = (bf16[512,1024]{1,0:T(8,128)(2,1)S(1)}, bf16[512,1024]{1,0:T(8,128)(2,1)S(1)}, u32[]{:S(2)}, u32[]{:S(2)}) collective-permute-start(bf16[512,1024]{1,0:T(8,128)(2,1)S(1)} %copy-done), channel_id=1, source_target_pairs={{0,3},{1,0},{2,1},{3,2},{4,7},{5,4},{6,5},{7,6},{8,11},{9,8},{10,9... | collective-permute-start | bytes 3145736 | tf_op jit(solution)/shard_map/ppermute | solution.py:68
  6.3 25.9 %collective-permute-start.1 = (bf16[512,1024]{1,0:T(8,128)(2,1)S(1)}, bf16[512,1024]{1,0:T(8,128)(2,1)}, u32[]{:S(2)}, u32[]{:S(2)}) collective-permute-start(bf16[512,1024]{1,0:T(8,128)(2,1)S(1)} %copy-done), channel_id=1, source_target_pairs={{0,1},{1,2},{2,3},{3,0},{4,5},{5,6},{6,7},{7,4},{8,9},{9,10},{10,1... | collective-permute-start | bytes 3145736 | tf_op jit(solution)/shard_map/ppermute | solution.py:68
  6.3 15.5 %collective-permute-start.3 = (bf16[512,256]{1,0:T(8,128)(2,1)S(1)}, bf16[512,256]{1,0:T(8,128)(2,1)}, u32[]{:S(2)}, u32[]{:S(2)}) collective-permute-start(bf16[512,256]{1,0:T(8,128)(2,1)S(1)} %get-tuple-element.52.refs_2_.refs_4_), channel_id=1, source_target_pairs={{0,4},{4,8},{8,12},{12,16},{16,20},{20,24},{24,28},{28,32},{32,36}... | collective-permute-start | bytes 786440 | tf_op jit(solution)/shard_map/ppermute | solution.py:63
  8.2 13.5 %collective-permute-start.2 = (bf16[384,256]{1,0:T(8,128)(2,1)}, bf16[384,256]{1,0:T(8,128)(2,1)}, u32[]{:S(2)}, u32[]{:S(2)}) collective-permute-start(bf16[384,256]{1,0:T(8,128)(2,1)} %get-tuple-element.54), channel_id=1, source_target_pairs={{0,8},{4,12},{8,16},{12,20},{16,24},{20,28},{24,32},{28,36},{32,40... | collective-permute-start | bytes 589832 | tf_op jit(solution)/shard_map/ppermute | solution.py:63
  27.6 15.8 %collective-permute-start.7 = (bf16[512,512]{1,0:T(8,128)(2,1)S(1)}, bf16[512,512]{1,0:T(8,128)(2,1)S(1)}, u32[]{:S(2)}, u32[]{:S(2)}) collective-permute-start(bf16[512,512]{1,0:T(8,128)(2,1)S(1)} %get-tuple-element.63.refs_0_), channel_id=1, source_target_pairs={{0,8},{4,12},{8,0},{12,4},{16,24},{20,28},{24,16},{28,20},{32,40},... | collective-permute-start | bytes 1572872 | tf_op jit(solution)/shard_map/ppermute | solution.py:57
  33.3 13.8 %collective-permute-start.4 = (bf16[256,1024]{1,0:T(8,128)(2,1)S(1)}, bf16[256,1024]{1,0:T(8,128)(2,1)S(1)}, u32[]{:S(2)}, u32[]{:S(2)}) collective-permute-start(bf16[256,1024]{1,0:T(8,128)(2,1)S(1)} %get-tuple-element.57), channel_id=1, source_target_pairs={{0,1},{1,2},{2,3},{3,0},{4,5},{5,6},{6,7},{7,4},{8,9},{9,10},{10,1... | collective-permute-start | bytes 1572872 | tf_op jit(solution)/shard_map/ppermute | solution.py:68
  33.4 13.7 %collective-permute-start.5 = (bf16[256,1024]{1,0:T(8,128)(2,1)S(1)}, bf16[256,1024]{1,0:T(8,128)(2,1)S(1)}, u32[]{:S(2)}, u32[]{:S(2)}) collective-permute-start(bf16[256,1024]{1,0:T(8,128)(2,1)S(1)} %get-tuple-element.58), channel_id=1, source_target_pairs={{0,3},{1,0},{2,1},{3,2},{4,7},{5,4},{6,5},{7,6},{8,11},{9,8},{10,9... | collective-permute-start | bytes 1572872 | tf_op jit(solution)/shard_map/ppermute | solution.py:68
  42.5 12.8 %collective-permute-start.10 = (bf16[512,512]{1,0:T(8,128)(2,1)S(1)}, bf16[512,512]{1,0:T(8,128)(2,1)S(1)}, u32[]{:S(2)}, u32[]{:S(2)}) collective-permute-start(bf16[512,512]{1,0:T(8,128)(2,1)S(1)} %get-tuple-element.65.refs_4_), channel_id=1, source_target_pairs={{0,8},{4,12},{8,0},{12,4},{16,24},{20,28},{24,16},{28,20},{32,40},... | collective-permute-start | bytes 1572872 | tf_op jit(solution)/shard_map/ppermute | solution.py:57
  43.5 14.3 %collective-permute-start.6 = (bf16[512,512]{1,0:T(8,128)(2,1)S(1)}, bf16[512,512]{1,0:T(8,128)(2,1)S(1)}, u32[]{:S(2)}, u32[]{:S(2)}) collective-permute-start(bf16[512,512]{1,0:T(8,128)(2,1)S(1)} %get-tuple-element.63.refs_0_), channel_id=1, source_target_pairs={{0,4},{4,0},{8,12},{12,8},{16,20},{20,16},{24,28},{28,24},{32,36},... | collective-permute-start | bytes 1572872 | tf_op jit(solution)/shard_map/ppermute | solution.py:57
  43.5 14.3 %collective-permute-start.8 = (bf16[512,512]{1,0:T(8,128)(2,1)S(1)}, bf16[512,512]{1,0:T(8,128)(2,1)S(1)}, u32[]{:S(2)}, u32[]{:S(2)}) collective-permute-start(bf16[512,512]{1,0:T(8,128)(2,1)S(1)} %collective-permute-done.7.refs_2_), channel_id=1, source_target_pairs={{0,4},{4,0},{8,12},{12,8},{16,20},{20,16},{24,28},{28,24},{32,36},... | collective-permute-start | bytes 1572872 | tf_op jit(solution)/shard_map/ppermute | solution.py:57
  55.2 2.5 %collective-permute-start.9 = (bf16[512,512]{1,0:T(8,128)(2,1)S(1)}, bf16[512,512]{1,0:T(8,128)(2,1)S(1)}, u32[]{:S(2)}, u32[]{:S(2)}) collective-permute-start(bf16[512,512]{1,0:T(8,128)(2,1)S(1)} %get-tuple-element.65.refs_4_), channel_id=1, source_target_pairs={{0,4},{4,0},{8,12},{12,8},{16,20},{20,16},{24,28},{28,24},{32,36},... | collective-permute-start | bytes 1572872 | tf_op jit(solution)/shard_map/ppermute | solution.py:57
  55.3 2.6 %collective-permute-start.11 = (bf16[512,512]{1,0:T(8,128)(2,1)S(1)}, bf16[512,512]{1,0:T(8,128)(2,1)S(1)}, u32[]{:S(2)}, u32[]{:S(2)}) collective-permute-start(bf16[512,512]{1,0:T(8,128)(2,1)S(1)} %collective-permute-done.10.refs_6_), channel_id=1, source_target_pairs={{0,4},{4,0},{8,12},{12,8},{16,20},{20,16},{24,28},{28,24},{32,36},... | collective-permute-start | bytes 1572872 | tf_op jit(solution)/shard_map/ppermute | solution.py:57
  55.8 14.3 %collective-permute-start.13 = (bf16[512,512]{1,0:T(8,128)(2,1)S(1)}, bf16[512,512]{1,0:T(8,128)(2,1)S(1)}, u32[]{:S(2)}, u32[]{:S(2)}) collective-permute-start(bf16[512,512]{1,0:T(8,128)(2,1)S(1)} %get-tuple-element.72.refs_7_), channel_id=1, source_target_pairs={{0,8},{4,12},{8,0},{12,4},{16,24},{20,28},{24,16},{28,20},{32,40},... | collective-permute-start | bytes 1572872 | tf_op jit(solution)/shard_map/ppermute | solution.py:57
  58.0 0.8 copy-start.8
  66.1 7.2 %collective-permute-start.12 = (bf16[512,512]{1,0:T(8,128)(2,1)S(1)}, bf16[512,512]{1,0:T(8,128)(2,1)S(1)}, u32[]{:S(2)}, u32[]{:S(2)}) collective-permute-start(bf16[512,512]{1,0:T(8,128)(2,1)S(1)} %get-tuple-element.72.refs_7_), channel_id=1, source_target_pairs={{0,4},{4,0},{8,12},{12,8},{16,20},{20,16},{24,28},{28,24},{32,36},... | collective-permute-start | bytes 1572872 | tf_op jit(solution)/shard_map/ppermute | solution.py:57
  70.1 6.5 %collective-permute-start.14 = (bf16[512,512]{1,0:T(8,128)(2,1)S(1)}, bf16[512,512]{1,0:T(8,128)(2,1)S(1)}, u32[]{:S(2)}, u32[]{:S(2)}) collective-permute-start(bf16[512,512]{1,0:T(8,128)(2,1)S(1)} %collective-permute-done.13.refs_9_), channel_id=1, source_target_pairs={{0,4},{4,0},{8,12},{12,8},{16,20},{20,16},{24,28},{28,24},{32,36},... | collective-permute-start | bytes 1572872 | tf_op jit(solution)/shard_map/ppermute | solution.py:57
  70.1 19.7 %collective-permute-start.15 = (bf16[512,512]{1,0:T(8,128)(2,1)S(1)}, bf16[512,512]{1,0:T(8,128)(2,1)S(1)}, u32[]{:S(2)}, u32[]{:S(2)}) collective-permute-start(bf16[512,512]{1,0:T(8,128)(2,1)S(1)} %get-tuple-element.77), channel_id=1, source_target_pairs={{0,1},{1,2},{2,3},{3,0},{4,5},{5,6},{6,7},{7,4},{8,9},{9,10},{10,1... | collective-permute-start | bytes 1572872 | tf_op jit(solution)/shard_map/ppermute | solution.py:68
  70.1 20.2 %collective-permute-start.16 = (bf16[512,512]{1,0:T(8,128)(2,1)S(1)}, bf16[512,512]{1,0:T(8,128)(2,1)S(1)}, u32[]{:S(2)}, u32[]{:S(2)}) collective-permute-start(bf16[512,512]{1,0:T(8,128)(2,1)S(1)} %get-tuple-element.78), channel_id=1, source_target_pairs={{0,3},{1,0},{2,1},{3,2},{4,7},{5,4},{6,5},{7,6},{8,11},{9,8},{10,9... | collective-permute-start | bytes 1572872 | tf_op jit(solution)/shard_map/ppermute | solution.py:68
  73.3 23.5 %collective-permute-start.18 = (bf16[512,512]{1,0:T(8,128)(2,1)S(1)}, bf16[512,512]{1,0:T(8,128)(2,1)S(1)}, u32[]{:S(2)}, u32[]{:S(2)}) collective-permute-start(bf16[512,512]{1,0:T(8,128)(2,1)S(1)} %get-tuple-element.80), channel_id=1, source_target_pairs={{0,1},{1,2},{2,3},{3,0},{4,5},{5,6},{6,7},{7,4},{8,9},{9,10},{10,1... | collective-permute-start | bytes 1572872 | tf_op jit(solution)/shard_map/ppermute | solution.py:68
  73.4 25.7 %collective-permute-start.19 = (bf16[512,512]{1,0:T(8,128)(2,1)S(1)}, bf16[512,512]{1,0:T(8,128)(2,1)S(1)}, u32[]{:S(2)}, u32[]{:S(2)}) collective-permute-start(bf16[512,512]{1,0:T(8,128)(2,1)S(1)} %get-tuple-element.81), channel_id=1, source_target_pairs={{0,3},{1,0},{2,1},{3,2},{4,7},{5,4},{6,5},{7,6},{8,11},{9,8},{10,9... | collective-permute-start | bytes 1572872 | tf_op jit(solution)/shard_map/ppermute | solution.py:68
  76.6 13.2 %collective-permute-start.22 = (bf16[512,512]{1,0:T(8,128)(2,1)S(1)}, bf16[512,512]{1,0:T(8,128)(2,1)S(1)}, u32[]{:S(2)}, u32[]{:S(2)}) collective-permute-start(bf16[512,512]{1,0:T(8,128)(2,1)S(1)} %get-tuple-element.87.refs_7_), channel_id=1, source_target_pairs={{0,8},{4,12},{8,0},{12,4},{16,24},{20,28},{24,16},{28,20},{32,40},... | collective-permute-start | bytes 1572872 | tf_op jit(solution)/shard_map/ppermute | solution.py:57
  78.3 12.0 %copy-start.5 = (bf16[512,1024]{1,0:T(8,128)(2,1)S(1)}, bf16[512,1024]{1,0:T(8,128)(2,1)}, u32[]{:S(2)}) copy-start(bf16[512,1024]{1,0:T(8,128)(2,1)} %get-tuple-element.76.rows) | copy-start | bytes 3145732
  89.8 9.2 %collective-permute-start.21 = (bf16[512,512]{1,0:T(8,128)(2,1)S(1)}, bf16[512,512]{1,0:T(8,128)(2,1)S(1)}, u32[]{:S(2)}, u32[]{:S(2)}) collective-permute-start(bf16[512,512]{1,0:T(8,128)(2,1)S(1)} %get-tuple-element.87.refs_7_), channel_id=1, source_target_pairs={{0,4},{4,0},{8,12},{12,8},{16,20},{20,16},{24,28},{28,24},{32,36},... | collective-permute-start | bytes 1572872 | tf_op jit(solution)/shard_map/ppermute | solution.py:57
  89.8 9.2 %collective-permute-start.23 = (bf16[512,512]{1,0:T(8,128)(2,1)S(1)}, bf16[512,512]{1,0:T(8,128)(2,1)S(1)}, u32[]{:S(2)}, u32[]{:S(2)}) collective-permute-start(bf16[512,512]{1,0:T(8,128)(2,1)S(1)} %collective-permute-done.22.refs_9_), channel_id=1, source_target_pairs={{0,4},{4,0},{8,12},{12,8},{16,20},{20,16},{24,28},{28,24},{32,36},... | collective-permute-start | bytes 1572872 | tf_op jit(solution)/shard_map/ppermute | solution.py:57
  93.6 27.3 %collective-permute-start.17 = (bf16[512,512]{1,0:T(8,128)(2,1)S(1)}, bf16[512,512]{1,0:T(8,128)(2,1)S(1)}, u32[]{:S(2)}, u32[]{:S(2)}) collective-permute-start(bf16[512,512]{1,0:T(8,128)(2,1)S(1)} %get-tuple-element.79), channel_id=1, source_target_pairs={{0,1},{1,2},{2,3},{3,0},{4,5},{5,6},{6,7},{7,4},{8,9},{9,10},{10,1... | collective-permute-start | bytes 1572872 | tf_op jit(solution)/shard_map/ppermute | solution.py:68
  96.9 24.0 %collective-permute-start.20 = (bf16[512,512]{1,0:T(8,128)(2,1)S(1)}, bf16[512,512]{1,0:T(8,128)(2,1)S(1)}, u32[]{:S(2)}, u32[]{:S(2)}) collective-permute-start(bf16[512,512]{1,0:T(8,128)(2,1)S(1)} %get-tuple-element.82), channel_id=1, source_target_pairs={{0,3},{1,0},{2,1},{3,2},{4,7},{5,4},{6,5},{7,6},{8,11},{9,8},{10,9... | collective-permute-start | bytes 1572872 | tf_op jit(solution)/shard_map/ppermute | solution.py:68
  99.0 21.9 %copy-start.4 = (bf16[512,1024]{1,0:T(8,128)(2,1)S(1)}, bf16[512,1024]{1,0:T(8,128)(2,1)}, u32[]{:S(2)}) copy-start(bf16[512,1024]{1,0:T(8,128)(2,1)} %get-tuple-element.67.own) | copy-start | bytes 3145732
  107.9 17.8 %collective-permute-start.24 = (bf16[512,256]{1,0:T(8,128)(2,1)S(1)}, bf16[512,256]{1,0:T(8,128)(2,1)S(1)}, u32[]{:S(2)}, u32[]{:S(2)}) collective-permute-start(bf16[512,256]{1,0:T(8,128)(2,1)S(1)} %get-tuple-element.95), channel_id=1, source_target_pairs={{4,0},{8,4},{12,8},{16,12},{20,16},{24,20},{28,24},{32,28},{36,32}... | collective-permute-start | bytes 786440 | tf_op jit(solution)/shard_map/ppermute | solution.py:63
  113.8 11.9 %collective-permute-start.25 = (bf16[384,256]{1,0:T(8,128)(2,1)S(1)}, bf16[384,256]{1,0:T(8,128)(2,1)S(1)}, u32[]{:S(2)}, u32[]{:S(2)}) collective-permute-start(bf16[384,256]{1,0:T(8,128)(2,1)S(1)} %get-tuple-element.97), channel_id=1, source_target_pairs={{8,0},{12,4},{16,8},{20,12},{24,16},{28,20},{32,24},{36,28},{40,32... | collective-permute-start | bytes 589832 | tf_op jit(solution)/shard_map/ppermute | solution.py:63
